TPU v7x, 128 devices: a whole 4x4x4 slice. The times are simulated.
128 devices in a mesh: role: 2 (over core), dev: 64 (over z, x, y).
Axes of the slice: x: 4, y: 4, z: 4, core: 2. Of those that a mesh axis runs over, the one named last changes fastest.
Arguments:
- residual_in: bfloat16 [2048, 4096], P(('role', 'dev')), may hold values from -6 to 6
- queries: bfloat16 [2048, 8192], P(('role', 'dev')), may hold values from -6 to 6
- key_cache: bfloat16 [2048, 4, 128, 128], P(('role', 'dev')), may hold values from -6 to 6
- value_cache: bfloat16 [2048, 4, 128, 128], P(('role', 'dev')), may hold values from -6 to 6
- lengths: int32 [2048], P(('role', 'dev')), may hold values from 2 to 128, as said below
- out_weight: bfloat16 [8192, 4096], P('dev'), may hold values from -0.0625 to 0.0625
- norm_gain: float32 [4096], replicated, may hold values from 0.5 to 1.5
- expert_ids: int32 [2048, 8], P(('role', 'dev')), may hold values from 0 to 127, all different within a row; in each aligned block of 16 rows (0 to 15, 16 to 31, ...) at most 2 rows name the same one
- gate_values: float32 [2048, 8], P(('role', 'dev')), may hold values from 0.05 to 1
- w_gate: bfloat16 [128, 4096, 768], P(('role', 'dev')), may hold values from -0.09375 to 0.09375
- w_up: bfloat16 [128, 4096, 768], P(('role', 'dev')), may hold values from -0.09375 to 0.09375
- w_down: bfloat16 [128, 768, 4096], P(('role', 'dev')), may hold values from -0.21875 to 0.21875
Outputs:
- layer_out: bfloat16 [2048, 4096], P(('role', 'dev'))
Inputs may be any that keep to these rules, and one draw needn't show every extreme that they name: `lengths`: every row has two or more live positions; some row has all 128 positions live. `expert_ids`: within the 16 rows of one device, no expert is chosen more than 2 times, a bound that some block reaches.
All inputs are finite; a program needn't handle non-finite values.
Results may differ from a plain program's by a relative error of at most 0.009.
Values may be sent and summed in bfloat16 or wider, within the bound.
No kernel may reach another device: no remote copies, remote signals or barrier semaphores. Data moves between devices by JAX's collectives and lax.ppermute only.
A program may use at most 128 MiB of HBM per device.

v0:
```python
import math

import jax
import jax.numpy as jnp
from jax import lax
from jax.sharding import PartitionSpec as P


def hadamard_table(order):
    indices = jnp.arange(order, dtype=jnp.int32)
    signs = jnp.ones((order, order), jnp.float32)
    stride = 1
    while stride < order:
        both = jnp.bitwise_and(
            jnp.bitwise_and(indices[:, None], stride), jnp.bitwise_and(indices[None, :], stride)
        )
        signs = signs * jnp.where(both > 0, -1.0, 1.0).astype(jnp.float32)
        stride = stride * 2
    return signs / math.sqrt(order)


def shards(
    residual_in,
    queries,
    key_cache,
    value_cache,
    lengths,
    out_weight,
    norm_gain,
    expert_ids,
    gate_values,
    w_gate,
    w_up,
    w_down,
):
    row_count = queries.shape[0]
    kv_heads = key_cache.shape[1]
    cache_len = key_cache.shape[2]
    head_dim = key_cache.shape[3]
    head_total = queries.shape[1] // head_dim
    groups = head_total // kv_heads
    width = residual_in.shape[1]
    query_heads = queries.reshape(row_count, kv_heads, groups, head_dim)
    scores = jnp.einsum(
        "rkgd,rkld->rkgl", query_heads, key_cache, preferred_element_type=jnp.float32
    ) / math.sqrt(head_dim)
    positions = jnp.arange(cache_len, dtype=jnp.int32)
    live = positions[None, :] < lengths[:, None]
    scores = jnp.where(live[:, None, None, :], scores, -1e30)
    peak = jnp.max(scores, axis=-1, keepdims=True)
    weights = jnp.exp(scores - peak)
    probs = (weights / jnp.sum(weights, axis=-1, keepdims=True)).astype(jnp.bfloat16)
    rotated = jnp.einsum(
        "rkgl,rkld->rkgd", probs, value_cache, preferred_element_type=jnp.float32
    ).astype(jnp.bfloat16)
    rotated = rotated.reshape(row_count, head_total, head_dim)
    table = hadamard_table(head_dim)
    received = lax.all_to_all(rotated, "dev", split_axis=1, concat_axis=0, tiled=True)
    local_heads = received.shape[1]
    plain = jnp.einsum(
        "rhd,de->rhe", received.astype(jnp.float32), table, precision=lax.Precision.HIGHEST
    ).astype(jnp.bfloat16)
    attn = lax.psum_scatter(
        jnp.dot(
            plain.reshape(lax.axis_size("dev") * row_count, local_heads * head_dim),
            out_weight,
            preferred_element_type=jnp.float32,
        ),
        "dev",
        scatter_dimension=0,
        tiled=True,
    )
    hidden_state = residual_in.astype(jnp.float32) + attn
    scale = lax.rsqrt(jnp.mean(hidden_state * hidden_state, axis=-1, keepdims=True) + 1e-06)
    normed = (hidden_state * scale * norm_gain[None, :]).astype(jnp.bfloat16)
    mix = gate_values / jnp.sum(gate_values, axis=-1, keepdims=True)
    top = expert_ids.shape[1]
    local_experts = w_gate.shape[0]
    expert_total = local_experts * lax.axis_size(("role", "dev"))
    capacity = max(2, 2 * top * row_count // expert_total)
    pairs = row_count * top
    flat = expert_ids.reshape(pairs)
    onehot = (flat[:, None] == jnp.arange(expert_total, dtype=jnp.int32)[None, :]).astype(
        jnp.float32
    )
    lower = (jnp.arange(pairs)[:, None] > jnp.arange(pairs)[None, :]).astype(jnp.float32)
    earlier = jnp.dot(lower, onehot, preferred_element_type=jnp.float32)
    slots = jnp.sum(earlier * onehot, axis=1).astype(jnp.int32)
    target = flat * capacity + slots
    select = (
        jnp.arange(expert_total * capacity, dtype=jnp.int32)[:, None] == target[None, :]
    ).astype(jnp.bfloat16)
    select_rows = jnp.sum(select.reshape(expert_total * capacity, row_count, top), axis=2)
    outgoing = jnp.dot(select_rows, normed, preferred_element_type=jnp.float32).astype(jnp.bfloat16)
    outgoing = outgoing.reshape(expert_total, capacity, width)
    arrived = lax.all_to_all(outgoing, ("role", "dev"), split_axis=0, concat_axis=0, tiled=True)
    sources = arrived.shape[0] // local_experts
    grouped = arrived.reshape(sources, local_experts, arrived.shape[1], arrived.shape[2])
    gate = jnp.einsum("secd,edf->secf", grouped, w_gate, preferred_element_type=jnp.float32)
    upper = jnp.einsum("secd,edf->secf", grouped, w_up, preferred_element_type=jnp.float32)
    act = (jax.nn.silu(gate) * upper).astype(jnp.bfloat16)
    result = jnp.einsum("secf,efd->secd", act, w_down, preferred_element_type=jnp.float32).astype(
        jnp.bfloat16
    )
    replies = lax.all_to_all(
        result.reshape(arrived.shape), ("role", "dev"), split_axis=0, concat_axis=0, tiled=True
    )
    flat_replies = replies.reshape(expert_total * capacity, width)
    picked = (
        jnp.take(flat_replies, target, axis=0).reshape(row_count, top, width).astype(jnp.float32)
    )
    mixed = hidden_state + jnp.sum(mix[:, :, None] * picked, axis=1)
    return mixed.astype(jnp.bfloat16)


def solution(mesh):
    return jax.shard_map(
        shards,
        mesh=mesh,
        in_specs=(
            P(("role", "dev"), None),
            P(("role", "dev"), None),
            P(("role", "dev"), None, None, None),
            P(("role", "dev"), None, None, None),
            P(("role", "dev")),
            P("dev", None),
            P(),
            P(("role", "dev"), None),
            P(("role", "dev"), None),
            P(("role", "dev"), None, None),
            P(("role", "dev"), None, None),
            P(("role", "dev"), None, None),
        ),
        out_specs=P(("role", "dev"), None),
        check_vma=False,
    )
```

profile of v0, /device:TPU:5, one launch (start us, length us, event | category | flops | bytes accessed | tf_op | source)
XLA Modules:
  0.0 549.4 jit_solution(11939828208685038571)
XLA Ops:
  6.5 0.0 copy-start
  6.5 1.1 copy.37
  7.7 0.7 iota_compare_fusion.5
  8.4 0.0 copy-done
  8.4 1.2 fusion.34
  9.6 0.4 fusion.96
  10.0 3.4 convolution_convert_fusion.2
  13.4 0.0 copy-start.4
  13.4 0.9 copy.30
  14.3 10.9 %all-to-all-start = ((bf16[16,64,128]{2,0,1:T(8,128)(2,1)}), bf16[16,64,128]{2,0,1:T(8,128)(2,1)S(1)}, u32[]{:S(2)}, u32[]{:S(2)}) async-start(bf16[16,64,128]{2,0,1:T(8,128)(2,1)} %copy.30), calls=%async_computation | async-start | bytes 524288 | tf_op jit(solution)/shard_map/all_to_all | solution.py:58
  25.2 0.0 reduce-scatter.2.cloned.1.call-start
  25.3 7.4 %all-to-all-done = bf16[16,64,128]{2,0,1:T(8,128)(2,1)S(1)} async-done(((bf16[16,64,128]{2,0,1:T(8,128)(2,1)}), bf16[16,64,128]{2,0,1:T(8,128)(2,1)S(1)}, u32[]{:S(2)}, u32[]{:S(2)}) %all-to-all-start) | async-done | bytes 262176 | tf_op jit(solution)/shard_map/all_to_all | solution.py:58
  32.8 0.5 convolution_convert_fusion.1
  33.3 0.0 copy-done.4
  33.3 8.0 %fusion.97 = f32[1024,4096]{1,0:T(8,128)} fusion(bf16[1024,128]{1,0:T(8,128)(2,1)S(1)} %convolution_convert_fusion.1, bf16[128,4096]{1,0:T(8,128)(2,1)S(1)} %copy-done.4), kind=kOutput, calls=%fused_computation.109 | convolution fusion | flops 1073741824 | bytes 18087936 | tf_op jit(solution)/shard_map/dot_general | solution.py:64
  41.4 0.0 copy-start.7
  41.4 0.0 copy-start.3
  41.4 0.0 reduce-scatter.2.cloned.1.call-update
  41.4 0.7 copy-done.7
  42.0 0.1 copy.32
  42.1 0.1 reshape.214
  42.2 0.2 fusion.40
  42.4 0.1 convert_element_type.71
  42.5 0.1 fusion.53
  42.6 319.1 %reduce-scatter.2.cloned.1.call-done = f32[16,4096]{1,0:T(8,128)} async-done(((f32[1024,4096]{1,0:T(8,128)}), f32[16,4096]{1,0:T(8,128)}) %reduce-scatter.2.cloned.1.call-update) | async-done | bytes 262160 | tf_op jit(solution)/shard_map/reduce_scatter | solution.py:63
  361.7 0.0 copy-done.3
  361.7 1.1 multiply_reduce_fusion.1
  362.8 0.0 copy-done.5
  362.8 3.1 convolution_convert_fusion
  365.9 4.4 reshape.215
  370.3 101.8 %all_to_all.25 = bf16[128,2,4096]{2,1,0:T(2,128)(2,1)S(1)} all-to-all(bf16[128,2,4096]{2,1,0:T(2,128)(2,1)} %reshape.215), channel_id=1, replica_groups=mesh['role'=2,'dev'=64] {'role','dev'}, dimensions={0} | all-to-all | bytes 4194304 | tf_op jit(solution)/shard_map/all_to_all | solution.py:96
  472.1 0.0 copy-start.2
  472.1 1.3 copy-done.2
  473.3 6.5 %fusion.12 = f32[128,1,2,768]{3,0,2,1:T(8,128)S(1)} fusion(bf16[1,4096,768]{2,1,0:T(8,128)(2,1)} %param.21, bf16[128,2,4096]{2,1,0:T(2,128)(2,1)S(1)} %all_to_all.25), kind=kOutput, calls=%fused_computation.13 | convolution fusion | flops 1610612736 | bytes 9175040 | tf_op jit(solution)/shard_map/secd,edf->secf/dot_general | solution.py:99
  479.8 12.6 %fusion.7 = bf16[128,2,4096]{2,0,1:T(8,128)(2,1)} fusion(bf16[1,768,4096]{2,1,0:T(8,128)(2,1)} %param.23, bf16[1,4096,768]{2,1,0:T(8,128)(2,1)} %param.22, bf16[128,2,4096]{2,1,0:T(2,128)(2,1)} %copy-done.2, f32[128,1,2,768]{3,0,2,1:T(8,128)S(1)} %fusion.12), kind=kOutput, calls=%fused_computation.9 | convolution fusion | flops 3223453696 | bytes 17563648 | tf_op jit(solution)/shard_map/secf,efd->secd/dot_general | solution.py:102
  492.5 5.1 copy.36
  497.6 0.0 copy-start.6
  497.6 6.3 %all-to-all-start.2 = ((bf16[128,2,4096]{2,1,0:T(2,128)(2,1)}), bf16[128,2,4096]{2,1,0:T(2,128)(2,1)}, u32[]{:S(2)}, u32[]{:S(2)}) async-start(bf16[128,2,4096]{2,1,0:T(2,128)(2,1)} %copy.36), calls=%async_computation.3 | async-start | bytes 4194304 | tf_op jit(solution)/shard_map/all_to_all | solution.py:105
  503.8 0.1 mul.95
  503.9 0.0 copy-done.6
  504.0 0.1 copy.31
  504.1 28.7 %all-to-all-done.2 = bf16[128,2,4096]{2,1,0:T(2,128)(2,1)} async-done(((bf16[128,2,4096]{2,1,0:T(2,128)(2,1)}), bf16[128,2,4096]{2,1,0:T(2,128)(2,1)}, u32[]{:S(2)}, u32[]{:S(2)}) %all-to-all-start.2) | async-done | bytes 2097184 | tf_op jit(solution)/shard_map/all_to_all | solution.py:105
  532.7 4.1 reshape.220
  536.9 0.0 copy-start.1
  536.9 4.1 gather_fusion
  541.0 0.8 multiply_reduce_fusion
  541.8 0.0 copy-done.1
  541.8 0.7 add_convert_fusion
  (13 shorter events, 0.1 us)
Async XLA Ops:
  6.5 1.9 copy-start
  13.4 19.9 %copy-start.4 = (bf16[128,4096]{1,0:T(8,128)(2,1)S(1)}, bf16[128,4096]{1,0:T(8,128)(2,1)}, u32[]{:S(2)}) copy-start(bf16[128,4096]{1,0:T(8,128)(2,1)} %param.17) | copy-start | bytes 3145732
  14.3 18.4 %all-to-all-start = ((bf16[16,64,128]{2,0,1:T(8,128)(2,1)}), bf16[16,64,128]{2,0,1:T(8,128)(2,1)S(1)}, u32[]{:S(2)}, u32[]{:S(2)}) async-start(bf16[16,64,128]{2,0,1:T(8,128)(2,1)} %copy.30), calls=%async_computation | async-start | bytes 524288 | tf_op jit(solution)/shard_map/all_to_all | solution.py:58
  25.2 336.4 %reduce-scatter.2.cloned.1.call-start = ((), (), s32[]{:S(2)}) async-start(), calls=%async_computation.4 | async-start | bytes 17039360 | tf_op jit(solution)/shard_map/reduce_scatter | solution.py:63
  41.4 0.7 copy-start.7
  41.4 320.3 %copy-start.3 = (bf16[16,4096]{1,0:T(8,128)(2,1)S(1)}, bf16[16,4096]{1,0:T(8,128)(2,1)}, u32[]{:S(2)}) copy-start(bf16[16,4096]{1,0:T(8,128)(2,1)} %param.12) | copy-start | bytes 393220
  41.4 321.4 %copy-start.5 = (f32[4096]{0:T(1024)S(1)}, f32[4096]{0:T(1024)}, u32[]{:S(2)}) copy-start(f32[4096]{0:T(1024)} %param.18) | copy-start | bytes 49156
  472.1 1.3 copy-start.2
  497.6 6.4 %copy-start.6 = (f32[16,8]{0,1:T(8,128)S(1)}, f32[16,8]{0,1:T(8,128)}, u32[]{:S(2)}) copy-start(f32[16,8]{0,1:T(8,128)} %param.20) | copy-start | bytes 1540
  497.6 35.2 %all-to-all-start.2 = ((bf16[128,2,4096]{2,1,0:T(2,128)(2,1)}), bf16[128,2,4096]{2,1,0:T(2,128)(2,1)}, u32[]{:S(2)}, u32[]{:S(2)}) async-start(bf16[128,2,4096]{2,1,0:T(2,128)(2,1)} %copy.36), calls=%async_computation.3 | async-start | bytes 4194304 | tf_op jit(solution)/shard_map/all_to_all | solution.py:105
  536.9 4.9 copy-start.1
Sparse Core Ops, SparseCore 0:
  41.5 320.1 reduce-scatter.1
where the time goes:
time: 550 us; the launch traced here: 549 us
  waiting for transfers between devices  355 us (65%)
  blocking collectives  102 us (19%)
  matrix products  35.6 us (6%)
  local copies, waits for them, and re-layouts  22.1 us (4%)
  starting transfers between devices  17.2 us (3%)
  between operations  13.6 us (2%)
    reduce_scatter x1, waiting for transfers between devices, shards(): lax.psum_scatter(jnp.dot(plain.reshape(lax.axis_size('dev') * row_count,...  319 us
    all_to_all x1, blocking collectives, shards(): lax.all_to_all(outgoing, ('role', 'dev'), split_axis=0, concat_axis=0, ti...  102 us
    all_to_all x1, waiting for transfers between devices, shards(): lax.all_to_all(result.reshape(arrived.shape), ('role', 'dev'), split_axis...  28.7 us
    dot_general x1, matrix products, shards(): jnp.einsum('secf,efd->secd', act, w_down, preferred_element_type=jnp.floa...  12.6 us
  transfers between devices with their start and end apart: 3, of which 3 were waited for; matrix products, arithmetic and copies ran while one was open for 0% of the time, Pallas kernels for 0%

commit v1 on v0

v1 whole, which is shorter than its diff:
```python
import functools
import math

import jax
import jax.numpy as jnp
from jax import lax
from jax.experimental import pallas as pl
from jax.experimental.pallas import tpu as pltpu
from jax.sharding import PartitionSpec as P

BF16 = jnp.bfloat16
F32 = jnp.float32


def sign_table(order):
    indices = jnp.arange(order, dtype=jnp.int32)
    signs = jnp.ones((order, order), F32)
    stride = 1
    while stride < order:
        both = (indices[:, None] & stride) & (indices[None, :] & stride)
        signs = signs * jnp.where(both > 0, -1.0, 1.0).astype(F32)
        stride = stride * 2
    return signs


def expert_kernel(pieces, slots, x_ref, gate_ref, up_ref, down_ref, out_ref, x_s, gate_s, up_s, act_s, res_s):
    step = pl.program_id(0)
    group = x_ref.shape[0] // pieces
    span = group // pieces
    row = lax.broadcasted_iota(jnp.int32, (group, group), 0)
    col = lax.broadcasted_iota(jnp.int32, (group, group), 1)

    @pl.when(step == 0)
    def _():
        spread = (col == (row % span) * pieces + row // span).astype(F32).astype(BF16)
        for g in range(pieces):
            y = jnp.dot(spread, x_ref[pl.ds(g * group, group), :], preferred_element_type=F32).astype(BF16)
            for j in range(pieces):
                x_s[j, pl.ds(g * span, span), :] = y[j * span:(j + 1) * span, :]
        gate_s[...] = jnp.zeros_like(gate_s)
        up_s[...] = jnp.zeros_like(up_s)

    @pl.when(step < pieces)
    def _():
        x = x_s[step]
        gate_s[...] += jnp.dot(x, gate_ref[...], preferred_element_type=F32)
        up_s[...] += jnp.dot(x, up_ref[...], preferred_element_type=F32)

    @pl.when(step == pieces)
    def _():
        gate = gate_s[...]
        act_s[...] = (gate / (1.0 + jnp.exp(-gate)) * up_s[...]).astype(BF16)

    @pl.when(step >= pieces)
    def _():
        j = step - pieces
        y = jnp.dot(act_s[...], down_ref[...], preferred_element_type=F32).astype(BF16)
        at = pl.multiple_of(j * span, span)
        for g in range(pieces):
            res_s[g, pl.ds(at, span), :] = y[g * span:(g + 1) * span, :]

    @pl.when(step == 2 * pieces - 1)
    def _():
        gather = (row == (col % span) * pieces + col // span).astype(F32).astype(BF16)
        for g in range(pieces):
            out_ref[pl.ds(g * group, group), :] = jnp.dot(
                gather, res_s[g], preferred_element_type=F32
            ).astype(BF16)


def experts(x, w_gate, w_up, w_down, pieces, slots):
    rows, block = x.shape
    width, hidden = w_gate.shape
    tokens = rows // pieces
    last = pieces - 1
    return pl.pallas_call(
        functools.partial(expert_kernel, pieces, slots),
        grid=(2 * pieces,),
        out_shape=jax.ShapeDtypeStruct((rows, block), BF16),
        in_specs=[
            pl.BlockSpec((rows, block), lambda i: (0, 0)),
            pl.BlockSpec((block, hidden), lambda i: (jnp.minimum(i, last), 0)),
            pl.BlockSpec((block, hidden), lambda i: (jnp.minimum(i, last), 0)),
            pl.BlockSpec((hidden, block), lambda i: (0, jnp.maximum(i - pieces, 0))),
        ],
        out_specs=pl.BlockSpec((rows, block), lambda i: (0, 0)),
        scratch_shapes=[
            pltpu.VMEM((pieces, tokens, block), BF16),
            pltpu.VMEM((tokens, hidden), F32),
            pltpu.VMEM((tokens, hidden), F32),
            pltpu.VMEM((tokens, hidden), BF16),
            pltpu.VMEM((pieces, rows // pieces, block), BF16),
        ],
        compiler_params=pltpu.CompilerParams(vmem_limit_bytes=40 * 1024 * 1024),
        cost_estimate=pl.CostEstimate(
            flops=6 * tokens * width * hidden,
            bytes_accessed=6 * width * hidden + 4 * rows * block,
            transcendentals=tokens * hidden,
        ),
    )(x, w_gate, w_up, w_down)


def shards(
    residual_in,
    queries,
    key_cache,
    value_cache,
    lengths,
    out_weight,
    norm_gain,
    expert_ids,
    gate_values,
    w_gate,
    w_up,
    w_down,
):
    rows = queries.shape[0]
    kv_heads, cache_len, head_dim = key_cache.shape[1:]
    head_total = queries.shape[1] // head_dim
    width = residual_in.shape[1]
    chips = lax.axis_size("dev")
    pieces = 8
    clusters = chips // pieces
    block = width // pieces

    teams = [[c * pieces + i for i in range(pieces)] for c in range(clusters)]
    weight = out_weight.reshape(out_weight.shape[0], pieces, block).transpose(1, 0, 2)
    weight = lax.all_to_all(weight, "dev", 0, 0, tiled=True, axis_index_groups=teams)
    weight = weight.reshape(pieces * out_weight.shape[0], block)

    query_heads = queries.reshape(rows, kv_heads, head_total // kv_heads, head_dim)
    scores = jnp.einsum(
        "rkgd,rkld->rkgl", query_heads, key_cache, preferred_element_type=F32
    ) / math.sqrt(head_dim)
    positions = jnp.arange(cache_len, dtype=jnp.int32)
    live = positions[None, :] < lengths[:, None]
    scores = jnp.where(live[:, None, None, :], scores, -1e30)
    peak = jnp.max(scores, axis=-1, keepdims=True)
    weights = jnp.exp(scores - peak)
    probs = (weights / jnp.sum(weights, axis=-1, keepdims=True)).astype(BF16)
    rotated = jnp.einsum(
        "rkgl,rkld->rkgd", probs, value_cache, preferred_element_type=F32
    ).astype(BF16)
    table = sign_table(head_dim).astype(BF16)
    context = jnp.dot(
        rotated.reshape(rows * head_total, head_dim), table, preferred_element_type=F32
    ) * (1.0 / math.sqrt(head_dim))
    context = context.astype(BF16).reshape(rows, clusters, pieces * head_dim).transpose(1, 0, 2)
    context = jnp.broadcast_to(
        context[:, None], (clusters, pieces, rows, pieces * head_dim)
    ).reshape(chips, rows, pieces * head_dim)
    context = lax.all_to_all(context, "dev", 0, 0, tiled=True)
    part = jnp.dot(
        context.reshape(chips * rows, pieces * head_dim), weight, preferred_element_type=F32
    ).astype(BF16)
    part = lax.all_to_all(part.reshape(chips, rows, block), "dev", 0, 0, tiled=True)
    attn = jnp.sum(part.reshape(clusters, pieces, rows, block).astype(F32), axis=0)

    residual = residual_in.reshape(rows, pieces, block).transpose(1, 0, 2)
    hidden = residual.astype(F32) + attn
    scale = lax.rsqrt(jnp.sum(hidden * hidden, axis=(0, 2), keepdims=True) / width + 1e-06)
    normed = (hidden * scale * norm_gain.reshape(pieces, 1, block)).astype(BF16)
    normed = normed.reshape(pieces * rows, block)

    top = expert_ids.shape[1]
    expert_total = chips * lax.axis_size("role")
    slots = 2
    pairs = rows * top
    flat = expert_ids.reshape(pairs)
    same = flat[:, None] == flat[None, :]
    before = jnp.arange(pairs)[:, None] > jnp.arange(pairs)[None, :]
    slot = jnp.sum((same & before).astype(jnp.int32), axis=1)
    target = (flat * slots + slot).reshape(rows, top)
    places = expert_total * slots * pieces
    spot = target[None] * pieces + jnp.arange(pieces, dtype=jnp.int32)[:, None, None]
    spot = spot.reshape(pieces * rows, top)
    chosen = jnp.zeros((places, pieces * rows), jnp.bool_)
    for k in range(top):
        chosen = chosen | (jnp.arange(places, dtype=jnp.int32)[:, None] == spot[:, k][None, :])
    outgoing = jnp.dot(chosen.astype(BF16), normed, preferred_element_type=F32).astype(BF16)
    arrived = lax.all_to_all(
        outgoing.reshape(expert_total, slots * pieces, block), ("role", "dev"), 0, 0, tiled=True
    )
    result = experts(
        arrived.reshape(places, block), w_gate[0], w_up[0], w_down[0], pieces, slots
    )
    replies = lax.all_to_all(
        result.reshape(expert_total, slots * pieces, block), ("role", "dev"), 0, 0, tiled=True
    )
    mix = gate_values / jnp.sum(gate_values, axis=-1, keepdims=True)
    mix = jnp.broadcast_to(mix[None], (pieces, rows, top)).reshape(pieces * rows, top)
    mixer = jnp.zeros((pieces * rows, places), F32)
    for k in range(top):
        here = jnp.arange(places, dtype=jnp.int32)[None, :] == spot[:, k][:, None]
        mixer = mixer + jnp.where(here, mix[:, k][:, None], 0.0)
    rounded = lax.reduce_precision(mixer, exponent_bits=8, mantissa_bits=7)
    high = rounded.astype(BF16)
    low = (mixer - rounded).astype(BF16)
    both = jnp.dot(
        jnp.concatenate([high, low], axis=0),
        replies.reshape(places, block),
        preferred_element_type=F32,
    )
    mixed = hidden + (both[: pieces * rows] + both[pieces * rows :]).reshape(pieces, rows, block)
    return mixed.astype(BF16).transpose(1, 0, 2).reshape(rows, width)


def solution(mesh):
    both = ("role", "dev")
    return jax.shard_map(
        shards,
        mesh=mesh,
        in_specs=(
            P(both, None),
            P(both, None),
            P(both, None, None, None),
            P(both, None, None, None),
            P(both),
            P("dev", None),
            P(),
            P(both, None),
            P(both, None),
            P(both, None, None),
            P(both, None, None),
            P(both, None, None),
        ),
        out_specs=P(both, None),
        check_vma=False,
    )
```

time: 550 us -> 186 us (0.34)
  waiting for transfers between devices: 355 us -> 67.3 us
  blocking collectives: 102 us -> 39.2 us
  matrix products: 35.6 us -> 14.7 us
  Pallas kernels: 0 us -> 15.8 us
  between operations: 13.6 us -> 0.23 us
  starting transfers between devices: 17.2 us -> 28.5 us
  local copies, waits for them, and re-layouts: 22.1 us -> 14.4 us
    reduce_scatter x1 -> x0, waiting for transfers between devices: 319 us -> none  [shards(): lax.psum_scatter(jnp.dot(plain.reshape(lax.axis_size('dev') * row_count,...]
    all_to_all x1, blocking collectives: 102 us -> 39.2 us  [shards(): lax.all_to_all(outgoing.reshape(expert_total, slots * pieces, block), ('r...]
    all_to_all x2 -> x4, waiting for transfers between devices: 36.1 us -> 67.3 us  [the longest x1 26.5 us: shards(): lax.all_to_all(result.reshape(expert_total, slots * pieces, block), ('rol...]
    dot_general x6 -> x4, matrix products: 30.9 us -> 8.97 us  [the longest x1 4.1 us: shards(): jnp.dot(context.reshape(chips * rows, pieces * head_dim), weight, preferr...]
    pallas_call x0 -> x1, Pallas kernels: none -> 15.8 us  [experts(): pl.pallas_call(functools.partial(expert_kernel, pieces, slots), grid=(2 *...]
    all_to_all x2 -> x4, starting transfers between devices: 17.2 us -> 28.5 us  [the longest x1 9.72 us: shards(): context = lax.all_to_all(context, 'dev', 0, 0, tiled=True)]
    reshape x4 -> x3, local copies, waits for them, and re-layouts: 9.49 us -> 1.56 us  [the longest x1 0.82 us: shards(): context.astype(BF16).reshape(rows, clusters, pieces * head_dim)]
  transfers between devices with their start and end apart: 3 -> 4, of which waited for: 3 -> 4; matrix products, arithmetic and copies ran while one was open for 0% -> 8% of each run, Pallas kernels for 0% -> 0%
where the time goes in v1:
time: 186 us; the launch traced here: 185 us
  waiting for transfers between devices  67.3 us (36%)
  blocking collectives  39.2 us (21%)
  starting transfers between devices  28.5 us (15%)
  Pallas kernels  15.8 us (8%)
  matrix products  14.7 us (8%)
  local copies, waits for them, and re-layouts  14.4 us (8%)
  other arithmetic  4.73 us (3%)
    all_to_all x1, blocking collectives, shards(): lax.all_to_all(outgoing.reshape(expert_total, slots * pieces, block), ('r...  39.2 us
    all_to_all x1, waiting for transfers between devices, shards(): lax.all_to_all(result.reshape(expert_total, slots * pieces, block), ('rol...  26.5 us
    all_to_all x1, waiting for transfers between devices, shards(): context = lax.all_to_all(context, 'dev', 0, 0, tiled=True)  24.7 us
    pallas_call x1, Pallas kernels, experts(): pl.pallas_call(functools.partial(expert_kernel, pieces, slots), grid=(2 *...  15.8 us
    all_to_all x1, waiting for transfers between devices, shards(): lax.all_to_all(part.reshape(chips, rows, block), 'dev', 0, 0, tiled=True)  12.5 us
    all_to_all x1, starting transfers between devices, shards(): context = lax.all_to_all(context, 'dev', 0, 0, tiled=True)  9.72 us
    unnamed x21, local copies, waits for them, and re-layouts  8.41 us
    all_to_all x1, starting transfers between devices, shards(): lax.all_to_all(part.reshape(chips, rows, block), 'dev', 0, 0, tiled=True)  7.73 us
  transfers between devices with their start and end apart: 4, of which 4 were waited for; matrix products, arithmetic and copies ran while one was open for 8% of the time, Pallas kernels for 0%

profile of v1, /device:TPU:5, one launch (start us, length us, event | category | flops | bytes accessed | tf_op | source)
XLA Modules:
  0.0 184.9 jit_solution(6467291723946406560)
XLA Ops:
  0.0 0.0 copy-start
  0.0 2.4 %copy.43 = bf16[128,4096]{0,1:T(8,128)(2,1)} copy(bf16[128,4096]{1,0:T(8,128)(2,1)} %param.17) | data formatting | bytes 2097152 | tf_op args[5]
  2.4 4.8 %all-to-all-start.1 = ((bf16[8,128,512]{1,2,0:T(8,128)(2,1)}), bf16[8,128,512]{1,2,0:T(8,128)(2,1)S(1)}, u32[]{:S(2)}, u32[]{:S(2)}) async-start(bf16[8,128,512]{1,2,0:T(8,128)(2,1)} %bitcast.103), calls=%async_computation.1 | async-start | bytes 2097152 | tf_op jit(solution)/shard_map/all_to_all | solution.py:128
  7.3 1.0 copy.50
  8.3 0.0 copy-done.8
  8.3 0.1 iota_compare_fusion.20
  8.4 0.0 copy-done
  8.4 1.2 fusion.3
  9.6 0.8 copy-done.3
  10.4 0.4 fusion.52
  10.8 4.5 %convolution_convert_fusion.2 = bf16[16,4,16,128]{3,2,1,0:T(8,128)(2,1)} fusion(bf16[16,4,128,128]{3,2,1,0:T(8,128)(2,1)} %param.15, f32[16,4,16]{2,1,0:T(4,128)S(1)} %fusion.52, f32[16,4,16,128]{3,2,1,0:T(8,128)} %copy-done.3), kind=kOutput, calls=%fused_computation.12 | convolution fusion | flops 34079872 | bytes 2887680 | tf_op jit(solution)/shard_map/rkgl,rkld->rkgd/dot_general | solution.py:141
  15.2 1.3 fusion.4
  16.6 0.8 reshape.176
  17.4 1.1 copy.42
  18.5 3.7 %all-to-all-done.1 = bf16[8,128,512]{1,2,0:T(8,128)(2,1)S(1)} async-done(((bf16[8,128,512]{1,2,0:T(8,128)(2,1)}), bf16[8,128,512]{1,2,0:T(8,128)(2,1)S(1)}, u32[]{:S(2)}, u32[]{:S(2)}) %all-to-all-start.1) | async-done | bytes 1048608 | tf_op jit(solution)/shard_map/all_to_all | solution.py:128
  22.2 1.6 broadcast_in_dim.158
  23.7 9.7 %all-to-all-start = ((bf16[64,16,1024]{2,1,0:T(8,128)(2,1)}), bf16[64,16,1024]{2,1,0:T(8,128)(2,1)}, u32[]{:S(2)}, u32[]{:S(2)}) async-start(bf16[64,16,1024]{2,1,0:T(8,128)(2,1)} %bitcast.97), calls=%async_computation | async-start | bytes 4194304 | tf_op jit(solution)/shard_map/all_to_all | solution.py:152
  33.5 1.3 copy.44
  34.8 24.7 %all-to-all-done = bf16[64,16,1024]{2,1,0:T(8,128)(2,1)} async-done(((bf16[64,16,1024]{2,1,0:T(8,128)(2,1)}), bf16[64,16,1024]{2,1,0:T(8,128)(2,1)}, u32[]{:S(2)}, u32[]{:S(2)}) %all-to-all-start) | async-done | bytes 2097184 | tf_op jit(solution)/shard_map/all_to_all | solution.py:152
  59.5 4.1 %convolution_convert_fusion.1 = bf16[1024,512]{1,0:T(8,128)(2,1)} fusion(bf16[1024,1024]{1,0:T(8,128)(2,1)} %bitcast.4, bf16[1024,512]{1,0:T(8,128)(2,1)} %bitcast.107), kind=kOutput, calls=%fused_computation.5 | convolution fusion | flops 1074266112 | bytes 4194304 | tf_op jit(solution)/shard_map/dot_general | solution.py:153
  63.6 7.7 %all-to-all-start.2 = ((bf16[64,16,512]{2,1,0:T(8,128)(2,1)}), bf16[64,16,512]{2,1,0:T(8,128)(2,1)}, u32[]{:S(2)}, u32[]{:S(2)}) async-start(bf16[64,16,512]{2,1,0:T(8,128)(2,1)} %bitcast.8), calls=%async_computation.2 | async-start | bytes 2097152 | tf_op jit(solution)/shard_map/all_to_all | solution.py:156
  71.3 0.0 copy-done.7
  71.4 0.0 copy-done.4
  71.4 0.0 copy-done.5
  71.4 0.1 copy.45
  71.5 0.1 eq.240
  71.6 0.2 convert_reduce_fusion.1
  71.7 0.1 reduce_sum.50
  71.8 0.1 copy.46
  71.9 0.1 add.65
  72.0 0.1 add.67
  72.1 12.5 %all-to-all-done.2 = bf16[64,16,512]{2,1,0:T(8,128)(2,1)} async-done(((bf16[64,16,512]{2,1,0:T(8,128)(2,1)}), bf16[64,16,512]{2,1,0:T(8,128)(2,1)}, u32[]{:S(2)}, u32[]{:S(2)}) %all-to-all-start.2) | async-done | bytes 1048608 | tf_op jit(solution)/shard_map/all_to_all | solution.py:156
  84.6 1.4 convert_reduce_fusion
  86.0 0.2 multiply_reduce_fusion
  86.2 0.1 multiply_convert_fusion
  86.3 1.1 convolution_convert_fusion
  87.4 39.2 %all_to_all.25 = bf16[128,16,512]{2,1,0:T(8,128)(2,1)S(1)} all-to-all(bf16[128,16,512]{2,1,0:T(8,128)(2,1)S(1)} %bitcast.104), channel_id=1, replica_groups=mesh['role'=2,'dev'=64] {'role','dev'}, dimensions={0} | all-to-all | bytes 4194304 | tf_op jit(solution)/shard_map/all_to_all | solution.py:181
  126.6 2.8 %copy-done.2 = bf16[1,4096,768]{2,1,0:T(8,128)(2,1)S(1)} copy-done((bf16[1,4096,768]{2,1,0:T(8,128)(2,1)S(1)}, bf16[1,4096,768]{2,1,0:T(8,128)(2,1)}, u32[]{:S(2)}) %copy-start.2) | copy-done | bytes 6291480
  129.3 15.8 %shard_map.118 = bf16[2048,512]{1,0:T(8,128)(2,1)S(1)} custom-call(bf16[2048,512]{1,0:T(8,128)(2,1)S(1)} %bitcast.95, bf16[4096,768]{1,0:T(8,128)(2,1)S(1)} %bitcast.96, bf16[4096,768]{1,0:T(8,128)(2,1)} %bitcast.98, bf16[768,4096]{1,0:T(8,128)(2,1)} %bitcast.99), custom_call_target="tpu_custom_call" | custom-call | flops 4831838208 | bytes 23068672 | tf_op jit(solution)/shard_map/pallas_call | solution.py:76
  145.1 0.0 copy-start.1
  145.1 1.3 copy-done.1
  146.4 6.3 %all-to-all-start.4 = ((bf16[128,16,512]{2,1,0:T(8,128)(2,1)}), bf16[128,16,512]{2,1,0:T(8,128)(2,1)}, u32[]{:S(2)}, u32[]{:S(2)}) async-start(bf16[128,16,512]{2,1,0:T(8,128)(2,1)} %bitcast.94), calls=%async_computation.4 | async-start | bytes 4194304 | tf_op jit(solution)/shard_map/all_to_all | solution.py:187
  152.7 0.1 reshape.182
  152.8 2.2 %reduce-precision_convert_fusion = (bf16[128,2048]{1,0:T(8,128)(2,1)S(1)}, bf16[128,2048]{1,0:T(8,128)(2,1)}) fusion(f32[128]{0:T(128)S(1)} %get-tuple-element.8, s32[128]{0:T(128)S(1)} %get-tuple-element.16, f32[128]{0:T(128)S(1)} %get-tuple-element.9, s32[128]{0:T(128)S(1)} %get-tuple-element.17, f32[128]{0:T(128)S(1)} %get-tuple-element.10, ...), kind=kLoop, calls=%fused_computation.4 | loop fusion | flops 7077888 | bytes 1056768 | tf_op jit(solution)/shard_map/convert_element_type | solution.py:197
  155.1 26.5 %all-to-all-done.4 = bf16[128,16,512]{2,1,0:T(8,128)(2,1)} async-done(((bf16[128,16,512]{2,1,0:T(8,128)(2,1)}), bf16[128,16,512]{2,1,0:T(8,128)(2,1)}, u32[]{:S(2)}, u32[]{:S(2)}) %all-to-all-start.4) | async-done | bytes 2097184 | tf_op jit(solution)/shard_map/all_to_all | solution.py:187
  181.6 2.5 %fusion.6 = f32[256,512]{1,0:T(8,128)S(1)} fusion(bf16[2048,512]{1,0:T(8,128)(2,1)} %bitcast.33, bf16[128,2048]{1,0:T(8,128)(2,1)} %get-tuple-element.6, bf16[128,2048]{1,0:T(8,128)(2,1)S(1)} %get-tuple-element.5), kind=kOutput, calls=%fused_computation.14 | convolution fusion | flops 538968064 | bytes 3670016 | tf_op jit(solution)/shard_map/dot_general | solution.py:199
  184.1 0.1 fusion.28
  184.2 0.7 copy.49
  (25 shorter events, 0.2 us)
Async XLA Ops:
  0.0 8.4 %copy-start = (bf16[16,4,128,128]{3,2,1,0:T(8,128)(2,1)S(1)}, bf16[16,4,128,128]{3,2,1,0:T(8,128)(2,1)}, u32[]{:S(2)}) copy-start(bf16[16,4,128,128]{3,2,1,0:T(8,128)(2,1)} %param.14) | copy-start | bytes 6291460
  0.0 8.3 %copy-start.8 = (s32[16]{0:T(128)S(1)}, s32[16]{0:T(128)}, u32[]{:S(2)}) copy-start(s32[16]{0:T(128)} %param.16) | copy-start | bytes 196
  2.4 19.7 %all-to-all-start.1 = ((bf16[8,128,512]{1,2,0:T(8,128)(2,1)}), bf16[8,128,512]{1,2,0:T(8,128)(2,1)S(1)}, u32[]{:S(2)}, u32[]{:S(2)}) async-start(bf16[8,128,512]{1,2,0:T(8,128)(2,1)} %bitcast.103), calls=%async_computation.1 | async-start | bytes 2097152 | tf_op jit(solution)/shard_map/all_to_all | solution.py:128
  9.6 0.8 copy-start.3
  23.7 35.8 %all-to-all-start = ((bf16[64,16,1024]{2,1,0:T(8,128)(2,1)}), bf16[64,16,1024]{2,1,0:T(8,128)(2,1)}, u32[]{:S(2)}, u32[]{:S(2)}) async-start(bf16[64,16,1024]{2,1,0:T(8,128)(2,1)} %bitcast.97), calls=%async_computation | async-start | bytes 4194304 | tf_op jit(solution)/shard_map/all_to_all | solution.py:152
  63.6 7.7 %copy-start.7 = (f32[4096]{0:T(1024)S(1)}, f32[4096]{0:T(1024)}, u32[]{:S(2)}) copy-start(f32[4096]{0:T(1024)} %param.18) | copy-start | bytes 49156
  63.6 7.8 %copy-start.4 = (bf16[16,4096]{1,0:T(8,128)(2,1)S(1)}, bf16[16,4096]{1,0:T(8,128)(2,1)}, u32[]{:S(2)}) copy-start(bf16[16,4096]{1,0:T(8,128)(2,1)} %param.12) | copy-start | bytes 393220
  63.6 7.8 %copy-start.5 = (s32[16,8]{0,1:T(8,128)S(1)}, s32[16,8]{0,1:T(8,128)}, u32[]{:S(2)}) copy-start(s32[16,8]{0,1:T(8,128)} %param.19) | copy-start | bytes 1540
  63.6 21.0 %all-to-all-start.2 = ((bf16[64,16,512]{2,1,0:T(8,128)(2,1)}), bf16[64,16,512]{2,1,0:T(8,128)(2,1)}, u32[]{:S(2)}, u32[]{:S(2)}) async-start(bf16[64,16,512]{2,1,0:T(8,128)(2,1)} %bitcast.8), calls=%async_computation.2 | async-start | bytes 2097152 | tf_op jit(solution)/shard_map/all_to_all | solution.py:156
  126.6 2.8 %copy-start.2 = (bf16[1,4096,768]{2,1,0:T(8,128)(2,1)S(1)}, bf16[1,4096,768]{2,1,0:T(8,128)(2,1)}, u32[]{:S(2)}) copy-start(bf16[1,4096,768]{2,1,0:T(8,128)(2,1)} %param.21) | copy-start | bytes 18874372
  145.1 1.3 copy-start.1
  146.4 6.3 %copy-start.6 = (f32[16,8]{0,1:T(8,128)S(1)}, f32[16,8]{0,1:T(8,128)}, u32[]{:S(2)}) copy-start(f32[16,8]{0,1:T(8,128)} %param.20) | copy-start | bytes 1540
  146.4 35.2 %all-to-all-start.4 = ((bf16[128,16,512]{2,1,0:T(8,128)(2,1)}), bf16[128,16,512]{2,1,0:T(8,128)(2,1)}, u32[]{:S(2)}, u32[]{:S(2)}) async-start(bf16[128,16,512]{2,1,0:T(8,128)(2,1)} %bitcast.94), calls=%async_computation.4 | async-start | bytes 4194304 | tf_op jit(solution)/shard_map/all_to_all | solution.py:187

commit v2 on v1

--- a/solution.py
+++ b/solution.py
@@ -23,81 +23,117 @@
     return signs
 
 
-def expert_kernel(pieces, slots, x_ref, gate_ref, up_ref, down_ref, out_ref, x_s, gate_s, up_s, act_s, res_s):
-    step = pl.program_id(0)
-    group = x_ref.shape[0] // pieces
+def expert_kernel(pieces, x_hbm, gate_hbm, up_hbm, down_hbm, out_hbm,
+                  in_s, x_s, gate_s, up_s, down_s, act_s, res_s, out_s, x_sem, w_sem, d_sem, o_sem):
+    group, block = in_s.shape[1:]
     span = group // pieces
+    parts, _, wide = gate_s.shape
+    outs, _, tall = down_s.shape
+    loads = [pltpu.make_async_copy(x_hbm, in_s, x_sem)]
+    for i in range(parts):
+        cut = pl.ds(i * wide, wide)
+        loads.append(pltpu.make_async_copy(gate_hbm.at[:, cut], gate_s.at[i], w_sem.at[i, 0]))
+        loads.append(pltpu.make_async_copy(up_hbm.at[:, cut], up_s.at[i], w_sem.at[i, 1]))
+    for i in range(outs):
+        loads.append(pltpu.make_async_copy(down_hbm.at[:, pl.ds(i * tall, tall)], down_s.at[i], d_sem.at[i]))
+    for load in loads:
+        load.start()
+
     row = lax.broadcasted_iota(jnp.int32, (group, group), 0)
     col = lax.broadcasted_iota(jnp.int32, (group, group), 1)
-
-    @pl.when(step == 0)
-    def _():
-        spread = (col == (row % span) * pieces + row // span).astype(F32).astype(BF16)
-        for g in range(pieces):
-            y = jnp.dot(spread, x_ref[pl.ds(g * group, group), :], preferred_element_type=F32).astype(BF16)
-            for j in range(pieces):
-                x_s[j, pl.ds(g * span, span), :] = y[j * span:(j + 1) * span, :]
-        gate_s[...] = jnp.zeros_like(gate_s)
-        up_s[...] = jnp.zeros_like(up_s)
-
-    @pl.when(step < pieces)
-    def _():
-        x = x_s[step]
-        gate_s[...] += jnp.dot(x, gate_ref[...], preferred_element_type=F32)
-        up_s[...] += jnp.dot(x, up_ref[...], preferred_element_type=F32)
-
-    @pl.when(step == pieces)
-    def _():
-        gate = gate_s[...]
-        act_s[...] = (gate / (1.0 + jnp.exp(-gate)) * up_s[...]).astype(BF16)
-
-    @pl.when(step >= pieces)
-    def _():
-        j = step - pieces
-        y = jnp.dot(act_s[...], down_ref[...], preferred_element_type=F32).astype(BF16)
-        at = pl.multiple_of(j * span, span)
-        for g in range(pieces):
-            res_s[g, pl.ds(at, span), :] = y[g * span:(g + 1) * span, :]
-
-    @pl.when(step == 2 * pieces - 1)
-    def _():
-        gather = (row == (col % span) * pieces + col // span).astype(F32).astype(BF16)
-        for g in range(pieces):
-            out_ref[pl.ds(g * group, group), :] = jnp.dot(
-                gather, res_s[g], preferred_element_type=F32
-            ).astype(BF16)
-
-
-def experts(x, w_gate, w_up, w_down, pieces, slots):
+    spread = (col == (row % span) * pieces + row // span).astype(F32).astype(BF16)
+    gather = (row == (col % span) * pieces + col // span).astype(F32).astype(BF16)
+    loads[0].wait()
+    for g in range(in_s.shape[0]):
+        y = jnp.dot(spread, in_s[g], preferred_element_type=F32).astype(BF16)
+        for j in range(pieces):
+            x_s[g * span:(g + 1) * span, j * block:(j + 1) * block] = y[j * span:(j + 1) * span, :]
+    for i in range(parts):
+        loads[1 + 2 * i].wait()
+        gate = jnp.dot(x_s[...], gate_s[i], preferred_element_type=F32)
+        loads[2 + 2 * i].wait()
+        up = jnp.dot(x_s[...], up_s[i], preferred_element_type=F32)
+        act_s[:, i * wide:(i + 1) * wide] = (gate / (1.0 + jnp.exp(-gate)) * up).astype(BF16)
+    for i in range(outs):
+        loads[1 + 2 * parts + i].wait()
+        y = jnp.dot(act_s[...], down_s[i], preferred_element_type=F32).astype(BF16)
+        for n in range(tall // block):
+            j = i * (tall // block) + n
+            for g in range(in_s.shape[0]):
+                res_s[g, j * span:(j + 1) * span, :] = y[g * span:(g + 1) * span, n * block:(n + 1) * block]
+    stores = []
+    for g in range(in_s.shape[0]):
+        out_s[g] = jnp.dot(gather, res_s[g], preferred_element_type=F32).astype(BF16)
+        store = pltpu.make_async_copy(out_s.at[g], out_hbm.at[g], o_sem.at[g])
+        store.start()
+        stores.append(store)
+    for store in stores:
+        store.wait()
+
+
+def experts(x, w_gate, w_up, w_down, pieces):
     rows, block = x.shape
     width, hidden = w_gate.shape
     tokens = rows // pieces
-    last = pieces - 1
-    return pl.pallas_call(
-        functools.partial(expert_kernel, pieces, slots),
-        grid=(2 * pieces,),
-        out_shape=jax.ShapeDtypeStruct((rows, block), BF16),
-        in_specs=[
-            pl.BlockSpec((rows, block), lambda i: (0, 0)),
-            pl.BlockSpec((block, hidden), lambda i: (jnp.minimum(i, last), 0)),
-            pl.BlockSpec((block, hidden), lambda i: (jnp.minimum(i, last), 0)),
-            pl.BlockSpec((hidden, block), lambda i: (0, jnp.maximum(i - pieces, 0))),
+    groups = pieces
+    group = rows // groups
+    wide, tall = 256, 1024
+    if hidden % wide or width % tall or tall % block:
+        wide, tall = hidden, width
+    parts, outs = hidden // wide, width // tall
+    result = pl.pallas_call(
+        functools.partial(expert_kernel, pieces),
+        out_shape=jax.ShapeDtypeStruct((groups, group, block), BF16),
+        in_specs=[pl.BlockSpec(memory_space=pl.ANY)] * 4,
+        out_specs=pl.BlockSpec(memory_space=pl.ANY),
+        scratch_shapes=[
+            pltpu.VMEM((groups, group, block), BF16),
+            pltpu.VMEM((tokens, width), BF16),
+            pltpu.VMEM((parts, width, wide), BF16),
+            pltpu.VMEM((parts, width, wide), BF16),
+            pltpu.VMEM((outs, hidden, tall), BF16),
+            pltpu.VMEM((tokens, hidden), BF16),
+            pltpu.VMEM((groups, group, block), BF16),
+            pltpu.VMEM((groups, group, block), BF16),
+            pltpu.SemaphoreType.DMA,
+            pltpu.SemaphoreType.DMA((parts, 2)),
+            pltpu.SemaphoreType.DMA((outs,)),
+            pltpu.SemaphoreType.DMA((groups,)),
         ],
-        out_specs=pl.BlockSpec((rows, block), lambda i: (0, 0)),
-        scratch_shapes=[
-            pltpu.VMEM((pieces, tokens, block), BF16),
-            pltpu.VMEM((tokens, hidden), F32),
-            pltpu.VMEM((tokens, hidden), F32),
-            pltpu.VMEM((tokens, hidden), BF16),
-            pltpu.VMEM((pieces, rows // pieces, block), BF16),
-        ],
-        compiler_params=pltpu.CompilerParams(vmem_limit_bytes=40 * 1024 * 1024),
+        compiler_params=pltpu.CompilerParams(vmem_limit_bytes=52 * 1024 * 1024),
         cost_estimate=pl.CostEstimate(
             flops=6 * tokens * width * hidden,
             bytes_accessed=6 * width * hidden + 4 * rows * block,
             transcendentals=tokens * hidden,
         ),
-    )(x, w_gate, w_up, w_down)
+    )(x.reshape(groups, group, block), w_gate, w_up, w_down)
+    return result.reshape(rows, block)
+
+
+def project_kernel(a_ref, w_ref, out_ref):
+    out_ref[...] = jnp.dot(a_ref[...], w_ref[...], preferred_element_type=F32).astype(BF16)
+
+
+def project(a, w):
+    rows, depth = a.shape
+    columns = w.shape[1]
+    tile = 256
+    return pl.pallas_call(
+        project_kernel,
+        grid=(rows // tile,),
+        out_shape=jax.ShapeDtypeStruct((rows, columns), BF16),
+        in_specs=[
+            pl.BlockSpec((tile, depth), lambda i: (i, 0)),
+            pl.BlockSpec((depth, columns), lambda i: (0, 0)),
+        ],
+        out_specs=pl.BlockSpec((tile, columns), lambda i: (i, 0)),
+        compiler_params=pltpu.CompilerParams(vmem_limit_bytes=24 * 1024 * 1024),
+        cost_estimate=pl.CostEstimate(
+            flops=2 * rows * depth * columns,
+            bytes_accessed=2 * (rows * depth + depth * columns + rows * columns),
+            transcendentals=0,
+        ),
+    )(a, w)
 
 
 def shards(
@@ -150,9 +186,7 @@
         context[:, None], (clusters, pieces, rows, pieces * head_dim)
     ).reshape(chips, rows, pieces * head_dim)
     context = lax.all_to_all(context, "dev", 0, 0, tiled=True)
-    part = jnp.dot(
-        context.reshape(chips * rows, pieces * head_dim), weight, preferred_element_type=F32
-    ).astype(BF16)
+    part = project(context.reshape(chips * rows, pieces * head_dim), weight)
     part = lax.all_to_all(part.reshape(chips, rows, block), "dev", 0, 0, tiled=True)
     attn = jnp.sum(part.reshape(clusters, pieces, rows, block).astype(F32), axis=0)
 
@@ -182,7 +216,7 @@
         outgoing.reshape(expert_total, slots * pieces, block), ("role", "dev"), 0, 0, tiled=True
     )
     result = experts(
-        arrived.reshape(places, block), w_gate[0], w_up[0], w_down[0], pieces, slots
+        arrived.reshape(places, block), w_gate[0], w_up[0], w_down[0], pieces
     )
     replies = lax.all_to_all(
         result.reshape(expert_total, slots * pieces, block), ("role", "dev"), 0, 0, tiled=True

time: 186 us -> 181 us (0.973)
  blocking collectives: 39.2 us -> 75 us
  waiting for transfers between devices: 67.3 us -> 42.6 us
  starting transfers between devices: 28.5 us -> 18.8 us
  local copies, waits for them, and re-layouts: 14.4 us -> 8.8 us
  matrix products: 14.7 us -> 10.6 us
  Pallas kernels: 15.8 us -> 19.9 us
    all_to_all x0 -> x1, blocking collectives: none -> 35.4 us  [shards(): context = lax.all_to_all(context, 'dev', 0, 0, tiled=True)]
    all_to_all x1 -> x0, waiting for transfers between devices: 24.7 us -> none  [shards(): context = lax.all_to_all(context, 'dev', 0, 0, tiled=True)]
    all_to_all x1 -> x0, starting transfers between devices: 9.72 us -> none  [shards(): context = lax.all_to_all(context, 'dev', 0, 0, tiled=True)]
    unnamed x21 -> x18, local copies, waits for them, and re-layouts: 8.41 us -> 2.95 us
    pallas_call x1 -> x2, Pallas kernels: 15.8 us -> 19.9 us  [the longest x1 18.2 us: experts(): pl.pallas_call(functools.partial(expert_kernel, pieces), out_shape=jax.Sh...]
    dot_general x1 -> x0, matrix products: 4.1 us -> none  [shards(): jnp.dot(context.reshape(chips * rows, pieces * head_dim), weight, preferr...]
    reshape x0 -> x1, local copies, waits for them, and re-layouts: none -> 2.48 us  [shards(): out_weight.reshape(out_weight.shape[0], pieces, block).transpose(1, 0, 2)]
  transfers between devices with their start and end apart: 4 -> 3, of which waited for: 4 -> 3; matrix products, arithmetic and copies ran while one was open for 8% -> 7% of each run, Pallas kernels for 0% -> 0%
where the time goes in v2:
time: 181 us
  blocking collectives  75 us (41%)
  waiting for transfers between devices  42.6 us (24%)
  Pallas kernels  19.9 us (11%)
  starting transfers between devices  18.8 us (10%)
  matrix products  10.6 us (6%)
  local copies, waits for them, and re-layouts  8.8 us (5%)
  other arithmetic  4.73 us (3%)
    all_to_all x1, blocking collectives, shards(): lax.all_to_all(outgoing.reshape(expert_total, slots * pieces, block), ('r...  39.6 us
    all_to_all x1, blocking collectives, shards(): context = lax.all_to_all(context, 'dev', 0, 0, tiled=True)  35.4 us
    all_to_all x1, waiting for transfers between devices, shards(): lax.all_to_all(result.reshape(expert_total, slots * pieces, block), ('rol...  26.6 us
    pallas_call x1, Pallas kernels, experts(): pl.pallas_call(functools.partial(expert_kernel, pieces), out_shape=jax.Sh...  18.2 us
    all_to_all x1, waiting for transfers between devices, shards(): lax.all_to_all(part.reshape(chips, rows, block), 'dev', 0, 0, tiled=True)  12.5 us
    all_to_all x1, starting transfers between devices, shards(): lax.all_to_all(part.reshape(chips, rows, block), 'dev', 0, 0, tiled=True)  7.73 us
    all_to_all x1, starting transfers between devices, shards(): lax.all_to_all(result.reshape(expert_total, slots * pieces, block), ('rol...  6.27 us
    all_to_all x1, starting transfers between devices, shards(): lax.all_to_all(weight, 'dev', 0, 0, tiled=True, axis_index_groups=teams)  4.82 us
  transfers between devices with their start and end apart: 3, of which 3 were waited for; matrix products, arithmetic and copies ran while one was open for 7% of the time, Pallas kernels for 0%

profile of v2, /device:TPU:5, one launch (start us, length us, event | category | flops | bytes accessed | tf_op | source)
XLA Modules:
  0.0 180.7 jit_solution(9616312604632182187)
XLA Ops:
  0.0 0.0 copy-start
  0.0 0.0 copy-start.7
  0.0 2.5 %copy.52 = bf16[16,8,8,512]{3,2,0,1:T(8,128)(2,1)} copy(bf16[16,8,8,512]{3,2,1,0:T(8,128)(2,1)} %bitcast.112) | data formatting | bytes 2097152 | tf_op jit(solution)/shard_map/reshape | solution.py:163
  2.5 4.8 %all-to-all-start.1 = ((bf16[8,128,512]{2,1,0:T(8,128)(2,1)}), bf16[8,128,512]{2,1,0:T(8,128)(2,1)S(1)}, u32[]{:S(2)}, u32[]{:S(2)}) async-start(bf16[8,128,512]{2,1,0:T(8,128)(2,1)} %bitcast.108), calls=%async_computation.1 | async-start | bytes 2097152 | tf_op jit(solution)/shard_map/all_to_all | solution.py:164
  7.3 1.0 copy.43
  8.3 0.0 copy-done.7
  8.4 0.1 iota_compare_fusion.20
  8.4 0.0 copy-done
  8.4 1.2 fusion.3
  9.6 0.8 copy-done.2
  10.5 0.4 fusion.52
  10.8 4.5 %convolution_convert_fusion.1 = bf16[16,4,16,128]{3,2,1,0:T(8,128)(2,1)} fusion(bf16[16,4,128,128]{3,2,1,0:T(8,128)(2,1)} %param.15, f32[16,4,16]{2,1,0:T(4,128)S(1)} %fusion.52, f32[16,4,16,128]{3,2,1,0:T(8,128)} %copy-done.2), kind=kOutput, calls=%fused_computation.11 | convolution fusion | flops 34079872 | bytes 2887680 | tf_op jit(solution)/shard_map/rkgl,rkld->rkgd/dot_general | solution.py:177
  15.3 1.3 fusion.4
  16.7 0.8 reshape.170
  17.5 1.1 copy.35
  18.6 3.6 %all-to-all-done.1 = bf16[8,128,512]{2,1,0:T(8,128)(2,1)S(1)} async-done(((bf16[8,128,512]{2,1,0:T(8,128)(2,1)}), bf16[8,128,512]{2,1,0:T(8,128)(2,1)S(1)}, u32[]{:S(2)}, u32[]{:S(2)}) %all-to-all-start.1) | async-done | bytes 1048608 | tf_op jit(solution)/shard_map/all_to_all | solution.py:164
  22.2 0.3 broadcast_in_dim.158
  22.5 35.4 %all_to_all.25 = bf16[64,16,1024]{2,1,0:T(8,128)(2,1)S(1)} all-to-all(bf16[64,16,1024]{2,1,0:T(8,128)(2,1)S(1)} %bitcast.99), channel_id=1, replica_groups=mesh['role'=2,'dev'=64] {'dev'}, dimensions={0} | all-to-all | bytes 4194304 | tf_op jit(solution)/shard_map/all_to_all | solution.py:188
  57.9 1.8 shard_map.118
  59.7 0.0 copy-start.1
  59.7 1.0 copy-done.1
  60.7 7.7 %all-to-all-start.2 = ((bf16[64,16,512]{2,1,0:T(8,128)(2,1)}), bf16[64,16,512]{2,1,0:T(8,128)(2,1)}, u32[]{:S(2)}, u32[]{:S(2)}) async-start(bf16[64,16,512]{2,1,0:T(8,128)(2,1)} %bitcast.98), calls=%async_computation.2 | async-start | bytes 2097152 | tf_op jit(solution)/shard_map/all_to_all | solution.py:190
  68.5 0.0 copy-done.6
  68.5 0.0 copy-done.3
  68.5 0.0 copy-done.4
  68.5 0.1 copy.37
  68.6 0.1 eq.240
  68.7 0.2 convert_reduce_fusion.1
  68.9 0.1 reduce_sum.50
  69.0 0.1 copy.38
  69.1 0.1 add.65
  69.1 0.1 add.67
  69.3 12.5 %all-to-all-done.2 = bf16[64,16,512]{2,1,0:T(8,128)(2,1)} async-done(((bf16[64,16,512]{2,1,0:T(8,128)(2,1)}), bf16[64,16,512]{2,1,0:T(8,128)(2,1)}, u32[]{:S(2)}, u32[]{:S(2)}) %all-to-all-start.2) | async-done | bytes 1048608 | tf_op jit(solution)/shard_map/all_to_all | solution.py:190
  81.7 1.4 convert_reduce_fusion
  83.1 0.2 multiply_reduce_fusion
  83.3 0.1 multiply_convert_fusion
  83.4 1.1 convolution_convert_fusion
  84.5 39.6 %all_to_all.26 = bf16[128,16,512]{2,1,0:T(8,128)(2,1)} all-to-all(bf16[128,16,512]{2,1,0:T(8,128)(2,1)S(1)} %bitcast.109), channel_id=1, replica_groups=mesh['role'=2,'dev'=64] {'role','dev'}, dimensions={0} | all-to-all | bytes 4194304 | tf_op jit(solution)/shard_map/all_to_all | solution.py:215
  124.1 18.2 %shard_map.119 = bf16[8,256,512]{2,1,0:T(8,128)(2,1)} custom-call(bf16[8,256,512]{2,1,0:T(8,128)(2,1)} %bitcast.101, bf16[4096,768]{1,0:T(8,128)(2,1)} %bitcast.102, bf16[4096,768]{1,0:T(8,128)(2,1)} %bitcast.103, bf16[768,4096]{1,0:T(8,128)(2,1)} %bitcast.104), custom_call_target="tpu_custom_call" | custom-call | flops 4831838208 | bytes 23068672 | tf_op jit(solution)/shard_map/pallas_call | solution.py:84
  142.3 0.0 copy-start.5
  142.3 6.3 %all-to-all-start.4 = ((bf16[128,16,512]{2,1,0:T(8,128)(2,1)}), bf16[128,16,512]{2,1,0:T(8,128)(2,1)}, u32[]{:S(2)}, u32[]{:S(2)}) async-start(bf16[128,16,512]{2,1,0:T(8,128)(2,1)} %bitcast.100), calls=%async_computation.4 | async-start | bytes 4194304 | tf_op jit(solution)/shard_map/all_to_all | solution.py:221
  148.5 0.0 copy-done.5
  148.6 0.1 reshape.176
  148.7 2.2 %reduce-precision_convert_fusion = (bf16[128,2048]{1,0:T(8,128)(2,1)S(1)}, bf16[128,2048]{1,0:T(8,128)(2,1)}) fusion(f32[128]{0:T(128)S(1)} %get-tuple-element.8, s32[128]{0:T(128)S(1)} %get-tuple-element.16, f32[128]{0:T(128)S(1)} %get-tuple-element.9, s32[128]{0:T(128)S(1)} %get-tuple-element.17, f32[128]{0:T(128)S(1)} %get-tuple-element.10, ...), kind=kLoop, calls=%fused_computation.4 | loop fusion | flops 7077888 | bytes 1056768 | tf_op jit(solution)/shard_map/convert_element_type | solution.py:231
  150.9 26.6 %all-to-all-done.4 = bf16[128,16,512]{2,1,0:T(8,128)(2,1)} async-done(((bf16[128,16,512]{2,1,0:T(8,128)(2,1)}), bf16[128,16,512]{2,1,0:T(8,128)(2,1)}, u32[]{:S(2)}, u32[]{:S(2)}) %all-to-all-start.4) | async-done | bytes 2097184 | tf_op jit(solution)/shard_map/all_to_all | solution.py:221
  177.5 2.5 %fusion.6 = f32[256,512]{1,0:T(8,128)S(1)} fusion(bf16[2048,512]{1,0:T(8,128)(2,1)} %bitcast.32, bf16[128,2048]{1,0:T(8,128)(2,1)} %get-tuple-element.6, bf16[128,2048]{1,0:T(8,128)(2,1)S(1)} %get-tuple-element.5), kind=kOutput, calls=%fused_computation.14 | convolution fusion | flops 538968064 | bytes 3670016 | tf_op jit(solution)/shard_map/dot_general | solution.py:233
  180.0 0.1 fusion.28
  180.1 0.7 copy.42
  (21 shorter events, 0.2 us)
Async XLA Ops:
  0.0 8.4 %copy-start = (bf16[16,4,128,128]{3,2,1,0:T(8,128)(2,1)S(1)}, bf16[16,4,128,128]{3,2,1,0:T(8,128)(2,1)}, u32[]{:S(2)}) copy-start(bf16[16,4,128,128]{3,2,1,0:T(8,128)(2,1)} %param.14) | copy-start | bytes 6291460
  0.0 8.3 %copy-start.7 = (s32[16]{0:T(128)S(1)}, s32[16]{0:T(128)}, u32[]{:S(2)}) copy-start(s32[16]{0:T(128)} %param.16) | copy-start | bytes 196
  2.5 19.7 %all-to-all-start.1 = ((bf16[8,128,512]{2,1,0:T(8,128)(2,1)}), bf16[8,128,512]{2,1,0:T(8,128)(2,1)S(1)}, u32[]{:S(2)}, u32[]{:S(2)}) async-start(bf16[8,128,512]{2,1,0:T(8,128)(2,1)} %bitcast.108), calls=%async_computation.1 | async-start | bytes 2097152 | tf_op jit(solution)/shard_map/all_to_all | solution.py:164
  9.6 0.8 copy-start.2
  59.7 1.0 copy-start.1
  60.7 7.7 %copy-start.6 = (f32[4096]{0:T(1024)S(1)}, f32[4096]{0:T(1024)}, u32[]{:S(2)}) copy-start(f32[4096]{0:T(1024)} %param.18) | copy-start | bytes 49156
  60.7 7.8 %copy-start.3 = (bf16[16,4096]{1,0:T(8,128)(2,1)S(1)}, bf16[16,4096]{1,0:T(8,128)(2,1)}, u32[]{:S(2)}) copy-start(bf16[16,4096]{1,0:T(8,128)(2,1)} %param.12) | copy-start | bytes 393220
  60.7 7.8 %copy-start.4 = (s32[16,8]{0,1:T(8,128)S(1)}, s32[16,8]{0,1:T(8,128)}, u32[]{:S(2)}) copy-start(s32[16,8]{0,1:T(8,128)} %param.19) | copy-start | bytes 1540
  60.7 21.0 %all-to-all-start.2 = ((bf16[64,16,512]{2,1,0:T(8,128)(2,1)}), bf16[64,16,512]{2,1,0:T(8,128)(2,1)}, u32[]{:S(2)}, u32[]{:S(2)}) async-start(bf16[64,16,512]{2,1,0:T(8,128)(2,1)} %bitcast.98), calls=%async_computation.2 | async-start | bytes 2097152 | tf_op jit(solution)/shard_map/all_to_all | solution.py:190
  142.3 6.3 %copy-start.5 = (f32[16,8]{0,1:T(8,128)S(1)}, f32[16,8]{0,1:T(8,128)}, u32[]{:S(2)}) copy-start(f32[16,8]{0,1:T(8,128)} %param.20) | copy-start | bytes 1540
  142.3 35.2 %all-to-all-start.4 = ((bf16[128,16,512]{2,1,0:T(8,128)(2,1)}), bf16[128,16,512]{2,1,0:T(8,128)(2,1)}, u32[]{:S(2)}, u32[]{:S(2)}) async-start(bf16[128,16,512]{2,1,0:T(8,128)(2,1)} %bitcast.100), calls=%async_computation.4 | async-start | bytes 4194304 | tf_op jit(solution)/shard_map/all_to_all | solution.py:221

commit v3 on v2

--- a/solution.py
+++ b/solution.py
@@ -3,6 +3,7 @@
 
 import jax
 import jax.numpy as jnp
+import numpy as np
 from jax import lax
 from jax.experimental import pallas as pl
 from jax.experimental.pallas import tpu as pltpu
@@ -13,14 +14,74 @@
 
 
 def sign_table(order):
-    indices = jnp.arange(order, dtype=jnp.int32)
-    signs = jnp.ones((order, order), F32)
-    stride = 1
-    while stride < order:
-        both = (indices[:, None] & stride) & (indices[None, :] & stride)
-        signs = signs * jnp.where(both > 0, -1.0, 1.0).astype(F32)
-        stride = stride * 2
+    signs = np.ones((1, 1), np.float32)
+    while signs.shape[0] < order:
+        signs = np.block([[signs, signs], [signs, -signs]])
     return signs
+
+
+def attend_kernel(copies, len_ref, q_ref, k_ref, v_ref, table_ref, out_ref):
+    rows, _, cache_len, dim = k_ref.shape
+    heads = q_ref.shape[1] // dim
+    total = rows * heads
+    at = lax.broadcasted_iota(jnp.int32, (total, total), 0)
+    to = lax.broadcasted_iota(jnp.int32, (total, total), 1)
+    turn_in = (to == (at % heads) * rows + at // heads).astype(F32).astype(BF16)
+    turn_out = (to == (at % rows) * heads + at // rows).astype(F32).astype(BF16)
+    stacked = jnp.concatenate([q_ref[:, h * dim:(h + 1) * dim] for h in range(heads)], axis=0)
+    q = jnp.dot(turn_in, stacked, preferred_element_type=F32).astype(BF16)
+    position = lax.broadcasted_iota(jnp.int32, (heads, cache_len), 1)
+    scores = []
+    for r in range(rows):
+        s = lax.dot_general(
+            q[r * heads:(r + 1) * heads], k_ref[r, 0], (((1,), (1,)), ((), ())), preferred_element_type=F32
+        )
+        scores.append(jnp.where(position < len_ref[r], s * (1.0 / math.sqrt(dim)), -1e30))
+    scores = jnp.concatenate(scores, axis=0)
+    weights = jnp.exp(scores - jnp.max(scores, axis=-1, keepdims=True))
+    probs = (weights / jnp.sum(weights, axis=-1, keepdims=True)).astype(BF16)
+    rotated = jnp.concatenate(
+        [
+            jnp.dot(probs[r * heads:(r + 1) * heads], v_ref[r, 0], preferred_element_type=F32).astype(BF16)
+            for r in range(rows)
+        ],
+        axis=0,
+    )
+    turned = jnp.dot(turn_out, rotated, preferred_element_type=F32).astype(BF16)
+    context = jnp.dot(turned, table_ref[...], preferred_element_type=F32) * (1.0 / math.sqrt(dim))
+    context = context.astype(BF16)
+    each = out_ref.shape[3] // dim
+    for h in range(heads):
+        piece = context[h * rows:(h + 1) * rows]
+        for c in range(copies):
+            out_ref[h // each, c, :, (h % each) * dim:(h % each + 1) * dim] = piece
+
+
+def attend(lengths, queries, key_cache, value_cache, clusters, copies):
+    rows, kv_heads, cache_len, dim = key_cache.shape
+    share = queries.shape[1] // kv_heads
+    columns = queries.shape[1] // clusters
+    table = jnp.asarray(sign_table(dim), BF16)
+    per = clusters // kv_heads
+    return pl.pallas_call(
+        functools.partial(attend_kernel, copies),
+        grid=(kv_heads,),
+        out_shape=jax.ShapeDtypeStruct((clusters, copies, rows, columns), BF16),
+        in_specs=[
+            pl.BlockSpec(memory_space=pltpu.SMEM),
+            pl.BlockSpec((rows, share), lambda i: (0, i)),
+            pl.BlockSpec((rows, 1, cache_len, dim), lambda i: (0, i, 0, 0)),
+            pl.BlockSpec((rows, 1, cache_len, dim), lambda i: (0, i, 0, 0)),
+            pl.BlockSpec((dim, dim), lambda i: (0, 0)),
+        ],
+        out_specs=pl.BlockSpec((per, copies, rows, columns), lambda i: (i, 0, 0, 0)),
+        compiler_params=pltpu.CompilerParams(vmem_limit_bytes=24 * 1024 * 1024),
+        cost_estimate=pl.CostEstimate(
+            flops=4 * rows * queries.shape[1] * cache_len,
+            bytes_accessed=4 * rows * kv_heads * cache_len * dim + 2 * clusters * copies * rows * columns,
+            transcendentals=rows * queries.shape[1] // dim * cache_len,
+        ),
+    )(lengths, queries, key_cache, value_cache, table)
 
 
 def expert_kernel(pieces, x_hbm, gate_hbm, up_hbm, down_hbm, out_hbm,
@@ -151,8 +212,7 @@
     w_down,
 ):
     rows = queries.shape[0]
-    kv_heads, cache_len, head_dim = key_cache.shape[1:]
-    head_total = queries.shape[1] // head_dim
+    head_dim = key_cache.shape[3]
     width = residual_in.shape[1]
     chips = lax.axis_size("dev")
     pieces = 8
@@ -164,27 +224,8 @@
     weight = lax.all_to_all(weight, "dev", 0, 0, tiled=True, axis_index_groups=teams)
     weight = weight.reshape(pieces * out_weight.shape[0], block)
 
-    query_heads = queries.reshape(rows, kv_heads, head_total // kv_heads, head_dim)
-    scores = jnp.einsum(
-        "rkgd,rkld->rkgl", query_heads, key_cache, preferred_element_type=F32
-    ) / math.sqrt(head_dim)
-    positions = jnp.arange(cache_len, dtype=jnp.int32)
-    live = positions[None, :] < lengths[:, None]
-    scores = jnp.where(live[:, None, None, :], scores, -1e30)
-    peak = jnp.max(scores, axis=-1, keepdims=True)
-    weights = jnp.exp(scores - peak)
-    probs = (weights / jnp.sum(weights, axis=-1, keepdims=True)).astype(BF16)
-    rotated = jnp.einsum(
-        "rkgl,rkld->rkgd", probs, value_cache, preferred_element_type=F32
-    ).astype(BF16)
-    table = sign_table(head_dim).astype(BF16)
-    context = jnp.dot(
-        rotated.reshape(rows * head_total, head_dim), table, preferred_element_type=F32
-    ) * (1.0 / math.sqrt(head_dim))
-    context = context.astype(BF16).reshape(rows, clusters, pieces * head_dim).transpose(1, 0, 2)
-    context = jnp.broadcast_to(
-        context[:, None], (clusters, pieces, rows, pieces * head_dim)
-    ).reshape(chips, rows, pieces * head_dim)
+    context = attend(lengths, queries, key_cache, value_cache, clusters, pieces)
+    context = context.reshape(chips, rows, pieces * head_dim)
     context = lax.all_to_all(context, "dev", 0, 0, tiled=True)
     part = project(context.reshape(chips * rows, pieces * head_dim), weight)
     part = lax.all_to_all(part.reshape(chips, rows, block), "dev", 0, 0, tiled=True)

time: 181 us -> 179 us (0.989)
  matrix products: 10.6 us -> 2.81 us
  Pallas kernels: 19.9 us -> 26.3 us
  waiting for transfers between devices: 42.6 us -> 45.8 us
  local copies, waits for them, and re-layouts: 8.8 us -> 6.81 us
    dot_general x3 -> x0, matrix products: 7.02 us -> none  [the longest x1 4.49 us: shards(): jnp.einsum('rkgl,rkld->rkgd', probs, value_cache, preferred_element_type=...]
    pallas_call x0 -> x1, Pallas kernels: none -> 5.38 us  [attend(): pl.pallas_call(functools.partial(attend_kernel, copies), grid=(kv_heads,)...]
    all_to_all x1, waiting for transfers between devices: 3.62 us -> 6.31 us  [shards(): lax.all_to_all(weight, 'dev', 0, 0, tiled=True, axis_index_groups=teams)]
  transfers between devices with their start and end apart: 3 -> 3, of which waited for: 3 -> 3; matrix products, arithmetic and copies ran while one was open for 7% -> 2% of each run, Pallas kernels for 0% -> 3%
where the time goes in v3:
time: 179 us; the launch traced here: 178 us
  blocking collectives  75 us (42%)
  waiting for transfers between devices  45.8 us (26%)
  Pallas kernels  26.3 us (15%)
  starting transfers between devices  18.2 us (10%)
  local copies, waits for them, and re-layouts  6.81 us (4%)
  other arithmetic  3.02 us (2%)
  matrix products  2.81 us (2%)
    all_to_all x1, blocking collectives, shards(): lax.all_to_all(outgoing.reshape(expert_total, slots * pieces, block), ('r...  39.6 us
    all_to_all x1, blocking collectives, shards(): context = lax.all_to_all(context, 'dev', 0, 0, tiled=True)  35.4 us
    all_to_all x1, waiting for transfers between devices, shards(): lax.all_to_all(result.reshape(expert_total, slots * pieces, block), ('rol...  26.9 us
    pallas_call x1, Pallas kernels, experts(): pl.pallas_call(functools.partial(expert_kernel, pieces), out_shape=jax.Sh...  18.2 us
    all_to_all x1, waiting for transfers between devices, shards(): lax.all_to_all(part.reshape(chips, rows, block), 'dev', 0, 0, tiled=True)  12.5 us
    all_to_all x1, starting transfers between devices, shards(): lax.all_to_all(part.reshape(chips, rows, block), 'dev', 0, 0, tiled=True)  7.54 us
    all_to_all x1, waiting for transfers between devices, shards(): lax.all_to_all(weight, 'dev', 0, 0, tiled=True, axis_index_groups=teams)  6.31 us
    all_to_all x1, starting transfers between devices, shards(): lax.all_to_all(result.reshape(expert_total, slots * pieces, block), ('rol...  5.81 us
  transfers between devices with their start and end apart: 3, of which 3 were waited for; matrix products, arithmetic and copies ran while one was open for 2% of the time, Pallas kernels for 3%

profile of v3, /device:TPU:5, one launch (start us, length us, event | category | flops | bytes accessed | tf_op | source)
XLA Modules:
  0.0 178.1 jit_solution(12711179575471470498)
XLA Ops:
  0.0 0.0 copy-start.2
  0.0 0.0 copy-start.3
  0.0 0.0 copy-start.4
  0.0 2.3 %copy.48 = bf16[16,8,8,512]{3,2,0,1:T(8,128)(2,1)} copy(bf16[16,8,8,512]{3,2,1,0:T(8,128)(2,1)} %bitcast.100) | data formatting | bytes 2097152 | tf_op jit(solution)/shard_map/reshape | solution.py:223
  2.3 4.8 %all-to-all-start.1 = ((bf16[8,128,512]{2,1,0:T(8,128)(2,1)}), bf16[8,128,512]{2,1,0:T(8,128)(2,1)S(1)}, u32[]{:S(2)}, u32[]{:S(2)}) async-start(bf16[8,128,512]{2,1,0:T(8,128)(2,1)} %bitcast.84), calls=%async_computation.1 | async-start | bytes 2097152 | tf_op jit(solution)/shard_map/all_to_all | solution.py:224
  7.2 0.0 copy-done.2
  7.2 0.0 copy-done.3
  7.2 0.0 copy-done.4
  7.2 0.0 copy-start
  7.2 1.6 copy-done
  8.8 0.0 copy-start.1
  8.8 1.6 copy-done.1
  10.4 5.4 %shard_map.127 = bf16[8,8,16,1024]{3,2,1,0:T(8,128)(2,1)S(1)} custom-call(s32[16]{0:T(128)S(1)} %copy-done.4, bf16[16,8192]{1,0:T(8,128)(2,1)S(1)} %copy-done.2, bf16[16,4,128,128]{3,2,1,0:T(8,128)(2,1)S(1)} %copy-done, bf16[16,4,128,128]{3,2,1,0:T(8,128)(2,1)S(1)} %copy-done.1, bf16[128,128]{1,0:T(8,128)(2,1)S(1)} %copy-done.3), custom_call_target="tpu_custom_call" | custom-call | flops 67108864 | bytes 6291456 | tf_op jit(solution)/shard_map/pallas_call | solution.py:66
  15.8 6.3 %all-to-all-done.1 = bf16[8,128,512]{2,1,0:T(8,128)(2,1)S(1)} async-done(((bf16[8,128,512]{2,1,0:T(8,128)(2,1)}), bf16[8,128,512]{2,1,0:T(8,128)(2,1)S(1)}, u32[]{:S(2)}, u32[]{:S(2)}) %all-to-all-start.1) | async-done | bytes 1048608 | tf_op jit(solution)/shard_map/all_to_all | solution.py:224
  22.1 35.4 %all_to_all.25 = bf16[64,16,1024]{2,1,0:T(8,128)(2,1)S(1)} all-to-all(bf16[64,16,1024]{2,1,0:T(8,128)(2,1)S(1)} %bitcast.85), channel_id=1, replica_groups=mesh['role'=2,'dev'=64] {'dev'}, dimensions={0} | all-to-all | bytes 4194304 | tf_op jit(solution)/shard_map/all_to_all | solution.py:229
  57.5 2.7 %shard_map.128 = bf16[1024,512]{1,0:T(8,128)(2,1)} custom-call(bf16[1024,1024]{1,0:T(8,128)(2,1)S(1)} %bitcast.86, bf16[1024,512]{1,0:T(8,128)(2,1)S(1)} %bitcast.87), custom_call_target="tpu_custom_call" | custom-call | flops 1073741824 | bytes 4194304 | tf_op jit(solution)/shard_map/pallas_call | solution.py:182
  60.2 0.0 copy-start.8
  60.2 0.0 copy-start.5
  60.2 0.0 copy-start.6
  60.2 7.5 %all-to-all-start.2 = ((bf16[64,16,512]{2,1,0:T(8,128)(2,1)}), bf16[64,16,512]{2,1,0:T(8,128)(2,1)S(1)}, u32[]{:S(2)}, u32[]{:S(2)}) async-start(bf16[64,16,512]{2,1,0:T(8,128)(2,1)} %bitcast.5), calls=%async_computation.2 | async-start | bytes 2097152 | tf_op jit(solution)/shard_map/all_to_all | solution.py:231
  67.8 0.0 copy-done.8
  67.8 0.0 copy-done.5
  67.8 0.0 copy-done.6
  67.8 0.1 copy.34
  67.9 0.1 eq.240
  68.0 0.2 convert_reduce_fusion.1
  68.2 0.1 reduce_sum.40
  68.3 0.1 copy.35
  68.4 0.1 add.65
  68.5 0.1 add.67
  68.6 12.5 %all-to-all-done.2 = bf16[64,16,512]{2,1,0:T(8,128)(2,1)S(1)} async-done(((bf16[64,16,512]{2,1,0:T(8,128)(2,1)}), bf16[64,16,512]{2,1,0:T(8,128)(2,1)S(1)}, u32[]{:S(2)}, u32[]{:S(2)}) %all-to-all-start.2) | async-done | bytes 1048608 | tf_op jit(solution)/shard_map/all_to_all | solution.py:231
  81.1 0.2 convert_reduce_fusion
  81.3 0.2 multiply_reduce_fusion
  81.5 0.1 multiply_convert_fusion
  81.6 1.1 convolution_convert_fusion
  82.6 39.6 %all_to_all.26 = bf16[128,16,512]{2,1,0:T(8,128)(2,1)} all-to-all(bf16[128,16,512]{2,1,0:T(8,128)(2,1)S(1)} %bitcast.98), channel_id=1, replica_groups=mesh['role'=2,'dev'=64] {'role','dev'}, dimensions={0} | all-to-all | bytes 4194304 | tf_op jit(solution)/shard_map/all_to_all | solution.py:256
  122.2 18.2 %shard_map.129 = bf16[8,256,512]{2,1,0:T(8,128)(2,1)} custom-call(bf16[8,256,512]{2,1,0:T(8,128)(2,1)} %bitcast.89, bf16[4096,768]{1,0:T(8,128)(2,1)} %bitcast.90, bf16[4096,768]{1,0:T(8,128)(2,1)} %bitcast.91, bf16[768,4096]{1,0:T(8,128)(2,1)} %bitcast.92), custom_call_target="tpu_custom_call" | custom-call | flops 4831838208 | bytes 23068672 | tf_op jit(solution)/shard_map/pallas_call | solution.py:145
  140.4 0.0 copy-start.7
  140.4 5.8 %all-to-all-start.4 = ((bf16[128,16,512]{2,1,0:T(8,128)(2,1)}), bf16[128,16,512]{2,1,0:T(8,128)(2,1)S(1)}, u32[]{:S(2)}, u32[]{:S(2)}) async-start(bf16[128,16,512]{2,1,0:T(8,128)(2,1)} %bitcast.88), calls=%async_computation.4 | async-start | bytes 4194304 | tf_op jit(solution)/shard_map/all_to_all | solution.py:262
  146.2 0.0 copy-done.7
  146.3 0.1 reshape.74
  146.4 2.2 %reduce-precision_convert_fusion = (bf16[128,2048]{1,0:T(8,128)(2,1)S(1)}, bf16[128,2048]{1,0:T(8,128)(2,1)}) fusion(f32[128]{0:T(128)S(1)} %get-tuple-element.8, s32[128]{0:T(128)S(1)} %get-tuple-element.16, f32[128]{0:T(128)S(1)} %get-tuple-element.9, s32[128]{0:T(128)S(1)} %get-tuple-element.17, f32[128]{0:T(128)S(1)} %get-tuple-element.10, ...), kind=kLoop, calls=%fused_computation.3 | loop fusion | flops 7077888 | bytes 1056768 | tf_op jit(solution)/shard_map/convert_element_type | solution.py:272
  148.6 26.9 %all-to-all-done.4 = bf16[128,16,512]{2,1,0:T(8,128)(2,1)S(1)} async-done(((bf16[128,16,512]{2,1,0:T(8,128)(2,1)}), bf16[128,16,512]{2,1,0:T(8,128)(2,1)S(1)}, u32[]{:S(2)}, u32[]{:S(2)}) %all-to-all-start.4) | async-done | bytes 2097184 | tf_op jit(solution)/shard_map/all_to_all | solution.py:262
  175.5 1.7 fusion.1
  177.3 0.1 fusion.22
  177.4 0.7 copy.39
  (13 shorter events, 0.1 us)
Async XLA Ops:
  0.0 7.2 %copy-start.2 = (bf16[16,8192]{1,0:T(8,128)(2,1)S(1)}, bf16[16,8192]{1,0:T(8,128)(2,1)}, u32[]{:S(2)}) copy-start(bf16[16,8192]{1,0:T(8,128)(2,1)} %q_ref.1) | copy-start | bytes 786436
  0.0 7.2 %copy-start.3 = (bf16[128,128]{1,0:T(8,128)(2,1)S(1)}, bf16[128,128]{1,0:T(8,128)(2,1)}, u32[]{:S(2)}) copy-start(bf16[128,128]{1,0:T(8,128)(2,1)} %constant.15.clone.table_ref) | copy-start | bytes 98308
  0.0 7.2 %copy-start.4 = (s32[16]{0:T(128)S(1)}, s32[16]{0:T(128)}, u32[]{:S(2)}) copy-start(s32[16]{0:T(128)} %len_ref.1) | copy-start | bytes 196
  2.3 19.7 %all-to-all-start.1 = ((bf16[8,128,512]{2,1,0:T(8,128)(2,1)}), bf16[8,128,512]{2,1,0:T(8,128)(2,1)S(1)}, u32[]{:S(2)}, u32[]{:S(2)}) async-start(bf16[8,128,512]{2,1,0:T(8,128)(2,1)} %bitcast.84), calls=%async_computation.1 | async-start | bytes 2097152 | tf_op jit(solution)/shard_map/all_to_all | solution.py:224
  7.2 1.6 copy-start
  8.8 1.6 copy-start.1
  60.2 7.6 %copy-start.8 = (f32[4096]{0:T(1024)S(1)}, f32[4096]{0:T(1024)}, u32[]{:S(2)}) copy-start(f32[4096]{0:T(1024)} %param.19) | copy-start | bytes 49156
  60.2 7.6 %copy-start.5 = (bf16[16,4096]{1,0:T(8,128)(2,1)S(1)}, bf16[16,4096]{1,0:T(8,128)(2,1)}, u32[]{:S(2)}) copy-start(bf16[16,4096]{1,0:T(8,128)(2,1)} %param.13) | copy-start | bytes 393220
  60.2 7.6 %copy-start.6 = (s32[16,8]{0,1:T(8,128)S(1)}, s32[16,8]{0,1:T(8,128)}, u32[]{:S(2)}) copy-start(s32[16,8]{0,1:T(8,128)} %param.20) | copy-start | bytes 1540
  60.2 20.9 %all-to-all-start.2 = ((bf16[64,16,512]{2,1,0:T(8,128)(2,1)}), bf16[64,16,512]{2,1,0:T(8,128)(2,1)S(1)}, u32[]{:S(2)}, u32[]{:S(2)}) async-start(bf16[64,16,512]{2,1,0:T(8,128)(2,1)} %bitcast.5), calls=%async_computation.2 | async-start | bytes 2097152 | tf_op jit(solution)/shard_map/all_to_all | solution.py:231
  140.4 5.8 %copy-start.7 = (f32[16,8]{0,1:T(8,128)S(1)}, f32[16,8]{0,1:T(8,128)}, u32[]{:S(2)}) copy-start(f32[16,8]{0,1:T(8,128)} %param.21) | copy-start | bytes 1540
  140.4 35.1 %all-to-all-start.4 = ((bf16[128,16,512]{2,1,0:T(8,128)(2,1)}), bf16[128,16,512]{2,1,0:T(8,128)(2,1)S(1)}, u32[]{:S(2)}, u32[]{:S(2)}) async-start(bf16[128,16,512]{2,1,0:T(8,128)(2,1)} %bitcast.88), calls=%async_computation.4 | async-start | bytes 4194304 | tf_op jit(solution)/shard_map/all_to_all | solution.py:262

commit v4 on v3

--- a/solution.py
+++ b/solution.py
@@ -84,46 +84,37 @@
     )(lengths, queries, key_cache, value_cache, table)
 
 
-def expert_kernel(pieces, x_hbm, gate_hbm, up_hbm, down_hbm, out_hbm,
-                  in_s, x_s, gate_s, up_s, down_s, act_s, res_s, out_s, x_sem, w_sem, d_sem, o_sem):
-    group, block = in_s.shape[1:]
+def expert_kernel(pieces, x_ref, gate_ref, up_hbm, down_hbm, out_hbm,
+                  up_ref, down_ref, x_s, act_s, res_s, out_s, w_sem, o_sem):
+    group, block = x_ref.shape[1:]
     span = group // pieces
-    parts, _, wide = gate_s.shape
-    outs, _, tall = down_s.shape
-    loads = [pltpu.make_async_copy(x_hbm, in_s, x_sem)]
-    for i in range(parts):
-        cut = pl.ds(i * wide, wide)
-        loads.append(pltpu.make_async_copy(gate_hbm.at[:, cut], gate_s.at[i], w_sem.at[i, 0]))
-        loads.append(pltpu.make_async_copy(up_hbm.at[:, cut], up_s.at[i], w_sem.at[i, 1]))
-    for i in range(outs):
-        loads.append(pltpu.make_async_copy(down_hbm.at[:, pl.ds(i * tall, tall)], down_s.at[i], d_sem.at[i]))
-    for load in loads:
-        load.start()
-
+    fetch_up = pltpu.make_async_copy(up_hbm, up_ref, w_sem.at[0])
+    fetch_down = pltpu.make_async_copy(down_hbm, down_ref, w_sem.at[1])
+    fetch_up.start()
+    fetch_down.start()
     row = lax.broadcasted_iota(jnp.int32, (group, group), 0)
     col = lax.broadcasted_iota(jnp.int32, (group, group), 1)
     spread = (col == (row % span) * pieces + row // span).astype(F32).astype(BF16)
     gather = (row == (col % span) * pieces + col // span).astype(F32).astype(BF16)
-    loads[0].wait()
-    for g in range(in_s.shape[0]):
-        y = jnp.dot(spread, in_s[g], preferred_element_type=F32).astype(BF16)
+    for g in range(x_ref.shape[0]):
+        y = jnp.dot(spread, x_ref[g], preferred_element_type=F32).astype(BF16)
         for j in range(pieces):
             x_s[g * span:(g + 1) * span, j * block:(j + 1) * block] = y[j * span:(j + 1) * span, :]
-    for i in range(parts):
-        loads[1 + 2 * i].wait()
-        gate = jnp.dot(x_s[...], gate_s[i], preferred_element_type=F32)
-        loads[2 + 2 * i].wait()
-        up = jnp.dot(x_s[...], up_s[i], preferred_element_type=F32)
-        act_s[:, i * wide:(i + 1) * wide] = (gate / (1.0 + jnp.exp(-gate)) * up).astype(BF16)
-    for i in range(outs):
-        loads[1 + 2 * parts + i].wait()
-        y = jnp.dot(act_s[...], down_s[i], preferred_element_type=F32).astype(BF16)
-        for n in range(tall // block):
-            j = i * (tall // block) + n
-            for g in range(in_s.shape[0]):
+    gate = jnp.dot(x_s[...], gate_ref[...], preferred_element_type=F32)
+    gate = gate / (1.0 + jnp.exp(-gate))
+    fetch_up.wait()
+    up = jnp.dot(x_s[...], up_ref[...], preferred_element_type=F32)
+    act_s[...] = (gate * up).astype(BF16)
+    fetch_down.wait()
+    tall = 2 * block
+    for i in range(down_ref.shape[1] // tall):
+        y = jnp.dot(act_s[...], down_ref[:, i * tall:(i + 1) * tall], preferred_element_type=F32).astype(BF16)
+        for n in range(2):
+            j = i * 2 + n
+            for g in range(x_ref.shape[0]):
                 res_s[g, j * span:(j + 1) * span, :] = y[g * span:(g + 1) * span, n * block:(n + 1) * block]
     stores = []
-    for g in range(in_s.shape[0]):
+    for g in range(x_ref.shape[0]):
         out_s[g] = jnp.dot(gather, res_s[g], preferred_element_type=F32).astype(BF16)
         store = pltpu.make_async_copy(out_s.at[g], out_hbm.at[g], o_sem.at[g])
         store.start()
@@ -138,36 +129,32 @@
     tokens = rows // pieces
     groups = pieces
     group = rows // groups
-    wide, tall = 256, 1024
-    if hidden % wide or width % tall or tall % block:
-        wide, tall = hidden, width
-    parts, outs = hidden // wide, width // tall
+    operands = [
+        pltpu.with_memory_space_constraint(a, pltpu.VMEM)
+        for a in (x.reshape(groups, group, block), w_gate)
+    ] + [w_up, w_down]
     result = pl.pallas_call(
         functools.partial(expert_kernel, pieces),
         out_shape=jax.ShapeDtypeStruct((groups, group, block), BF16),
-        in_specs=[pl.BlockSpec(memory_space=pl.ANY)] * 4,
+        in_specs=[pl.BlockSpec(memory_space=pltpu.VMEM)] * 2 + [pl.BlockSpec(memory_space=pl.ANY)] * 2,
         out_specs=pl.BlockSpec(memory_space=pl.ANY),
         scratch_shapes=[
-            pltpu.VMEM((groups, group, block), BF16),
+            pltpu.VMEM((width, hidden), BF16),
+            pltpu.VMEM((hidden, width), BF16),
             pltpu.VMEM((tokens, width), BF16),
-            pltpu.VMEM((parts, width, wide), BF16),
-            pltpu.VMEM((parts, width, wide), BF16),
-            pltpu.VMEM((outs, hidden, tall), BF16),
             pltpu.VMEM((tokens, hidden), BF16),
             pltpu.VMEM((groups, group, block), BF16),
             pltpu.VMEM((groups, group, block), BF16),
-            pltpu.SemaphoreType.DMA,
-            pltpu.SemaphoreType.DMA((parts, 2)),
-            pltpu.SemaphoreType.DMA((outs,)),
+            pltpu.SemaphoreType.DMA((2,)),
             pltpu.SemaphoreType.DMA((groups,)),
         ],
-        compiler_params=pltpu.CompilerParams(vmem_limit_bytes=52 * 1024 * 1024),
+        compiler_params=pltpu.CompilerParams(vmem_limit_bytes=40 * 1024 * 1024),
         cost_estimate=pl.CostEstimate(
             flops=6 * tokens * width * hidden,
-            bytes_accessed=6 * width * hidden + 4 * rows * block,
+            bytes_accessed=4 * width * hidden + 4 * rows * block,
             transcendentals=tokens * hidden,
         ),
-    )(x.reshape(groups, group, block), w_gate, w_up, w_down)
+    )(*operands)
     return result.reshape(rows, block)
 
 

time: 179 us -> 173 us (0.966)
  Pallas kernels: 26.3 us -> 19.3 us
    pallas_call x1, Pallas kernels: 18.2 us -> 11.1 us  [experts(): pl.pallas_call(functools.partial(expert_kernel, pieces), out_shape=jax.Sh...]
where the time goes in v4:
time: 173 us; the launch traced here: 172 us
  blocking collectives  74.6 us (43%)
  waiting for transfers between devices  45.7 us (26%)
  Pallas kernels  19.3 us (11%)
  starting transfers between devices  18.4 us (11%)
  local copies, waits for them, and re-layouts  6.82 us (4%)
  other arithmetic  4.27 us (2%)
  matrix products  2.81 us (2%)
    all_to_all x1, blocking collectives, shards(): lax.all_to_all(outgoing.reshape(expert_total, slots * pieces, block), ('r...  39.2 us
    all_to_all x1, blocking collectives, shards(): context = lax.all_to_all(context, 'dev', 0, 0, tiled=True)  35.4 us
    all_to_all x1, waiting for transfers between devices, shards(): lax.all_to_all(result.reshape(expert_total, slots * pieces, block), ('rol...  26.9 us
    all_to_all x1, waiting for transfers between devices, shards(): lax.all_to_all(part.reshape(chips, rows, block), 'dev', 0, 0, tiled=True)  12.4 us
    pallas_call x1, Pallas kernels, experts(): pl.pallas_call(functools.partial(expert_kernel, pieces), out_shape=jax.Sh...  11.1 us
    all_to_all x1, starting transfers between devices, shards(): lax.all_to_all(part.reshape(chips, rows, block), 'dev', 0, 0, tiled=True)  7.73 us
    all_to_all x1, waiting for transfers between devices, shards(): lax.all_to_all(weight, 'dev', 0, 0, tiled=True, axis_index_groups=teams)  6.31 us
    all_to_all x1, starting transfers between devices, shards(): lax.all_to_all(result.reshape(expert_total, slots * pieces, block), ('rol...  5.81 us
  transfers between devices with their start and end apart: 3, of which 3 were waited for; matrix products, arithmetic and copies ran while one was open for 2% of the time, Pallas kernels for 3%

profile of v4, /device:TPU:5, one launch (start us, length us, event | category | flops | bytes accessed | tf_op | source)
XLA Modules:
  0.0 172.0 jit_solution(2001900760097801852)
XLA Ops:
  0.0 0.0 copy-start.3
  0.0 0.0 copy-start.4
  0.0 2.3 %copy.48 = bf16[16,8,8,512]{3,2,0,1:T(8,128)(2,1)} copy(bf16[16,8,8,512]{3,2,1,0:T(8,128)(2,1)} %bitcast.100) | data formatting | bytes 2097152 | tf_op jit(solution)/shard_map/reshape | solution.py:210
  2.4 4.8 %all-to-all-start.1 = ((bf16[8,128,512]{2,1,0:T(8,128)(2,1)}), bf16[8,128,512]{2,1,0:T(8,128)(2,1)S(1)}, u32[]{:S(2)}, u32[]{:S(2)}) async-start(bf16[8,128,512]{2,1,0:T(8,128)(2,1)} %bitcast.84), calls=%async_computation.1 | async-start | bytes 2097152 | tf_op jit(solution)/shard_map/all_to_all | solution.py:211
  7.2 0.0 copy-done.2
  7.2 0.0 copy-done.3
  7.2 0.0 copy-done.4
  7.2 0.0 copy-start
  7.2 1.6 copy-done
  8.8 0.0 copy-start.1
  8.8 1.6 copy-done.1
  10.4 5.4 %shard_map.127 = bf16[8,8,16,1024]{3,2,1,0:T(8,128)(2,1)S(1)} custom-call(s32[16]{0:T(128)S(1)} %copy-done.4, bf16[16,8192]{1,0:T(8,128)(2,1)S(1)} %copy-done.2, bf16[16,4,128,128]{3,2,1,0:T(8,128)(2,1)S(1)} %copy-done, bf16[16,4,128,128]{3,2,1,0:T(8,128)(2,1)S(1)} %copy-done.1, bf16[128,128]{1,0:T(8,128)(2,1)S(1)} %copy-done.3), custom_call_target="tpu_custom_call" | custom-call | flops 67108864 | bytes 6291456 | tf_op jit(solution)/shard_map/pallas_call | solution.py:66
  15.8 6.3 %all-to-all-done.1 = bf16[8,128,512]{2,1,0:T(8,128)(2,1)S(1)} async-done(((bf16[8,128,512]{2,1,0:T(8,128)(2,1)}), bf16[8,128,512]{2,1,0:T(8,128)(2,1)S(1)}, u32[]{:S(2)}, u32[]{:S(2)}) %all-to-all-start.1) | async-done | bytes 1048608 | tf_op jit(solution)/shard_map/all_to_all | solution.py:211
  22.1 35.4 %all_to_all.25 = bf16[64,16,1024]{2,1,0:T(8,128)(2,1)S(1)} all-to-all(bf16[64,16,1024]{2,1,0:T(8,128)(2,1)S(1)} %bitcast.85), channel_id=1, replica_groups=mesh['role'=2,'dev'=64] {'dev'}, dimensions={0} | all-to-all | bytes 4194304 | tf_op jit(solution)/shard_map/all_to_all | solution.py:216
  57.5 2.7 %shard_map.128 = bf16[1024,512]{1,0:T(8,128)(2,1)} custom-call(bf16[1024,1024]{1,0:T(8,128)(2,1)S(1)} %bitcast.86, bf16[1024,512]{1,0:T(8,128)(2,1)S(1)} %bitcast.91), custom_call_target="tpu_custom_call" | custom-call | flops 1073741824 | bytes 4194304 | tf_op jit(solution)/shard_map/pallas_call | solution.py:169
  60.3 0.0 copy-start.8
  60.3 0.0 copy-start.5
  60.3 7.7 %all-to-all-start.2 = ((bf16[64,16,512]{2,1,0:T(8,128)(2,1)}), bf16[64,16,512]{2,1,0:T(8,128)(2,1)}, u32[]{:S(2)}, u32[]{:S(2)}) async-start(bf16[64,16,512]{2,1,0:T(8,128)(2,1)} %bitcast.5), calls=%async_computation.2 | async-start | bytes 2097152 | tf_op jit(solution)/shard_map/all_to_all | solution.py:218
  68.0 0.0 copy-done.8
  68.0 0.0 copy-done.5
  68.0 0.0 slice-start
  68.1 0.0 copy-done.6
  68.1 0.1 copy.34
  68.2 0.1 eq.240
  68.2 0.2 convert_reduce_fusion.1
  68.4 0.1 reduce_sum.40
  68.5 0.1 copy.35
  68.6 0.1 add.65
  68.7 0.1 add.67
  68.8 12.4 %all-to-all-done.2 = bf16[64,16,512]{2,1,0:T(8,128)(2,1)} async-done(((bf16[64,16,512]{2,1,0:T(8,128)(2,1)}), bf16[64,16,512]{2,1,0:T(8,128)(2,1)}, u32[]{:S(2)}, u32[]{:S(2)}) %all-to-all-start.2) | async-done | bytes 1048608 | tf_op jit(solution)/shard_map/all_to_all | solution.py:218
  81.2 1.4 convert_reduce_fusion
  82.7 0.2 multiply_reduce_fusion
  82.8 0.1 multiply_convert_fusion
  83.0 0.0 slice-start.1
  83.0 1.1 convolution_convert_fusion
  84.0 39.2 %all_to_all.26 = bf16[128,16,512]{2,1,0:T(8,128)(2,1)S(1)} all-to-all(bf16[128,16,512]{2,1,0:T(8,128)(2,1)S(1)} %bitcast.98), channel_id=1, replica_groups=mesh['role'=2,'dev'=64] {'role','dev'}, dimensions={0} | all-to-all | bytes 4194304 | tf_op jit(solution)/shard_map/all_to_all | solution.py:243
  123.2 0.0 slice-done
  123.2 0.0 slice-done.1
  123.2 11.1 %shard_map.129 = bf16[8,256,512]{2,1,0:T(8,128)(2,1)} custom-call(bf16[8,256,512]{2,1,0:T(8,128)(2,1)S(1)} %bitcast.87, bf16[4096,768]{1,0:T(8,128)(2,1)S(1)} %bitcast.90, bf16[4096,768]{1,0:T(8,128)(2,1)} %bitcast.92, bf16[768,4096]{1,0:T(8,128)(2,1)} %bitcast.93), custom_call_target="tpu_custom_call" | custom-call | flops 4831838208 | bytes 16777216 | tf_op jit(solution)/shard_map/pallas_call | solution.py:136
  134.4 0.0 copy-start.7
  134.4 5.8 %all-to-all-start.4 = ((bf16[128,16,512]{2,1,0:T(8,128)(2,1)}), bf16[128,16,512]{2,1,0:T(8,128)(2,1)S(1)}, u32[]{:S(2)}, u32[]{:S(2)}) async-start(bf16[128,16,512]{2,1,0:T(8,128)(2,1)} %bitcast.29), calls=%async_computation.4 | async-start | bytes 4194304 | tf_op jit(solution)/shard_map/all_to_all | solution.py:249
  140.2 0.0 copy-done.7
  140.3 0.1 reshape.74
  140.4 2.2 %reduce-precision_convert_fusion = (bf16[128,2048]{1,0:T(8,128)(2,1)S(1)}, bf16[128,2048]{1,0:T(8,128)(2,1)}) fusion(f32[128]{0:T(128)S(1)} %get-tuple-element.8, s32[128]{0:T(128)S(1)} %get-tuple-element.16, f32[128]{0:T(128)S(1)} %get-tuple-element.9, s32[128]{0:T(128)S(1)} %get-tuple-element.17, f32[128]{0:T(128)S(1)} %get-tuple-element.10, ...), kind=kLoop, calls=%fused_computation.3 | loop fusion | flops 7077888 | bytes 1056768 | tf_op jit(solution)/shard_map/convert_element_type | solution.py:259
  142.6 26.9 %all-to-all-done.4 = bf16[128,16,512]{2,1,0:T(8,128)(2,1)S(1)} async-done(((bf16[128,16,512]{2,1,0:T(8,128)(2,1)}), bf16[128,16,512]{2,1,0:T(8,128)(2,1)S(1)}, u32[]{:S(2)}, u32[]{:S(2)}) %all-to-all-start.4) | async-done | bytes 2097184 | tf_op jit(solution)/shard_map/all_to_all | solution.py:249
  169.5 1.7 %fusion.1 = f32[256,512]{1,0:T(8,128)S(1)} fusion(bf16[2048,512]{1,0:T(8,128)(2,1)S(1)} %bitcast.97, bf16[128,2048]{1,0:T(8,128)(2,1)} %get-tuple-element.6, bf16[128,2048]{1,0:T(8,128)(2,1)S(1)} %get-tuple-element.5), kind=kOutput, calls=%fused_computation.6 | convolution fusion | flops 538968064 | bytes 3670016 | tf_op jit(solution)/shard_map/dot_general | solution.py:261
  171.3 0.1 fusion.22
  171.4 0.7 copy.39
  (16 shorter events, 0.1 us)
Async XLA Ops:
  0.0 7.2 %copy-start.2 = (bf16[16,8192]{1,0:T(8,128)(2,1)S(1)}, bf16[16,8192]{1,0:T(8,128)(2,1)}, u32[]{:S(2)}) copy-start(bf16[16,8192]{1,0:T(8,128)(2,1)} %q_ref.1) | copy-start | bytes 786436
  0.0 7.2 %copy-start.3 = (bf16[128,128]{1,0:T(8,128)(2,1)S(1)}, bf16[128,128]{1,0:T(8,128)(2,1)}, u32[]{:S(2)}) copy-start(bf16[128,128]{1,0:T(8,128)(2,1)} %constant.15.clone.table_ref) | copy-start | bytes 98308
  0.0 7.2 %copy-start.4 = (s32[16]{0:T(128)S(1)}, s32[16]{0:T(128)}, u32[]{:S(2)}) copy-start(s32[16]{0:T(128)} %len_ref.1) | copy-start | bytes 196
  2.4 19.7 %all-to-all-start.1 = ((bf16[8,128,512]{2,1,0:T(8,128)(2,1)}), bf16[8,128,512]{2,1,0:T(8,128)(2,1)S(1)}, u32[]{:S(2)}, u32[]{:S(2)}) async-start(bf16[8,128,512]{2,1,0:T(8,128)(2,1)} %bitcast.84), calls=%async_computation.1 | async-start | bytes 2097152 | tf_op jit(solution)/shard_map/all_to_all | solution.py:211
  7.2 1.6 copy-start
  8.8 1.6 copy-start.1
  60.3 7.7 %copy-start.8 = (f32[4096]{0:T(1024)S(1)}, f32[4096]{0:T(1024)}, u32[]{:S(2)}) copy-start(f32[4096]{0:T(1024)} %param.19) | copy-start | bytes 49156
  60.3 7.8 %copy-start.5 = (bf16[16,4096]{1,0:T(8,128)(2,1)S(1)}, bf16[16,4096]{1,0:T(8,128)(2,1)}, u32[]{:S(2)}) copy-start(bf16[16,4096]{1,0:T(8,128)(2,1)} %param.13) | copy-start | bytes 393220
  60.3 7.8 %copy-start.6 = (s32[16,8]{0,1:T(8,128)S(1)}, s32[16,8]{0,1:T(8,128)}, u32[]{:S(2)}) copy-start(s32[16,8]{0,1:T(8,128)} %param.20) | copy-start | bytes 1540
  60.3 21.0 %all-to-all-start.2 = ((bf16[64,16,512]{2,1,0:T(8,128)(2,1)}), bf16[64,16,512]{2,1,0:T(8,128)(2,1)}, u32[]{:S(2)}, u32[]{:S(2)}) async-start(bf16[64,16,512]{2,1,0:T(8,128)(2,1)} %bitcast.5), calls=%async_computation.2 | async-start | bytes 2097152 | tf_op jit(solution)/shard_map/all_to_all | solution.py:218
  68.0 55.2 %slice-start = ((s8[6291456]{0:T(1024)(128)(4,1)}), s8[2097152]{0:T(1024)(128)(4,1)S(1)}, s32[]{:S(2)}) async-start(s8[6291456]{0:T(1024)(128)(4,1)} %bitcast.88), calls=%async_computation.5 | async-start | bytes 4194304
  83.0 40.3 %slice-start.1 = ((s8[6291456]{0:T(1024)(128)(4,1)}), s8[4194304]{0:T(1024)(128)(4,1)S(1)}, s32[]{:S(2)}) async-start(s8[6291456]{0:T(1024)(128)(4,1)} %bitcast.88), calls=%async_computation.6 | async-start | bytes 8388608
  134.4 5.8 %copy-start.7 = (f32[16,8]{0,1:T(8,128)S(1)}, f32[16,8]{0,1:T(8,128)}, u32[]{:S(2)}) copy-start(f32[16,8]{0,1:T(8,128)} %param.21) | copy-start | bytes 1540
  134.4 35.1 %all-to-all-start.4 = ((bf16[128,16,512]{2,1,0:T(8,128)(2,1)}), bf16[128,16,512]{2,1,0:T(8,128)(2,1)S(1)}, u32[]{:S(2)}, u32[]{:S(2)}) async-start(bf16[128,16,512]{2,1,0:T(8,128)(2,1)} %bitcast.29), calls=%async_computation.4 | async-start | bytes 4194304 | tf_op jit(solution)/shard_map/all_to_all | solution.py:249

commit v5 on v4

--- a/solution.py
+++ b/solution.py
@@ -11,6 +11,10 @@
 
 BF16 = jnp.bfloat16
 F32 = jnp.float32
+
+
+def in_hbm(x):
+    return pltpu.with_memory_space_constraint(x, pltpu.HBM)
 
 
 def sign_table(order):
@@ -66,7 +70,7 @@
     return pl.pallas_call(
         functools.partial(attend_kernel, copies),
         grid=(kv_heads,),
-        out_shape=jax.ShapeDtypeStruct((clusters, copies, rows, columns), BF16),
+        out_shape=pltpu.HBM((clusters, copies, rows, columns), BF16),
         in_specs=[
             pl.BlockSpec(memory_space=pltpu.SMEM),
             pl.BlockSpec((rows, share), lambda i: (0, i)),
@@ -75,13 +79,13 @@
             pl.BlockSpec((dim, dim), lambda i: (0, 0)),
         ],
         out_specs=pl.BlockSpec((per, copies, rows, columns), lambda i: (i, 0, 0, 0)),
-        compiler_params=pltpu.CompilerParams(vmem_limit_bytes=24 * 1024 * 1024),
+        compiler_params=pltpu.CompilerParams(vmem_limit_bytes=60 * 1024 * 1024),
         cost_estimate=pl.CostEstimate(
             flops=4 * rows * queries.shape[1] * cache_len,
             bytes_accessed=4 * rows * kv_heads * cache_len * dim + 2 * clusters * copies * rows * columns,
             transcendentals=rows * queries.shape[1] // dim * cache_len,
         ),
-    )(lengths, queries, key_cache, value_cache, table)
+    )(lengths, queries, in_hbm(key_cache), in_hbm(value_cache), table)
 
 
 def expert_kernel(pieces, x_ref, gate_ref, up_hbm, down_hbm, out_hbm,
@@ -132,12 +136,12 @@
     operands = [
         pltpu.with_memory_space_constraint(a, pltpu.VMEM)
         for a in (x.reshape(groups, group, block), w_gate)
-    ] + [w_up, w_down]
+    ] + [in_hbm(w_up), in_hbm(w_down)]
     result = pl.pallas_call(
         functools.partial(expert_kernel, pieces),
-        out_shape=jax.ShapeDtypeStruct((groups, group, block), BF16),
-        in_specs=[pl.BlockSpec(memory_space=pltpu.VMEM)] * 2 + [pl.BlockSpec(memory_space=pl.ANY)] * 2,
-        out_specs=pl.BlockSpec(memory_space=pl.ANY),
+        out_shape=pltpu.HBM((groups, group, block), BF16),
+        in_specs=[pl.BlockSpec(memory_space=pltpu.VMEM)] * 2 + [pl.BlockSpec(memory_space=pltpu.HBM)] * 2,
+        out_specs=pl.BlockSpec(memory_space=pltpu.HBM),
         scratch_shapes=[
             pltpu.VMEM((width, hidden), BF16),
             pltpu.VMEM((hidden, width), BF16),
@@ -158,30 +162,58 @@
     return result.reshape(rows, block)
 
 
-def project_kernel(a_ref, w_ref, out_ref):
-    out_ref[...] = jnp.dot(a_ref[...], w_ref[...], preferred_element_type=F32).astype(BF16)
-
-
-def project(a, w):
+def project_kernel(me_ref, a_ref, mine_hbm, other_hbm, out_hbm, w_s, out_s, w_sem, o_sem):
+    members, half, _ = mine_hbm.shape
+    tiles, tile, _ = out_s.shape
+    moves = []
+    for n, source in enumerate((mine_hbm, other_hbm)):
+        first = me_ref[0] if n == 0 else 1 - me_ref[0]
+        for m in range(members):
+            at = pl.multiple_of((2 * m + first) * half, half)
+            moves.append(pltpu.make_async_copy(source.at[m], w_s.at[pl.ds(at, half)], w_sem.at[n, m]))
+    for move in moves:
+        move.start()
+    for move in moves:
+        move.wait()
+    stores = []
+    for t in range(tiles):
+        out_s[t] = jnp.dot(
+            a_ref[t * tile:(t + 1) * tile, :], w_s[...], preferred_element_type=F32
+        ).astype(BF16)
+        stores.append(pltpu.make_async_copy(out_s.at[t], out_hbm.at[t], o_sem.at[t]))
+        stores[-1].start()
+    for store in stores:
+        store.wait()
+
+
+def project(me, a, mine, other):
     rows, depth = a.shape
-    columns = w.shape[1]
-    tile = 256
-    return pl.pallas_call(
+    members, half, columns = mine.shape
+    tiles = 4
+    result = pl.pallas_call(
         project_kernel,
-        grid=(rows // tile,),
-        out_shape=jax.ShapeDtypeStruct((rows, columns), BF16),
+        out_shape=pltpu.HBM((tiles, rows // tiles, columns), BF16),
         in_specs=[
-            pl.BlockSpec((tile, depth), lambda i: (i, 0)),
-            pl.BlockSpec((depth, columns), lambda i: (0, 0)),
-        ],
-        out_specs=pl.BlockSpec((tile, columns), lambda i: (i, 0)),
-        compiler_params=pltpu.CompilerParams(vmem_limit_bytes=24 * 1024 * 1024),
+            pl.BlockSpec(memory_space=pltpu.SMEM),
+            pl.BlockSpec(memory_space=pltpu.VMEM),
+            pl.BlockSpec(memory_space=pltpu.HBM),
+            pl.BlockSpec(memory_space=pltpu.HBM),
+        ],
+        out_specs=pl.BlockSpec(memory_space=pltpu.HBM),
+        scratch_shapes=[
+            pltpu.VMEM((depth, columns), BF16),
+            pltpu.VMEM((tiles, rows // tiles, columns), BF16),
+            pltpu.SemaphoreType.DMA((2, members)),
+            pltpu.SemaphoreType.DMA((tiles,)),
+        ],
+        compiler_params=pltpu.CompilerParams(vmem_limit_bytes=12 * 1024 * 1024),
         cost_estimate=pl.CostEstimate(
             flops=2 * rows * depth * columns,
             bytes_accessed=2 * (rows * depth + depth * columns + rows * columns),
             transcendentals=0,
         ),
-    )(a, w)
+    )(me, pltpu.with_memory_space_constraint(a, pltpu.VMEM), in_hbm(mine), in_hbm(other))
+    return result.reshape(rows, columns)
 
 
 def shards(
@@ -207,14 +239,17 @@
     block = width // pieces
 
     teams = [[c * pieces + i for i in range(pieces)] for c in range(clusters)]
-    weight = out_weight.reshape(out_weight.shape[0], pieces, block).transpose(1, 0, 2)
-    weight = lax.all_to_all(weight, "dev", 0, 0, tiled=True, axis_index_groups=teams)
-    weight = weight.reshape(pieces * out_weight.shape[0], block)
+    core = lax.axis_index("role").astype(jnp.int32)
+    half = out_weight.shape[0] // 2
+    mine = lax.dynamic_slice_in_dim(out_weight, core * half, half, 0)
+    mine = mine.reshape(half, pieces, block).transpose(1, 0, 2)
+    mine = lax.all_to_all(mine, "dev", 0, 0, tiled=True, axis_index_groups=teams)
+    other = lax.ppermute(mine, "role", [(0, 1), (1, 0)])
 
     context = attend(lengths, queries, key_cache, value_cache, clusters, pieces)
     context = context.reshape(chips, rows, pieces * head_dim)
     context = lax.all_to_all(context, "dev", 0, 0, tiled=True)
-    part = project(context.reshape(chips * rows, pieces * head_dim), weight)
+    part = project(core.reshape(1), context.reshape(chips * rows, pieces * head_dim), mine, other)
     part = lax.all_to_all(part.reshape(chips, rows, block), "dev", 0, 0, tiled=True)
     attn = jnp.sum(part.reshape(clusters, pieces, rows, block).astype(F32), axis=0)
 

time: 173 us -> 171 us (0.988)
  blocking collectives: 74.6 us -> 39.3 us
  waiting for transfers between devices: 45.7 us -> 65.3 us
  starting transfers between devices: 18.4 us -> 31.1 us
  Pallas kernels: 19.3 us -> 21.5 us
  other arithmetic: 4.27 us -> 2.34 us
    all_to_all x1 -> x0, blocking collectives: 35.4 us -> none  [shards(): context = lax.all_to_all(context, 'dev', 0, 0, tiled=True)]
    all_to_all x1 -> x2, waiting for transfers between devices: 6.31 us -> 23.7 us  [the longest x1 22.9 us: shards(): context = lax.all_to_all(context, 'dev', 0, 0, tiled=True)]
    all_to_all x1 -> x2, starting transfers between devices: 4.82 us -> 15.8 us  [the longest x1 11 us: shards(): context = lax.all_to_all(context, 'dev', 0, 0, tiled=True)]
    ppermute x0 -> x1, waiting for transfers between devices: none -> 1.88 us  [shards(): other = lax.ppermute(mine, 'role', [(0, 1), (1, 0)])]
    unnamed x23 -> x15, local copies, waits for them, and re-layouts: 3.29 us -> 4.91 us
  transfers between devices with their start and end apart: 3 -> 5, of which waited for: 3 -> 5; matrix products, arithmetic and copies ran while one was open for 2% -> 1% of each run, Pallas kernels for 3% -> 4%
where the time goes in v5:
time: 171 us; the launch traced here: 170 us
  waiting for transfers between devices  65.3 us (38%)
  blocking collectives  39.3 us (23%)
  starting transfers between devices  31.1 us (18%)
  Pallas kernels  21.5 us (13%)
  local copies, waits for them, and re-layouts  6.97 us (4%)
  matrix products  3.36 us (2%)
  other arithmetic  2.34 us (1%)
    all_to_all x1, blocking collectives, shards(): lax.all_to_all(outgoing.reshape(expert_total, slots * pieces, block), ('r...  39.3 us
    all_to_all x1, waiting for transfers between devices, shards(): lax.all_to_all(result.reshape(expert_total, slots * pieces, block), ('rol...  27.2 us
    all_to_all x1, waiting for transfers between devices, shards(): context = lax.all_to_all(context, 'dev', 0, 0, tiled=True)  22.9 us
    all_to_all x1, waiting for transfers between devices, shards(): lax.all_to_all(part.reshape(chips, rows, block), 'dev', 0, 0, tiled=True)  12.5 us
    pallas_call x1, Pallas kernels, experts(): pl.pallas_call(functools.partial(expert_kernel, pieces), out_shape=pltpu....  11.1 us
    all_to_all x1, starting transfers between devices, shards(): context = lax.all_to_all(context, 'dev', 0, 0, tiled=True)  11 us
    all_to_all x1, starting transfers between devices, shards(): lax.all_to_all(part.reshape(chips, rows, block), 'dev', 0, 0, tiled=True)  7.54 us
    pallas_call x1, Pallas kernels, attend(): pl.pallas_call(functools.partial(attend_kernel, copies), grid=(kv_heads,)...  6.99 us
  transfers between devices with their start and end apart: 5, of which 5 were waited for; matrix products, arithmetic and copies ran while one was open for 1% of the time, Pallas kernels for 4%

profile of v5, /device:TPU:5, one launch (start us, length us, event | category | flops | bytes accessed | tf_op | source)
XLA Modules:
  0.0 169.9 jit_solution(3357744413683011711)
XLA Ops:
  0.0 0.0 copy-start
  0.0 1.2 copy-done
  1.3 0.8 copy.47
  2.1 4.8 %all-to-all-start.1 = ((bf16[8,64,512]{2,1,0:T(8,128)(2,1)}), bf16[8,64,512]{2,1,0:T(8,128)(2,1)S(1)}, u32[]{:S(2)}, u32[]{:S(2)}) async-start(bf16[8,64,512]{2,1,0:T(8,128)(2,1)} %bitcast.84), calls=%async_computation.1 | async-start | bytes 1048576 | tf_op jit(solution)/shard_map/all_to_all | solution.py:246
  6.9 7.0 %shard_map.127 = bf16[8,8,16,1024]{3,2,1,0:T(8,128)(2,1)} custom-call(s32[16]{0:T(128)} %len_ref.1, bf16[16,8192]{1,0:T(8,128)(2,1)} %q_ref.1, bf16[16,4,128,128]{3,2,1,0:T(8,128)(2,1)} %k_ref.1, bf16[16,4,128,128]{3,2,1,0:T(8,128)(2,1)} %v_ref.1, bf16[128,128]{1,0:T(8,128)(2,1)} %constant.25.clone.table_ref), custom_call_target="tpu_custom_call" | custom-call | flops 67108864 | bytes 6291456 | tf_op jit(solution)/shard_map/pallas_call | solution.py:70
  13.9 0.8 all-to-all-done.1.mine_hbm
  14.7 0.0 copy-start.2
  14.7 0.8 copy-done.2
  15.5 11.0 %all-to-all-start = ((bf16[64,16,1024]{2,1,0:T(8,128)(2,1)}), bf16[64,16,1024]{2,1,0:T(8,128)(2,1)S(1)}, u32[]{:S(2)}, u32[]{:S(2)}) async-start(bf16[64,16,1024]{2,1,0:T(8,128)(2,1)} %bitcast.88), calls=%async_computation | async-start | bytes 4194304 | tf_op jit(solution)/shard_map/all_to_all | solution.py:251
  26.6 1.4 collective-permute-start
  28.0 1.9 %collective-permute-done.other_hbm = bf16[8,64,512]{2,1,0:T(8,128)(2,1)} collective-permute-done((bf16[8,64,512]{2,1,0:T(8,128)(2,1)}, bf16[8,64,512]{2,1,0:T(8,128)(2,1)}, u32[]{:S(2)}, u32[]{:S(2)}) %collective-permute-start) | collective-permute-done | bytes 524320 | tf_op jit(solution)/shard_map/ppermute | solution.py:247
  29.9 22.9 %all-to-all-done = bf16[64,16,1024]{2,1,0:T(8,128)(2,1)S(1)} async-done(((bf16[64,16,1024]{2,1,0:T(8,128)(2,1)}), bf16[64,16,1024]{2,1,0:T(8,128)(2,1)S(1)}, u32[]{:S(2)}, u32[]{:S(2)}) %all-to-all-start) | async-done | bytes 2097184 | tf_op jit(solution)/shard_map/all_to_all | solution.py:251
  52.7 3.3 %shard_map.128 = bf16[4,256,512]{2,1,0:T(8,128)(2,1)} custom-call(s32[1]{0:T(128)} %bitcast.1.me_ref, bf16[1024,1024]{1,0:T(8,128)(2,1)S(1)} %bitcast.85, bf16[8,64,512]{2,1,0:T(8,128)(2,1)} %copy-done.2, bf16[8,64,512]{2,1,0:T(8,128)(2,1)} %collective-permute-done.other_hbm), custom_call_target="tpu_custom_call" | custom-call | flops 1073741824 | bytes 4194304 | tf_op jit(solution)/shard_map/pallas_call | solution.py:193
  56.1 0.0 copy-start.6
  56.1 0.0 copy-start.3
  56.1 0.0 copy-start.4
  56.1 7.5 %all-to-all-start.2 = ((bf16[64,16,512]{2,1,0:T(8,128)(2,1)}), bf16[64,16,512]{2,1,0:T(8,128)(2,1)S(1)}, u32[]{:S(2)}, u32[]{:S(2)}) async-start(bf16[64,16,512]{2,1,0:T(8,128)(2,1)} %bitcast.92), calls=%async_computation.2 | async-start | bytes 2097152 | tf_op jit(solution)/shard_map/all_to_all | solution.py:253
  63.7 0.0 copy-done.6
  63.7 0.0 copy-done.3
  63.7 0.0 copy-done.4
  63.7 0.1 copy.33
  63.8 0.1 eq.240
  63.9 0.2 convert_reduce_fusion.1
  64.1 0.1 reduce_sum.40
  64.2 0.1 copy.34
  64.3 0.1 add.69
  64.4 0.1 add.71
  64.5 12.5 %all-to-all-done.2 = bf16[64,16,512]{2,1,0:T(8,128)(2,1)S(1)} async-done(((bf16[64,16,512]{2,1,0:T(8,128)(2,1)}), bf16[64,16,512]{2,1,0:T(8,128)(2,1)S(1)}, u32[]{:S(2)}, u32[]{:S(2)}) %all-to-all-start.2) | async-done | bytes 1048608 | tf_op jit(solution)/shard_map/all_to_all | solution.py:253
  76.9 0.2 convert_reduce_fusion
  77.1 0.2 multiply_reduce_fusion
  77.3 0.1 multiply_convert_fusion
  77.4 1.1 convolution_convert_fusion
  78.5 39.3 %all_to_all.25 = bf16[128,16,512]{2,1,0:T(8,128)(2,1)S(1)} all-to-all(bf16[128,16,512]{2,1,0:T(8,128)(2,1)S(1)} %bitcast.97), channel_id=1, replica_groups=mesh['role'=2,'dev'=64] {'role','dev'}, dimensions={0} | all-to-all | bytes 4194304 | tf_op jit(solution)/shard_map/all_to_all | solution.py:278
  117.7 0.0 copy-start.1
  117.7 2.8 %copy-done.1 = bf16[1,4096,768]{2,1,0:T(8,128)(2,1)S(1)} copy-done((bf16[1,4096,768]{2,1,0:T(8,128)(2,1)S(1)}, bf16[1,4096,768]{2,1,0:T(8,128)(2,1)}, u32[]{:S(2)}) %copy-start.1) | copy-done | bytes 6291480
  120.5 11.1 %shard_map.129 = bf16[8,256,512]{2,1,0:T(8,128)(2,1)} custom-call(bf16[8,256,512]{2,1,0:T(8,128)(2,1)S(1)} %bitcast.86, bf16[4096,768]{1,0:T(8,128)(2,1)S(1)} %bitcast.87, bf16[4096,768]{1,0:T(8,128)(2,1)} %bitcast.90, bf16[768,4096]{1,0:T(8,128)(2,1)} %bitcast.91), custom_call_target="tpu_custom_call" | custom-call | flops 4831838208 | bytes 16777216 | tf_op jit(solution)/shard_map/pallas_call | solution.py:140
  131.6 0.0 copy-start.5
  131.7 6.3 %all-to-all-start.4 = ((bf16[128,16,512]{2,1,0:T(8,128)(2,1)}), bf16[128,16,512]{2,1,0:T(8,128)(2,1)}, u32[]{:S(2)}, u32[]{:S(2)}) async-start(bf16[128,16,512]{2,1,0:T(8,128)(2,1)} %bitcast.89), calls=%async_computation.4 | async-start | bytes 4194304 | tf_op jit(solution)/shard_map/all_to_all | solution.py:284
  137.9 0.0 copy-done.5
  138.0 0.1 reshape.70
  138.1 1.6 reduce-precision_convert_fusion
  139.6 27.2 %all-to-all-done.4 = bf16[128,16,512]{2,1,0:T(8,128)(2,1)} async-done(((bf16[128,16,512]{2,1,0:T(8,128)(2,1)}), bf16[128,16,512]{2,1,0:T(8,128)(2,1)}, u32[]{:S(2)}, u32[]{:S(2)}) %all-to-all-start.4) | async-done | bytes 2097184 | tf_op jit(solution)/shard_map/all_to_all | solution.py:284
  166.9 2.3 %fusion.1 = f32[256,512]{1,0:T(8,128)S(1)} fusion(bf16[2048,512]{1,0:T(8,128)(2,1)} %bitcast.30, bf16[128,2048]{1,0:T(8,128)(2,1)S(1)} %get-tuple-element.6, bf16[128,2048]{1,0:T(8,128)(2,1)S(1)} %get-tuple-element.5), kind=kOutput, calls=%fused_computation.5 | convolution fusion | flops 538968064 | bytes 3670016 | tf_op jit(solution)/shard_map/dot_general | solution.py:296
  169.2 0.1 fusion.22
  169.3 0.7 copy.38
  (14 shorter events, 0.2 us)
Async XLA Ops:
  0.0 1.2 copy-start
  2.1 12.6 %all-to-all-start.1 = ((bf16[8,64,512]{2,1,0:T(8,128)(2,1)}), bf16[8,64,512]{2,1,0:T(8,128)(2,1)S(1)}, u32[]{:S(2)}, u32[]{:S(2)}) async-start(bf16[8,64,512]{2,1,0:T(8,128)(2,1)} %bitcast.84), calls=%async_computation.1 | async-start | bytes 1048576 | tf_op jit(solution)/shard_map/all_to_all | solution.py:246
  14.7 0.8 copy-start.2
  15.5 37.2 %all-to-all-start = ((bf16[64,16,1024]{2,1,0:T(8,128)(2,1)}), bf16[64,16,1024]{2,1,0:T(8,128)(2,1)S(1)}, u32[]{:S(2)}, u32[]{:S(2)}) async-start(bf16[64,16,1024]{2,1,0:T(8,128)(2,1)} %bitcast.88), calls=%async_computation | async-start | bytes 4194304 | tf_op jit(solution)/shard_map/all_to_all | solution.py:251
  26.6 3.3 %collective-permute-start = (bf16[8,64,512]{2,1,0:T(8,128)(2,1)}, bf16[8,64,512]{2,1,0:T(8,128)(2,1)}, u32[]{:S(2)}, u32[]{:S(2)}) collective-permute-start(bf16[8,64,512]{2,1,0:T(8,128)(2,1)} %copy-done.2), channel_id=1, source_target_pairs={{0,64},{64,0},{1,65},{65,1},{2,66},{66,2},{3,67},{67,3},{4,68},{68... | collective-permute-start | bytes 1572872 | tf_op jit(solution)/shard_map/ppermute | solution.py:247
  56.1 7.6 %copy-start.6 = (f32[4096]{0:T(1024)S(1)}, f32[4096]{0:T(1024)}, u32[]{:S(2)}) copy-start(f32[4096]{0:T(1024)} %param.19) | copy-start | bytes 49156
  56.1 7.6 %copy-start.3 = (bf16[16,4096]{1,0:T(8,128)(2,1)S(1)}, bf16[16,4096]{1,0:T(8,128)(2,1)}, u32[]{:S(2)}) copy-start(bf16[16,4096]{1,0:T(8,128)(2,1)} %param.13) | copy-start | bytes 393220
  56.1 7.6 %copy-start.4 = (s32[16,8]{0,1:T(8,128)S(1)}, s32[16,8]{0,1:T(8,128)}, u32[]{:S(2)}) copy-start(s32[16,8]{0,1:T(8,128)} %param.20) | copy-start | bytes 1540
  56.1 20.8 %all-to-all-start.2 = ((bf16[64,16,512]{2,1,0:T(8,128)(2,1)}), bf16[64,16,512]{2,1,0:T(8,128)(2,1)S(1)}, u32[]{:S(2)}, u32[]{:S(2)}) async-start(bf16[64,16,512]{2,1,0:T(8,128)(2,1)} %bitcast.92), calls=%async_computation.2 | async-start | bytes 2097152 | tf_op jit(solution)/shard_map/all_to_all | solution.py:253
  117.7 2.8 %copy-start.1 = (bf16[1,4096,768]{2,1,0:T(8,128)(2,1)S(1)}, bf16[1,4096,768]{2,1,0:T(8,128)(2,1)}, u32[]{:S(2)}) copy-start(bf16[1,4096,768]{2,1,0:T(8,128)(2,1)} %param.22) | copy-start | bytes 18874372
  131.6 6.3 %copy-start.5 = (f32[16,8]{0,1:T(8,128)S(1)}, f32[16,8]{0,1:T(8,128)}, u32[]{:S(2)}) copy-start(f32[16,8]{0,1:T(8,128)} %param.21) | copy-start | bytes 1540
  131.7 35.2 %all-to-all-start.4 = ((bf16[128,16,512]{2,1,0:T(8,128)(2,1)}), bf16[128,16,512]{2,1,0:T(8,128)(2,1)}, u32[]{:S(2)}, u32[]{:S(2)}) async-start(bf16[128,16,512]{2,1,0:T(8,128)(2,1)} %bitcast.89), calls=%async_computation.4 | async-start | bytes 4194304 | tf_op jit(solution)/shard_map/all_to_all | solution.py:284

commit v6 on v5

--- a/solution.py
+++ b/solution.py
@@ -88,14 +88,30 @@
     )(lengths, queries, in_hbm(key_cache), in_hbm(value_cache), table)
 
 
-def expert_kernel(pieces, x_ref, gate_ref, up_hbm, down_hbm, out_hbm,
-                  up_ref, down_ref, x_s, act_s, res_s, out_s, w_sem, o_sem):
+WIDE, TALL, AHEAD = 384, 2048, 2
+
+
+def expert_kernel(pieces, x_ref, gate_hbm, up_hbm, down_hbm, out_hbm,
+                  gate_s, up_s, down_s, x_s, act_s, res_s, out_s, w_sem, d_sem, o_sem):
     group, block = x_ref.shape[1:]
     span = group // pieces
-    fetch_up = pltpu.make_async_copy(up_hbm, up_ref, w_sem.at[0])
-    fetch_down = pltpu.make_async_copy(down_hbm, down_ref, w_sem.at[1])
-    fetch_up.start()
-    fetch_down.start()
+    parts, _, wide = gate_s.shape
+    outs, _, tall = down_s.shape
+    loads = []
+    for i in range(parts):
+        cut = pl.ds(i * wide, wide)
+        loads.append(pltpu.make_async_copy(gate_hbm.at[:, cut], gate_s.at[i], w_sem.at[i, 0]))
+        loads.append(pltpu.make_async_copy(up_hbm.at[:, cut], up_s.at[i], w_sem.at[i, 1]))
+    for i in range(outs):
+        loads.append(pltpu.make_async_copy(down_hbm.at[:, pl.ds(i * tall, tall)], down_s.at[i], d_sem.at[i]))
+
+    def arrive(n):
+        loads[n].wait()
+        if n + AHEAD < len(loads):
+            loads[n + AHEAD].start()
+
+    for first in loads[:AHEAD]:
+        first.start()
     row = lax.broadcasted_iota(jnp.int32, (group, group), 0)
     col = lax.broadcasted_iota(jnp.int32, (group, group), 1)
     spread = (col == (row % span) * pieces + row // span).astype(F32).astype(BF16)
@@ -104,17 +120,17 @@
         y = jnp.dot(spread, x_ref[g], preferred_element_type=F32).astype(BF16)
         for j in range(pieces):
             x_s[g * span:(g + 1) * span, j * block:(j + 1) * block] = y[j * span:(j + 1) * span, :]
-    gate = jnp.dot(x_s[...], gate_ref[...], preferred_element_type=F32)
-    gate = gate / (1.0 + jnp.exp(-gate))
-    fetch_up.wait()
-    up = jnp.dot(x_s[...], up_ref[...], preferred_element_type=F32)
-    act_s[...] = (gate * up).astype(BF16)
-    fetch_down.wait()
-    tall = 2 * block
-    for i in range(down_ref.shape[1] // tall):
-        y = jnp.dot(act_s[...], down_ref[:, i * tall:(i + 1) * tall], preferred_element_type=F32).astype(BF16)
-        for n in range(2):
-            j = i * 2 + n
+    for i in range(parts):
+        arrive(2 * i)
+        gate = jnp.dot(x_s[...], gate_s[i], preferred_element_type=F32)
+        arrive(2 * i + 1)
+        up = jnp.dot(x_s[...], up_s[i], preferred_element_type=F32)
+        act_s[:, i * wide:(i + 1) * wide] = (gate / (1.0 + jnp.exp(-gate)) * up).astype(BF16)
+    for i in range(outs):
+        arrive(2 * parts + i)
+        y = jnp.dot(act_s[...], down_s[i], preferred_element_type=F32).astype(BF16)
+        for n in range(tall // block):
+            j = i * (tall // block) + n
             for g in range(x_ref.shape[0]):
                 res_s[g, j * span:(j + 1) * span, :] = y[g * span:(g + 1) * span, n * block:(n + 1) * block]
     stores = []
@@ -133,29 +149,30 @@
     tokens = rows // pieces
     groups = pieces
     group = rows // groups
-    operands = [
-        pltpu.with_memory_space_constraint(a, pltpu.VMEM)
-        for a in (x.reshape(groups, group, block), w_gate)
-    ] + [in_hbm(w_up), in_hbm(w_down)]
+    wide, tall = min(WIDE, hidden), min(TALL, width)
+    operands = [pltpu.with_memory_space_constraint(x.reshape(groups, group, block), pltpu.VMEM)]
+    operands += [in_hbm(w_gate), in_hbm(w_up), in_hbm(w_down)]
     result = pl.pallas_call(
         functools.partial(expert_kernel, pieces),
         out_shape=pltpu.HBM((groups, group, block), BF16),
-        in_specs=[pl.BlockSpec(memory_space=pltpu.VMEM)] * 2 + [pl.BlockSpec(memory_space=pltpu.HBM)] * 2,
+        in_specs=[pl.BlockSpec(memory_space=pltpu.VMEM)] + [pl.BlockSpec(memory_space=pltpu.HBM)] * 3,
         out_specs=pl.BlockSpec(memory_space=pltpu.HBM),
         scratch_shapes=[
-            pltpu.VMEM((width, hidden), BF16),
-            pltpu.VMEM((hidden, width), BF16),
+            pltpu.VMEM((hidden // wide, width, wide), BF16),
+            pltpu.VMEM((hidden // wide, width, wide), BF16),
+            pltpu.VMEM((width // tall, hidden, tall), BF16),
             pltpu.VMEM((tokens, width), BF16),
             pltpu.VMEM((tokens, hidden), BF16),
             pltpu.VMEM((groups, group, block), BF16),
             pltpu.VMEM((groups, group, block), BF16),
-            pltpu.SemaphoreType.DMA((2,)),
+            pltpu.SemaphoreType.DMA((hidden // wide, 2)),
+            pltpu.SemaphoreType.DMA((width // tall,)),
             pltpu.SemaphoreType.DMA((groups,)),
         ],
-        compiler_params=pltpu.CompilerParams(vmem_limit_bytes=40 * 1024 * 1024),
+        compiler_params=pltpu.CompilerParams(vmem_limit_bytes=48 * 1024 * 1024),
         cost_estimate=pl.CostEstimate(
             flops=6 * tokens * width * hidden,
-            bytes_accessed=4 * width * hidden + 4 * rows * block,
+            bytes_accessed=6 * width * hidden + 4 * rows * block,
             transcendentals=tokens * hidden,
         ),
     )(*operands)

time: 171 us -> 168 us (0.982)
  local copies, waits for them, and re-layouts: 6.97 us -> 4.2 us
    unnamed x15 -> x13, local copies, waits for them, and re-layouts: 4.91 us -> 2.13 us
where the time goes in v6:
time: 168 us; the launch traced here: 167 us
  waiting for transfers between devices  65.3 us (39%)
  blocking collectives  39.3 us (23%)
  starting transfers between devices  31.1 us (19%)
  Pallas kernels  21.3 us (13%)
  local copies, waits for them, and re-layouts  4.2 us (2%)
  matrix products  3.36 us (2%)
  other arithmetic  2.34 us (1%)
    all_to_all x1, blocking collectives, shards(): lax.all_to_all(outgoing.reshape(expert_total, slots * pieces, block), ('r...  39.3 us
    all_to_all x1, waiting for transfers between devices, shards(): lax.all_to_all(result.reshape(expert_total, slots * pieces, block), ('rol...  27.2 us
    all_to_all x1, waiting for transfers between devices, shards(): context = lax.all_to_all(context, 'dev', 0, 0, tiled=True)  22.9 us
    all_to_all x1, waiting for transfers between devices, shards(): lax.all_to_all(part.reshape(chips, rows, block), 'dev', 0, 0, tiled=True)  12.5 us
    all_to_all x1, starting transfers between devices, shards(): context = lax.all_to_all(context, 'dev', 0, 0, tiled=True)  11 us
    pallas_call x1, Pallas kernels, experts(): pl.pallas_call(functools.partial(expert_kernel, pieces), out_shape=pltpu....  11 us
    all_to_all x1, starting transfers between devices, shards(): lax.all_to_all(part.reshape(chips, rows, block), 'dev', 0, 0, tiled=True)  7.54 us
    pallas_call x1, Pallas kernels, attend(): pl.pallas_call(functools.partial(attend_kernel, copies), grid=(kv_heads,)...  7 us
  transfers between devices with their start and end apart: 5, of which 5 were waited for; matrix products, arithmetic and copies ran while one was open for 1% of the time, Pallas kernels for 4%

profile of v6, /device:TPU:5, one launch (start us, length us, event | category | flops | bytes accessed | tf_op | source)
XLA Modules:
  0.0 167.0 jit_solution(16843087815501249594)
XLA Ops:
  0.0 0.0 copy-start
  0.0 1.2 copy-done
  1.3 0.8 copy.47
  2.1 4.8 %all-to-all-start.1 = ((bf16[8,64,512]{2,1,0:T(8,128)(2,1)}), bf16[8,64,512]{2,1,0:T(8,128)(2,1)S(1)}, u32[]{:S(2)}, u32[]{:S(2)}) async-start(bf16[8,64,512]{2,1,0:T(8,128)(2,1)} %bitcast.84), calls=%async_computation.1 | async-start | bytes 1048576 | tf_op jit(solution)/shard_map/all_to_all | solution.py:263
  6.9 7.0 %shard_map.127 = bf16[8,8,16,1024]{3,2,1,0:T(8,128)(2,1)} custom-call(s32[16]{0:T(128)} %len_ref.1, bf16[16,8192]{1,0:T(8,128)(2,1)} %q_ref.1, bf16[16,4,128,128]{3,2,1,0:T(8,128)(2,1)} %k_ref.1, bf16[16,4,128,128]{3,2,1,0:T(8,128)(2,1)} %v_ref.1, bf16[128,128]{1,0:T(8,128)(2,1)} %constant.25.clone.table_ref), custom_call_target="tpu_custom_call" | custom-call | flops 67108864 | bytes 6291456 | tf_op jit(solution)/shard_map/pallas_call | solution.py:70
  13.9 0.8 all-to-all-done.1.mine_hbm
  14.7 0.0 copy-start.1
  14.7 0.8 copy-done.1
  15.5 11.0 %all-to-all-start = ((bf16[64,16,1024]{2,1,0:T(8,128)(2,1)}), bf16[64,16,1024]{2,1,0:T(8,128)(2,1)S(1)}, u32[]{:S(2)}, u32[]{:S(2)}) async-start(bf16[64,16,1024]{2,1,0:T(8,128)(2,1)} %bitcast.87), calls=%async_computation | async-start | bytes 4194304 | tf_op jit(solution)/shard_map/all_to_all | solution.py:268
  26.6 1.4 collective-permute-start
  28.0 1.9 %collective-permute-done.other_hbm = bf16[8,64,512]{2,1,0:T(8,128)(2,1)} collective-permute-done((bf16[8,64,512]{2,1,0:T(8,128)(2,1)}, bf16[8,64,512]{2,1,0:T(8,128)(2,1)}, u32[]{:S(2)}, u32[]{:S(2)}) %collective-permute-start) | collective-permute-done | bytes 524320 | tf_op jit(solution)/shard_map/ppermute | solution.py:264
  29.9 22.9 %all-to-all-done = bf16[64,16,1024]{2,1,0:T(8,128)(2,1)S(1)} async-done(((bf16[64,16,1024]{2,1,0:T(8,128)(2,1)}), bf16[64,16,1024]{2,1,0:T(8,128)(2,1)S(1)}, u32[]{:S(2)}, u32[]{:S(2)}) %all-to-all-start) | async-done | bytes 2097184 | tf_op jit(solution)/shard_map/all_to_all | solution.py:268
  52.7 3.4 %shard_map.128 = bf16[4,256,512]{2,1,0:T(8,128)(2,1)} custom-call(s32[1]{0:T(128)} %bitcast.1.me_ref, bf16[1024,1024]{1,0:T(8,128)(2,1)S(1)} %bitcast.85, bf16[8,64,512]{2,1,0:T(8,128)(2,1)} %copy-done.1, bf16[8,64,512]{2,1,0:T(8,128)(2,1)} %collective-permute-done.other_hbm), custom_call_target="tpu_custom_call" | custom-call | flops 1073741824 | bytes 4194304 | tf_op jit(solution)/shard_map/pallas_call | solution.py:210
  56.1 0.0 copy-start.5
  56.1 0.0 copy-start.2
  56.1 0.0 copy-start.3
  56.1 7.5 %all-to-all-start.2 = ((bf16[64,16,512]{2,1,0:T(8,128)(2,1)}), bf16[64,16,512]{2,1,0:T(8,128)(2,1)S(1)}, u32[]{:S(2)}, u32[]{:S(2)}) async-start(bf16[64,16,512]{2,1,0:T(8,128)(2,1)} %bitcast.92), calls=%async_computation.2 | async-start | bytes 2097152 | tf_op jit(solution)/shard_map/all_to_all | solution.py:270
  63.7 0.0 copy-done.5
  63.7 0.0 copy-done.2
  63.7 0.0 copy-done.3
  63.8 0.1 copy.33
  63.8 0.1 eq.240
  63.9 0.2 convert_reduce_fusion.1
  64.1 0.1 reduce_sum.40
  64.2 0.1 copy.34
  64.3 0.1 add.69
  64.4 0.1 add.71
  64.5 12.5 %all-to-all-done.2 = bf16[64,16,512]{2,1,0:T(8,128)(2,1)S(1)} async-done(((bf16[64,16,512]{2,1,0:T(8,128)(2,1)}), bf16[64,16,512]{2,1,0:T(8,128)(2,1)S(1)}, u32[]{:S(2)}, u32[]{:S(2)}) %all-to-all-start.2) | async-done | bytes 1048608 | tf_op jit(solution)/shard_map/all_to_all | solution.py:270
  77.0 0.2 convert_reduce_fusion
  77.1 0.2 multiply_reduce_fusion
  77.3 0.1 multiply_convert_fusion
  77.4 1.1 convolution_convert_fusion
  78.5 39.3 %all_to_all.25 = bf16[128,16,512]{2,1,0:T(8,128)(2,1)S(1)} all-to-all(bf16[128,16,512]{2,1,0:T(8,128)(2,1)S(1)} %bitcast.97), channel_id=1, replica_groups=mesh['role'=2,'dev'=64] {'role','dev'}, dimensions={0} | all-to-all | bytes 4194304 | tf_op jit(solution)/shard_map/all_to_all | solution.py:295
  117.7 11.0 %shard_map.129 = bf16[8,256,512]{2,1,0:T(8,128)(2,1)} custom-call(bf16[8,256,512]{2,1,0:T(8,128)(2,1)S(1)} %bitcast.86, bf16[4096,768]{1,0:T(8,128)(2,1)} %bitcast.89, bf16[4096,768]{1,0:T(8,128)(2,1)} %bitcast.90, bf16[768,4096]{1,0:T(8,128)(2,1)} %bitcast.91), custom_call_target="tpu_custom_call" | custom-call | flops 4831838208 | bytes 23068672 | tf_op jit(solution)/shard_map/pallas_call | solution.py:155
  128.7 0.0 copy-start.4
  128.7 6.3 %all-to-all-start.4 = ((bf16[128,16,512]{2,1,0:T(8,128)(2,1)}), bf16[128,16,512]{2,1,0:T(8,128)(2,1)}, u32[]{:S(2)}, u32[]{:S(2)}) async-start(bf16[128,16,512]{2,1,0:T(8,128)(2,1)} %bitcast.88), calls=%async_computation.4 | async-start | bytes 4194304 | tf_op jit(solution)/shard_map/all_to_all | solution.py:301
  135.0 0.0 copy-done.4
  135.1 0.1 reshape.70
  135.2 1.6 reduce-precision_convert_fusion
  136.7 27.2 %all-to-all-done.4 = bf16[128,16,512]{2,1,0:T(8,128)(2,1)} async-done(((bf16[128,16,512]{2,1,0:T(8,128)(2,1)}), bf16[128,16,512]{2,1,0:T(8,128)(2,1)}, u32[]{:S(2)}, u32[]{:S(2)}) %all-to-all-start.4) | async-done | bytes 2097184 | tf_op jit(solution)/shard_map/all_to_all | solution.py:301
  164.0 2.3 %fusion.1 = f32[256,512]{1,0:T(8,128)S(1)} fusion(bf16[2048,512]{1,0:T(8,128)(2,1)} %bitcast.30, bf16[128,2048]{1,0:T(8,128)(2,1)S(1)} %get-tuple-element.6, bf16[128,2048]{1,0:T(8,128)(2,1)S(1)} %get-tuple-element.5), kind=kOutput, calls=%fused_computation.5 | convolution fusion | flops 538968064 | bytes 3670016 | tf_op jit(solution)/shard_map/dot_general | solution.py:313
  166.3 0.1 fusion.22
  166.4 0.7 copy.38
  (14 shorter events, 0.2 us)
Async XLA Ops:
  0.0 1.2 copy-start
  2.1 12.6 %all-to-all-start.1 = ((bf16[8,64,512]{2,1,0:T(8,128)(2,1)}), bf16[8,64,512]{2,1,0:T(8,128)(2,1)S(1)}, u32[]{:S(2)}, u32[]{:S(2)}) async-start(bf16[8,64,512]{2,1,0:T(8,128)(2,1)} %bitcast.84), calls=%async_computation.1 | async-start | bytes 1048576 | tf_op jit(solution)/shard_map/all_to_all | solution.py:263
  14.7 0.8 copy-start.1
  15.5 37.2 %all-to-all-start = ((bf16[64,16,1024]{2,1,0:T(8,128)(2,1)}), bf16[64,16,1024]{2,1,0:T(8,128)(2,1)S(1)}, u32[]{:S(2)}, u32[]{:S(2)}) async-start(bf16[64,16,1024]{2,1,0:T(8,128)(2,1)} %bitcast.87), calls=%async_computation | async-start | bytes 4194304 | tf_op jit(solution)/shard_map/all_to_all | solution.py:268
  26.6 3.3 %collective-permute-start = (bf16[8,64,512]{2,1,0:T(8,128)(2,1)}, bf16[8,64,512]{2,1,0:T(8,128)(2,1)}, u32[]{:S(2)}, u32[]{:S(2)}) collective-permute-start(bf16[8,64,512]{2,1,0:T(8,128)(2,1)} %copy-done.1), channel_id=1, source_target_pairs={{0,64},{64,0},{1,65},{65,1},{2,66},{66,2},{3,67},{67,3},{4,68},{68... | collective-permute-start | bytes 1572872 | tf_op jit(solution)/shard_map/ppermute | solution.py:264
  56.1 7.6 %copy-start.5 = (f32[4096]{0:T(1024)S(1)}, f32[4096]{0:T(1024)}, u32[]{:S(2)}) copy-start(f32[4096]{0:T(1024)} %param.19) | copy-start | bytes 49156
  56.1 7.6 %copy-start.2 = (bf16[16,4096]{1,0:T(8,128)(2,1)S(1)}, bf16[16,4096]{1,0:T(8,128)(2,1)}, u32[]{:S(2)}) copy-start(bf16[16,4096]{1,0:T(8,128)(2,1)} %param.13) | copy-start | bytes 393220
  56.1 7.6 %copy-start.3 = (s32[16,8]{0,1:T(8,128)S(1)}, s32[16,8]{0,1:T(8,128)}, u32[]{:S(2)}) copy-start(s32[16,8]{0,1:T(8,128)} %param.20) | copy-start | bytes 1540
  56.1 20.8 %all-to-all-start.2 = ((bf16[64,16,512]{2,1,0:T(8,128)(2,1)}), bf16[64,16,512]{2,1,0:T(8,128)(2,1)S(1)}, u32[]{:S(2)}, u32[]{:S(2)}) async-start(bf16[64,16,512]{2,1,0:T(8,128)(2,1)} %bitcast.92), calls=%async_computation.2 | async-start | bytes 2097152 | tf_op jit(solution)/shard_map/all_to_all | solution.py:270
  128.7 6.3 %copy-start.4 = (f32[16,8]{0,1:T(8,128)S(1)}, f32[16,8]{0,1:T(8,128)}, u32[]{:S(2)}) copy-start(f32[16,8]{0,1:T(8,128)} %param.21) | copy-start | bytes 1540
  128.7 35.2 %all-to-all-start.4 = ((bf16[128,16,512]{2,1,0:T(8,128)(2,1)}), bf16[128,16,512]{2,1,0:T(8,128)(2,1)}, u32[]{:S(2)}, u32[]{:S(2)}) async-start(bf16[128,16,512]{2,1,0:T(8,128)(2,1)} %bitcast.88), calls=%async_computation.4 | async-start | bytes 4194304 | tf_op jit(solution)/shard_map/all_to_all | solution.py:301

commit v7 on v6

--- a/solution.py
+++ b/solution.py
@@ -252,23 +252,26 @@
     width = residual_in.shape[1]
     chips = lax.axis_size("dev")
     pieces = 8
-    clusters = chips // pieces
+    members = 4
+    clusters = chips // members
     block = width // pieces
 
-    teams = [[c * pieces + i for i in range(pieces)] for c in range(clusters)]
+    teams = [[c * members + i for i in range(members)] for c in range(clusters)]
     core = lax.axis_index("role").astype(jnp.int32)
     half = out_weight.shape[0] // 2
     mine = lax.dynamic_slice_in_dim(out_weight, core * half, half, 0)
-    mine = mine.reshape(half, pieces, block).transpose(1, 0, 2)
+    mine = mine.reshape(half, members, width // members).transpose(1, 0, 2)
     mine = lax.all_to_all(mine, "dev", 0, 0, tiled=True, axis_index_groups=teams)
     other = lax.ppermute(mine, "role", [(0, 1), (1, 0)])
 
-    context = attend(lengths, queries, key_cache, value_cache, clusters, pieces)
-    context = context.reshape(chips, rows, pieces * head_dim)
+    context = attend(lengths, queries, key_cache, value_cache, clusters, members)
+    context = context.reshape(chips, rows, members * head_dim)
     context = lax.all_to_all(context, "dev", 0, 0, tiled=True)
-    part = project(core.reshape(1), context.reshape(chips * rows, pieces * head_dim), mine, other)
-    part = lax.all_to_all(part.reshape(chips, rows, block), "dev", 0, 0, tiled=True)
-    attn = jnp.sum(part.reshape(clusters, pieces, rows, block).astype(F32), axis=0)
+    part = project(core.reshape(1), context.reshape(chips * rows, members * head_dim), mine, other)
+    part = lax.all_to_all(part.reshape(chips, rows, width // members), "dev", 0, 0, tiled=True)
+    attn = jnp.sum(part.reshape(clusters, members, rows, width // members).astype(F32), axis=0)
+    attn = attn.reshape(members, rows, pieces // members, block).transpose(0, 2, 1, 3)
+    attn = attn.reshape(pieces, rows, block)
 
     residual = residual_in.reshape(rows, pieces, block).transpose(1, 0, 2)
     hidden = residual.astype(F32) + attn

time: 168 us -> 165 us (0.982)
  starting transfers between devices: 31.1 us -> 29.3 us
    all_to_all x1, waiting for transfers between devices: 22.9 us -> 10.5 us  [shards(): context = lax.all_to_all(context, 'dev', 0, 0, tiled=True)]
    all_to_all x1, waiting for transfers between devices: 12.5 us -> 24 us  [shards(): lax.all_to_all(part.reshape(chips, rows, width // members), 'dev', 0, 0,...]
  transfers between devices with their start and end apart: 5 -> 5, of which waited for: 5 -> 5; matrix products, arithmetic and copies ran while one was open for 1% -> 2% of each run, Pallas kernels for 4% -> 4%
where the time goes in v7:
time: 165 us; the launch traced here: 164 us
  waiting for transfers between devices  64.8 us (39%)
  blocking collectives  38.9 us (24%)
  starting transfers between devices  29.3 us (18%)
  Pallas kernels  21.1 us (13%)
  local copies, waits for them, and re-layouts  4.14 us (3%)
  matrix products  3.36 us (2%)
  other arithmetic  2.58 us (2%)
    all_to_all x1, blocking collectives, shards(): lax.all_to_all(outgoing.reshape(expert_total, slots * pieces, block), ('r...  38.9 us
    all_to_all x1, waiting for transfers between devices, shards(): lax.all_to_all(result.reshape(expert_total, slots * pieces, block), ('rol...  27.2 us
    all_to_all x1, waiting for transfers between devices, shards(): lax.all_to_all(part.reshape(chips, rows, width // members), 'dev', 0, 0,...  24 us
    pallas_call x1, Pallas kernels, experts(): pl.pallas_call(functools.partial(expert_kernel, pieces), out_shape=pltpu....  11 us
    all_to_all x1, waiting for transfers between devices, shards(): context = lax.all_to_all(context, 'dev', 0, 0, tiled=True)  10.5 us
    all_to_all x1, starting transfers between devices, shards(): context = lax.all_to_all(context, 'dev', 0, 0, tiled=True)  9.42 us
    all_to_all x1, starting transfers between devices, shards(): lax.all_to_all(part.reshape(chips, rows, width // members), 'dev', 0, 0,...  7.16 us
    pallas_call x1, Pallas kernels, attend(): pl.pallas_call(functools.partial(attend_kernel, copies), grid=(kv_heads,)...  6.7 us
  transfers between devices with their start and end apart: 5, of which 5 were waited for; matrix products, arithmetic and copies ran while one was open for 2% of the time, Pallas kernels for 4%

profile of v7, /device:TPU:5, one launch (start us, length us, event | category | flops | bytes accessed | tf_op | source)
XLA Modules:
  0.0 164.5 jit_solution(5521924769737924703)
XLA Ops:
  0.0 0.0 copy-start
  0.0 1.2 copy-done
  1.3 0.9 copy.47
  2.1 4.2 %all-to-all-start.1 = ((bf16[4,64,1024]{2,1,0:T(8,128)(2,1)}), bf16[4,64,1024]{2,1,0:T(8,128)(2,1)S(1)}, u32[]{:S(2)}, u32[]{:S(2)}) async-start(bf16[4,64,1024]{2,1,0:T(8,128)(2,1)} %bitcast.85), calls=%async_computation.1 | async-start | bytes 1048576 | tf_op jit(solution)/shard_map/all_to_all | solution.py:264
  6.3 6.7 %shard_map.127 = bf16[16,4,16,512]{3,2,1,0:T(8,128)(2,1)} custom-call(s32[16]{0:T(128)} %len_ref.1, bf16[16,8192]{1,0:T(8,128)(2,1)} %q_ref.1, bf16[16,4,128,128]{3,2,1,0:T(8,128)(2,1)} %k_ref.1, bf16[16,4,128,128]{3,2,1,0:T(8,128)(2,1)} %v_ref.1, bf16[128,128]{1,0:T(8,128)(2,1)} %constant.25.clone.table_ref), custom_call_target="tpu_custom_call" | custom-call | flops 67108864 | bytes 5242880 | tf_op jit(solution)/shard_map/pallas_call | solution.py:70
  13.0 1.6 all-to-all-done.1.mine_hbm
  14.6 0.0 copy-start.1
  14.6 9.4 %all-to-all-start = ((bf16[64,16,512]{2,1,0:T(8,128)(2,1)}), bf16[64,16,512]{2,1,0:T(8,128)(2,1)S(1)}, u32[]{:S(2)}, u32[]{:S(2)}) async-start(bf16[64,16,512]{2,1,0:T(8,128)(2,1)} %bitcast.100), calls=%async_computation | async-start | bytes 2097152 | tf_op jit(solution)/shard_map/all_to_all | solution.py:269
  24.0 2.3 %collective-permute-start = (bf16[4,64,1024]{2,1,0:T(8,128)(2,1)S(1)}, bf16[4,64,1024]{2,1,0:T(8,128)(2,1)S(1)}, u32[]{:S(2)}, u32[]{:S(2)}) collective-permute-start(bf16[4,64,1024]{2,1,0:T(8,128)(2,1)S(1)} %all-to-all-done.1.mine_hbm), channel_id=1, source_target_pairs={{0,64},{64,0},{1,65},{65,1},{2,66},{66,2},{3,67},{67,3},{4,68},{68... | collective-permute-start | bytes 1572872 | tf_op jit(solution)/shard_map/ppermute | solution.py:265
  26.3 1.5 collective-permute-done.other_hbm
  27.8 0.0 copy-start.2
  27.8 10.5 %all-to-all-done = bf16[64,16,512]{2,1,0:T(8,128)(2,1)S(1)} async-done(((bf16[64,16,512]{2,1,0:T(8,128)(2,1)}), bf16[64,16,512]{2,1,0:T(8,128)(2,1)S(1)}, u32[]{:S(2)}, u32[]{:S(2)}) %all-to-all-start) | async-done | bytes 1048608 | tf_op jit(solution)/shard_map/all_to_all | solution.py:269
  38.3 0.0 copy-done.1
  38.3 0.0 copy-done.2
  38.3 3.4 %shard_map.128 = bf16[4,256,1024]{2,1,0:T(8,128)(2,1)} custom-call(s32[1]{0:T(128)} %bitcast.1.me_ref, bf16[1024,512]{1,0:T(8,128)(2,1)S(1)} %bitcast.87, bf16[4,64,1024]{2,1,0:T(8,128)(2,1)} %copy-done.1, bf16[4,64,1024]{2,1,0:T(8,128)(2,1)} %copy-done.2), custom_call_target="tpu_custom_call" | custom-call | flops 1073741824 | bytes 4194304 | tf_op jit(solution)/shard_map/pallas_call | solution.py:210
  41.7 0.0 copy-start.3
  41.7 0.0 copy-start.4
  41.8 7.2 %all-to-all-start.2 = ((bf16[64,16,1024]{2,1,0:T(8,128)(2,1)}), bf16[64,16,1024]{2,1,0:T(8,128)(2,1)S(1)}, u32[]{:S(2)}, u32[]{:S(2)}) async-start(bf16[64,16,1024]{2,1,0:T(8,128)(2,1)} %bitcast.89), calls=%async_computation.2 | async-start | bytes 4194304 | tf_op jit(solution)/shard_map/all_to_all | solution.py:271
  48.9 0.0 copy-done.3
  49.0 0.7 mul.46
  49.7 0.0 copy-done.4
  49.7 0.1 copy.33
  49.8 0.1 eq.240
  49.8 0.2 convert_reduce_fusion.1
  50.0 0.1 reduce_sum.40
  50.1 0.1 copy.34
  50.2 0.1 add.69
  50.3 0.1 add.71
  50.4 24.0 %all-to-all-done.2 = bf16[64,16,1024]{2,1,0:T(8,128)(2,1)S(1)} async-done(((bf16[64,16,1024]{2,1,0:T(8,128)(2,1)}), bf16[64,16,1024]{2,1,0:T(8,128)(2,1)S(1)}, u32[]{:S(2)}, u32[]{:S(2)}) %all-to-all-start.2) | async-done | bytes 2097184 | tf_op jit(solution)/shard_map/all_to_all | solution.py:271
  74.4 0.4 convert_reduce_fusion
  74.9 0.2 multiply_reduce_fusion
  75.0 0.1 multiply_convert_fusion
  75.2 1.1 convolution_convert_fusion
  76.2 38.9 %all_to_all.25 = bf16[128,16,512]{2,1,0:T(8,128)(2,1)S(1)} all-to-all(bf16[128,16,512]{2,1,0:T(8,128)(2,1)S(1)} %bitcast.101), channel_id=1, replica_groups=mesh['role'=2,'dev'=64] {'role','dev'}, dimensions={0} | all-to-all | bytes 4194304 | tf_op jit(solution)/shard_map/all_to_all | solution.py:298
  115.2 11.0 %shard_map.129 = bf16[8,256,512]{2,1,0:T(8,128)(2,1)} custom-call(bf16[8,256,512]{2,1,0:T(8,128)(2,1)S(1)} %bitcast.86, bf16[4096,768]{1,0:T(8,128)(2,1)} %bitcast.91, bf16[4096,768]{1,0:T(8,128)(2,1)} %bitcast.92, bf16[768,4096]{1,0:T(8,128)(2,1)} %bitcast.93), custom_call_target="tpu_custom_call" | custom-call | flops 4831838208 | bytes 23068672 | tf_op jit(solution)/shard_map/pallas_call | solution.py:155
  126.2 0.0 copy-start.5
  126.2 6.3 %all-to-all-start.4 = ((bf16[128,16,512]{2,1,0:T(8,128)(2,1)}), bf16[128,16,512]{2,1,0:T(8,128)(2,1)}, u32[]{:S(2)}, u32[]{:S(2)}) async-start(bf16[128,16,512]{2,1,0:T(8,128)(2,1)} %bitcast.90), calls=%async_computation.4 | async-start | bytes 4194304 | tf_op jit(solution)/shard_map/all_to_all | solution.py:304
  132.5 0.0 copy-done.5
  132.5 0.1 reshape.75
  132.6 1.6 reduce-precision_convert_fusion
  134.2 27.2 %all-to-all-done.4 = bf16[128,16,512]{2,1,0:T(8,128)(2,1)} async-done(((bf16[128,16,512]{2,1,0:T(8,128)(2,1)}), bf16[128,16,512]{2,1,0:T(8,128)(2,1)}, u32[]{:S(2)}, u32[]{:S(2)}) %all-to-all-start.4) | async-done | bytes 2097184 | tf_op jit(solution)/shard_map/all_to_all | solution.py:304
  161.4 2.3 %fusion.1 = f32[256,512]{1,0:T(8,128)S(1)} fusion(bf16[2048,512]{1,0:T(8,128)(2,1)} %bitcast.31, bf16[128,2048]{1,0:T(8,128)(2,1)S(1)} %get-tuple-element.8, bf16[128,2048]{1,0:T(8,128)(2,1)S(1)} %get-tuple-element.7), kind=kOutput, calls=%fused_computation.5 | convolution fusion | flops 538968064 | bytes 3670016 | tf_op jit(solution)/shard_map/dot_general | solution.py:316
  163.7 0.1 fusion.22
  163.8 0.7 copy.38
  (15 shorter events, 0.2 us)
Async XLA Ops:
  0.0 1.2 copy-start
  2.1 12.5 %all-to-all-start.1 = ((bf16[4,64,1024]{2,1,0:T(8,128)(2,1)}), bf16[4,64,1024]{2,1,0:T(8,128)(2,1)S(1)}, u32[]{:S(2)}, u32[]{:S(2)}) async-start(bf16[4,64,1024]{2,1,0:T(8,128)(2,1)} %bitcast.85), calls=%async_computation.1 | async-start | bytes 1048576 | tf_op jit(solution)/shard_map/all_to_all | solution.py:264
  14.6 23.7 %copy-start.1 = (bf16[4,64,1024]{2,1,0:T(8,128)(2,1)}, bf16[4,64,1024]{2,1,0:T(8,128)(2,1)S(1)}, u32[]{:S(2)}) copy-start(bf16[4,64,1024]{2,1,0:T(8,128)(2,1)S(1)} %all-to-all-done.1.mine_hbm) | copy-start | bytes 1572868
  14.6 23.7 %all-to-all-start = ((bf16[64,16,512]{2,1,0:T(8,128)(2,1)}), bf16[64,16,512]{2,1,0:T(8,128)(2,1)S(1)}, u32[]{:S(2)}, u32[]{:S(2)}) async-start(bf16[64,16,512]{2,1,0:T(8,128)(2,1)} %bitcast.100), calls=%async_computation | async-start | bytes 2097152 | tf_op jit(solution)/shard_map/all_to_all | solution.py:269
  24.0 3.8 %collective-permute-start = (bf16[4,64,1024]{2,1,0:T(8,128)(2,1)S(1)}, bf16[4,64,1024]{2,1,0:T(8,128)(2,1)S(1)}, u32[]{:S(2)}, u32[]{:S(2)}) collective-permute-start(bf16[4,64,1024]{2,1,0:T(8,128)(2,1)S(1)} %all-to-all-done.1.mine_hbm), channel_id=1, source_target_pairs={{0,64},{64,0},{1,65},{65,1},{2,66},{66,2},{3,67},{67,3},{4,68},{68... | collective-permute-start | bytes 1572872 | tf_op jit(solution)/shard_map/ppermute | solution.py:265
  27.8 10.5 %copy-start.2 = (bf16[4,64,1024]{2,1,0:T(8,128)(2,1)}, bf16[4,64,1024]{2,1,0:T(8,128)(2,1)S(1)}, u32[]{:S(2)}) copy-start(bf16[4,64,1024]{2,1,0:T(8,128)(2,1)S(1)} %collective-permute-done.other_hbm) | copy-start | bytes 1572868
  41.7 7.2 %copy-start.3 = (bf16[16,4096]{1,0:T(8,128)(2,1)S(1)}, bf16[16,4096]{1,0:T(8,128)(2,1)}, u32[]{:S(2)}) copy-start(bf16[16,4096]{1,0:T(8,128)(2,1)} %param.13) | copy-start | bytes 393220
  41.7 7.9 %copy-start.4 = (s32[16,8]{0,1:T(8,128)S(1)}, s32[16,8]{0,1:T(8,128)}, u32[]{:S(2)}) copy-start(s32[16,8]{0,1:T(8,128)} %param.20) | copy-start | bytes 1540
  41.8 32.7 %all-to-all-start.2 = ((bf16[64,16,1024]{2,1,0:T(8,128)(2,1)}), bf16[64,16,1024]{2,1,0:T(8,128)(2,1)S(1)}, u32[]{:S(2)}, u32[]{:S(2)}) async-start(bf16[64,16,1024]{2,1,0:T(8,128)(2,1)} %bitcast.89), calls=%async_computation.2 | async-start | bytes 4194304 | tf_op jit(solution)/shard_map/all_to_all | solution.py:271
  126.2 6.3 %copy-start.5 = (f32[16,8]{0,1:T(8,128)S(1)}, f32[16,8]{0,1:T(8,128)}, u32[]{:S(2)}) copy-start(f32[16,8]{0,1:T(8,128)} %param.21) | copy-start | bytes 1540
  126.2 35.2 %all-to-all-start.4 = ((bf16[128,16,512]{2,1,0:T(8,128)(2,1)}), bf16[128,16,512]{2,1,0:T(8,128)(2,1)}, u32[]{:S(2)}, u32[]{:S(2)}) async-start(bf16[128,16,512]{2,1,0:T(8,128)(2,1)} %bitcast.90), calls=%async_computation.4 | async-start | bytes 4194304 | tf_op jit(solution)/shard_map/all_to_all | solution.py:304

commit v8 on v7

--- a/solution.py
+++ b/solution.py
@@ -91,17 +91,16 @@
 WIDE, TALL, AHEAD = 384, 2048, 2
 
 
-def expert_kernel(pieces, x_ref, gate_hbm, up_hbm, down_hbm, out_hbm,
-                  gate_s, up_s, down_s, x_s, act_s, res_s, out_s, w_sem, d_sem, o_sem):
+def expert_kernel(pieces, x_ref, gate_ref, up_hbm, down_hbm, out_hbm,
+                  up_s, down_s, x_s, act_s, res_s, out_s, w_sem, d_sem, o_sem):
     group, block = x_ref.shape[1:]
     span = group // pieces
-    parts, _, wide = gate_s.shape
+    parts, _, wide = up_s.shape
     outs, _, tall = down_s.shape
     loads = []
     for i in range(parts):
         cut = pl.ds(i * wide, wide)
-        loads.append(pltpu.make_async_copy(gate_hbm.at[:, cut], gate_s.at[i], w_sem.at[i, 0]))
-        loads.append(pltpu.make_async_copy(up_hbm.at[:, cut], up_s.at[i], w_sem.at[i, 1]))
+        loads.append(pltpu.make_async_copy(up_hbm.at[:, cut], up_s.at[i], w_sem.at[i]))
     for i in range(outs):
         loads.append(pltpu.make_async_copy(down_hbm.at[:, pl.ds(i * tall, tall)], down_s.at[i], d_sem.at[i]))
 
@@ -121,13 +120,12 @@
         for j in range(pieces):
             x_s[g * span:(g + 1) * span, j * block:(j + 1) * block] = y[j * span:(j + 1) * span, :]
     for i in range(parts):
-        arrive(2 * i)
-        gate = jnp.dot(x_s[...], gate_s[i], preferred_element_type=F32)
-        arrive(2 * i + 1)
+        gate = jnp.dot(x_s[...], gate_ref[:, i * wide:(i + 1) * wide], preferred_element_type=F32)
+        arrive(i)
         up = jnp.dot(x_s[...], up_s[i], preferred_element_type=F32)
         act_s[:, i * wide:(i + 1) * wide] = (gate / (1.0 + jnp.exp(-gate)) * up).astype(BF16)
     for i in range(outs):
-        arrive(2 * parts + i)
+        arrive(parts + i)
         y = jnp.dot(act_s[...], down_s[i], preferred_element_type=F32).astype(BF16)
         for n in range(tall // block):
             j = i * (tall // block) + n
@@ -150,29 +148,30 @@
     groups = pieces
     group = rows // groups
     wide, tall = min(WIDE, hidden), min(TALL, width)
-    operands = [pltpu.with_memory_space_constraint(x.reshape(groups, group, block), pltpu.VMEM)]
-    operands += [in_hbm(w_gate), in_hbm(w_up), in_hbm(w_down)]
+    operands = [
+        pltpu.with_memory_space_constraint(a, pltpu.VMEM)
+        for a in (x.reshape(groups, group, block), w_gate)
+    ] + [in_hbm(w_up), in_hbm(w_down)]
     result = pl.pallas_call(
         functools.partial(expert_kernel, pieces),
         out_shape=pltpu.HBM((groups, group, block), BF16),
-        in_specs=[pl.BlockSpec(memory_space=pltpu.VMEM)] + [pl.BlockSpec(memory_space=pltpu.HBM)] * 3,
+        in_specs=[pl.BlockSpec(memory_space=pltpu.VMEM)] * 2 + [pl.BlockSpec(memory_space=pltpu.HBM)] * 2,
         out_specs=pl.BlockSpec(memory_space=pltpu.HBM),
         scratch_shapes=[
-            pltpu.VMEM((hidden // wide, width, wide), BF16),
             pltpu.VMEM((hidden // wide, width, wide), BF16),
             pltpu.VMEM((width // tall, hidden, tall), BF16),
             pltpu.VMEM((tokens, width), BF16),
             pltpu.VMEM((tokens, hidden), BF16),
             pltpu.VMEM((groups, group, block), BF16),
             pltpu.VMEM((groups, group, block), BF16),
-            pltpu.SemaphoreType.DMA((hidden // wide, 2)),
+            pltpu.SemaphoreType.DMA((hidden // wide,)),
             pltpu.SemaphoreType.DMA((width // tall,)),
             pltpu.SemaphoreType.DMA((groups,)),
         ],
-        compiler_params=pltpu.CompilerParams(vmem_limit_bytes=48 * 1024 * 1024),
+        compiler_params=pltpu.CompilerParams(vmem_limit_bytes=36 * 1024 * 1024),
         cost_estimate=pl.CostEstimate(
             flops=6 * tokens * width * hidden,
-            bytes_accessed=6 * width * hidden + 4 * rows * block,
+            bytes_accessed=4 * width * hidden + 4 * rows * block,
             transcendentals=tokens * hidden,
         ),
     )(*operands)

time: 165 us -> 164 us (level)
  no operation moved by 1% of the time
where the time goes in v8:
time: 164 us; the launch traced here: 163 us
  waiting for transfers between devices  64.8 us (40%)
  blocking collectives  38.9 us (24%)
  starting transfers between devices  29.3 us (18%)
  Pallas kernels  19.6 us (12%)
  local copies, waits for them, and re-layouts  4.16 us (3%)
  matrix products  3.36 us (2%)
  other arithmetic  2.58 us (2%)
    all_to_all x1, blocking collectives, shards(): lax.all_to_all(outgoing.reshape(expert_total, slots * pieces, block), ('r...  38.9 us
    all_to_all x1, waiting for transfers between devices, shards(): lax.all_to_all(result.reshape(expert_total, slots * pieces, block), ('rol...  27.2 us
    all_to_all x1, waiting for transfers between devices, shards(): lax.all_to_all(part.reshape(chips, rows, width // members), 'dev', 0, 0,...  24 us
    all_to_all x1, waiting for transfers between devices, shards(): context = lax.all_to_all(context, 'dev', 0, 0, tiled=True)  10.5 us
    pallas_call x1, Pallas kernels, experts(): pl.pallas_call(functools.partial(expert_kernel, pieces), out_shape=pltpu....  9.5 us
    all_to_all x1, starting transfers between devices, shards(): context = lax.all_to_all(context, 'dev', 0, 0, tiled=True)  9.42 us
    all_to_all x1, starting transfers between devices, shards(): lax.all_to_all(part.reshape(chips, rows, width // members), 'dev', 0, 0,...  7.16 us
    pallas_call x1, Pallas kernels, attend(): pl.pallas_call(functools.partial(attend_kernel, copies), grid=(kv_heads,)...  6.72 us
  transfers between devices with their start and end apart: 5, of which 5 were waited for; matrix products, arithmetic and copies ran while one was open for 2% of the time, Pallas kernels for 4%

profile of v8, /device:TPU:5, one launch (start us, length us, event | category | flops | bytes accessed | tf_op | source)
XLA Modules:
  0.0 163.0 jit_solution(16760709624896058961)
XLA Ops:
  0.0 0.0 copy-start
  0.0 1.2 copy-done
  1.3 0.9 copy.47
  2.1 4.2 %all-to-all-start.1 = ((bf16[4,64,1024]{2,1,0:T(8,128)(2,1)}), bf16[4,64,1024]{2,1,0:T(8,128)(2,1)S(1)}, u32[]{:S(2)}, u32[]{:S(2)}) async-start(bf16[4,64,1024]{2,1,0:T(8,128)(2,1)} %bitcast.85), calls=%async_computation.1 | async-start | bytes 1048576 | tf_op jit(solution)/shard_map/all_to_all | solution.py:263
  6.3 6.7 %shard_map.127 = bf16[16,4,16,512]{3,2,1,0:T(8,128)(2,1)} custom-call(s32[16]{0:T(128)} %len_ref.1, bf16[16,8192]{1,0:T(8,128)(2,1)} %q_ref.1, bf16[16,4,128,128]{3,2,1,0:T(8,128)(2,1)} %k_ref.1, bf16[16,4,128,128]{3,2,1,0:T(8,128)(2,1)} %v_ref.1, bf16[128,128]{1,0:T(8,128)(2,1)} %constant.25.clone.table_ref), custom_call_target="tpu_custom_call" | custom-call | flops 67108864 | bytes 5242880 | tf_op jit(solution)/shard_map/pallas_call | solution.py:70
  13.0 1.6 all-to-all-done.1.mine_hbm
  14.6 0.0 copy-start.1
  14.6 9.4 %all-to-all-start = ((bf16[64,16,512]{2,1,0:T(8,128)(2,1)}), bf16[64,16,512]{2,1,0:T(8,128)(2,1)S(1)}, u32[]{:S(2)}, u32[]{:S(2)}) async-start(bf16[64,16,512]{2,1,0:T(8,128)(2,1)} %bitcast.102), calls=%async_computation | async-start | bytes 2097152 | tf_op jit(solution)/shard_map/all_to_all | solution.py:268
  24.0 2.3 %collective-permute-start = (bf16[4,64,1024]{2,1,0:T(8,128)(2,1)S(1)}, bf16[4,64,1024]{2,1,0:T(8,128)(2,1)S(1)}, u32[]{:S(2)}, u32[]{:S(2)}) collective-permute-start(bf16[4,64,1024]{2,1,0:T(8,128)(2,1)S(1)} %all-to-all-done.1.mine_hbm), channel_id=1, source_target_pairs={{0,64},{64,0},{1,65},{65,1},{2,66},{66,2},{3,67},{67,3},{4,68},{68... | collective-permute-start | bytes 1572872 | tf_op jit(solution)/shard_map/ppermute | solution.py:264
  26.3 1.5 collective-permute-done.other_hbm
  27.8 0.0 copy-start.2
  27.8 10.5 %all-to-all-done = bf16[64,16,512]{2,1,0:T(8,128)(2,1)S(1)} async-done(((bf16[64,16,512]{2,1,0:T(8,128)(2,1)}), bf16[64,16,512]{2,1,0:T(8,128)(2,1)S(1)}, u32[]{:S(2)}, u32[]{:S(2)}) %all-to-all-start) | async-done | bytes 1048608 | tf_op jit(solution)/shard_map/all_to_all | solution.py:268
  38.3 0.0 copy-done.1
  38.3 0.0 copy-done.2
  38.3 3.4 %shard_map.128 = bf16[4,256,1024]{2,1,0:T(8,128)(2,1)} custom-call(s32[1]{0:T(128)} %bitcast.1.me_ref, bf16[1024,512]{1,0:T(8,128)(2,1)S(1)} %bitcast.90, bf16[4,64,1024]{2,1,0:T(8,128)(2,1)} %copy-done.1, bf16[4,64,1024]{2,1,0:T(8,128)(2,1)} %copy-done.2), custom_call_target="tpu_custom_call" | custom-call | flops 1073741824 | bytes 4194304 | tf_op jit(solution)/shard_map/pallas_call | solution.py:209
  41.7 0.0 copy-start.3
  41.7 0.0 copy-start.4
  41.8 7.2 %all-to-all-start.2 = ((bf16[64,16,1024]{2,1,0:T(8,128)(2,1)}), bf16[64,16,1024]{2,1,0:T(8,128)(2,1)S(1)}, u32[]{:S(2)}, u32[]{:S(2)}) async-start(bf16[64,16,1024]{2,1,0:T(8,128)(2,1)} %bitcast.92), calls=%async_computation.2 | async-start | bytes 4194304 | tf_op jit(solution)/shard_map/all_to_all | solution.py:270
  48.9 0.0 copy-done.3
  49.0 0.7 mul.46
  49.7 0.0 copy-done.4
  49.7 0.1 copy.33
  49.8 0.1 eq.240
  49.9 0.2 convert_reduce_fusion.1
  50.0 0.1 reduce_sum.40
  50.1 0.1 copy.34
  50.2 0.1 add.69
  50.3 0.1 add.71
  50.4 24.0 %all-to-all-done.2 = bf16[64,16,1024]{2,1,0:T(8,128)(2,1)S(1)} async-done(((bf16[64,16,1024]{2,1,0:T(8,128)(2,1)}), bf16[64,16,1024]{2,1,0:T(8,128)(2,1)S(1)}, u32[]{:S(2)}, u32[]{:S(2)}) %all-to-all-start.2) | async-done | bytes 2097184 | tf_op jit(solution)/shard_map/all_to_all | solution.py:270
  74.4 0.0 slice-start
  74.4 0.4 convert_reduce_fusion
  74.9 0.2 multiply_reduce_fusion
  75.1 0.1 multiply_convert_fusion
  75.2 0.0 slice-start.1
  75.2 1.1 convolution_convert_fusion
  76.3 38.9 %all_to_all.25 = bf16[128,16,512]{2,1,0:T(8,128)(2,1)S(1)} all-to-all(bf16[128,16,512]{2,1,0:T(8,128)(2,1)S(1)} %bitcast.103), channel_id=1, replica_groups=mesh['role'=2,'dev'=64] {'role','dev'}, dimensions={0} | all-to-all | bytes 4194304 | tf_op jit(solution)/shard_map/all_to_all | solution.py:297
  115.2 0.0 slice-done
  115.2 0.0 slice-done.1
  115.2 9.5 %shard_map.129 = bf16[8,256,512]{2,1,0:T(8,128)(2,1)} custom-call(bf16[8,256,512]{2,1,0:T(8,128)(2,1)S(1)} %bitcast.86, bf16[4096,768]{1,0:T(8,128)(2,1)S(1)} %bitcast.89, bf16[4096,768]{1,0:T(8,128)(2,1)} %bitcast.94, bf16[768,4096]{1,0:T(8,128)(2,1)} %bitcast.95), custom_call_target="tpu_custom_call" | custom-call | flops 4831838208 | bytes 16777216 | tf_op jit(solution)/shard_map/pallas_call | solution.py:155
  124.7 0.0 copy-start.5
  124.7 6.3 %all-to-all-start.4 = ((bf16[128,16,512]{2,1,0:T(8,128)(2,1)}), bf16[128,16,512]{2,1,0:T(8,128)(2,1)}, u32[]{:S(2)}, u32[]{:S(2)}) async-start(bf16[128,16,512]{2,1,0:T(8,128)(2,1)} %bitcast.93), calls=%async_computation.4 | async-start | bytes 4194304 | tf_op jit(solution)/shard_map/all_to_all | solution.py:303
  131.0 0.0 copy-done.5
  131.0 0.1 reshape.75
  131.1 1.6 reduce-precision_convert_fusion
  132.7 27.2 %all-to-all-done.4 = bf16[128,16,512]{2,1,0:T(8,128)(2,1)} async-done(((bf16[128,16,512]{2,1,0:T(8,128)(2,1)}), bf16[128,16,512]{2,1,0:T(8,128)(2,1)}, u32[]{:S(2)}, u32[]{:S(2)}) %all-to-all-start.4) | async-done | bytes 2097184 | tf_op jit(solution)/shard_map/all_to_all | solution.py:303
  159.9 2.3 %fusion.1 = f32[256,512]{1,0:T(8,128)S(1)} fusion(bf16[2048,512]{1,0:T(8,128)(2,1)} %bitcast.31, bf16[128,2048]{1,0:T(8,128)(2,1)S(1)} %get-tuple-element.8, bf16[128,2048]{1,0:T(8,128)(2,1)S(1)} %get-tuple-element.7), kind=kOutput, calls=%fused_computation.5 | convolution fusion | flops 538968064 | bytes 3670016 | tf_op jit(solution)/shard_map/dot_general | solution.py:315
  162.3 0.1 fusion.22
  162.3 0.7 copy.38
  (16 shorter events, 0.2 us)
Async XLA Ops:
  0.0 1.2 copy-start
  2.1 12.5 %all-to-all-start.1 = ((bf16[4,64,1024]{2,1,0:T(8,128)(2,1)}), bf16[4,64,1024]{2,1,0:T(8,128)(2,1)S(1)}, u32[]{:S(2)}, u32[]{:S(2)}) async-start(bf16[4,64,1024]{2,1,0:T(8,128)(2,1)} %bitcast.85), calls=%async_computation.1 | async-start | bytes 1048576 | tf_op jit(solution)/shard_map/all_to_all | solution.py:263
  14.6 23.7 %copy-start.1 = (bf16[4,64,1024]{2,1,0:T(8,128)(2,1)}, bf16[4,64,1024]{2,1,0:T(8,128)(2,1)S(1)}, u32[]{:S(2)}) copy-start(bf16[4,64,1024]{2,1,0:T(8,128)(2,1)S(1)} %all-to-all-done.1.mine_hbm) | copy-start | bytes 1572868
  14.6 23.7 %all-to-all-start = ((bf16[64,16,512]{2,1,0:T(8,128)(2,1)}), bf16[64,16,512]{2,1,0:T(8,128)(2,1)S(1)}, u32[]{:S(2)}, u32[]{:S(2)}) async-start(bf16[64,16,512]{2,1,0:T(8,128)(2,1)} %bitcast.102), calls=%async_computation | async-start | bytes 2097152 | tf_op jit(solution)/shard_map/all_to_all | solution.py:268
  24.0 3.8 %collective-permute-start = (bf16[4,64,1024]{2,1,0:T(8,128)(2,1)S(1)}, bf16[4,64,1024]{2,1,0:T(8,128)(2,1)S(1)}, u32[]{:S(2)}, u32[]{:S(2)}) collective-permute-start(bf16[4,64,1024]{2,1,0:T(8,128)(2,1)S(1)} %all-to-all-done.1.mine_hbm), channel_id=1, source_target_pairs={{0,64},{64,0},{1,65},{65,1},{2,66},{66,2},{3,67},{67,3},{4,68},{68... | collective-permute-start | bytes 1572872 | tf_op jit(solution)/shard_map/ppermute | solution.py:264
  27.8 10.5 %copy-start.2 = (bf16[4,64,1024]{2,1,0:T(8,128)(2,1)}, bf16[4,64,1024]{2,1,0:T(8,128)(2,1)S(1)}, u32[]{:S(2)}) copy-start(bf16[4,64,1024]{2,1,0:T(8,128)(2,1)S(1)} %collective-permute-done.other_hbm) | copy-start | bytes 1572868
  41.7 7.2 %copy-start.3 = (bf16[16,4096]{1,0:T(8,128)(2,1)S(1)}, bf16[16,4096]{1,0:T(8,128)(2,1)}, u32[]{:S(2)}) copy-start(bf16[16,4096]{1,0:T(8,128)(2,1)} %param.13) | copy-start | bytes 393220
  41.7 7.9 %copy-start.4 = (s32[16,8]{0,1:T(8,128)S(1)}, s32[16,8]{0,1:T(8,128)}, u32[]{:S(2)}) copy-start(s32[16,8]{0,1:T(8,128)} %param.20) | copy-start | bytes 1540
  41.8 32.7 %all-to-all-start.2 = ((bf16[64,16,1024]{2,1,0:T(8,128)(2,1)}), bf16[64,16,1024]{2,1,0:T(8,128)(2,1)S(1)}, u32[]{:S(2)}, u32[]{:S(2)}) async-start(bf16[64,16,1024]{2,1,0:T(8,128)(2,1)} %bitcast.92), calls=%async_computation.2 | async-start | bytes 4194304 | tf_op jit(solution)/shard_map/all_to_all | solution.py:270
  74.4 40.8 %slice-start = ((s8[6291456]{0:T(1024)(128)(4,1)}), s8[4194304]{0:T(1024)(128)(4,1)S(1)}, s32[]{:S(2)}) async-start(s8[6291456]{0:T(1024)(128)(4,1)} %bitcast.87), calls=%async_computation.5 | async-start | bytes 8388608
  75.2 40.0 %slice-start.1 = ((s8[6291456]{0:T(1024)(128)(4,1)}), s8[2097152]{0:T(1024)(128)(4,1)S(1)}, s32[]{:S(2)}) async-start(s8[6291456]{0:T(1024)(128)(4,1)} %bitcast.87), calls=%async_computation.6 | async-start | bytes 4194304
  124.7 6.3 %copy-start.5 = (f32[16,8]{0,1:T(8,128)S(1)}, f32[16,8]{0,1:T(8,128)}, u32[]{:S(2)}) copy-start(f32[16,8]{0,1:T(8,128)} %param.21) | copy-start | bytes 1540
  124.7 35.2 %all-to-all-start.4 = ((bf16[128,16,512]{2,1,0:T(8,128)(2,1)}), bf16[128,16,512]{2,1,0:T(8,128)(2,1)}, u32[]{:S(2)}, u32[]{:S(2)}) async-start(bf16[128,16,512]{2,1,0:T(8,128)(2,1)} %bitcast.93), calls=%async_computation.4 | async-start | bytes 4194304 | tf_op jit(solution)/shard_map/all_to_all | solution.py:303

commit v9 on v8

--- a/solution.py
+++ b/solution.py
@@ -88,7 +88,7 @@
     )(lengths, queries, in_hbm(key_cache), in_hbm(value_cache), table)
 
 
-WIDE, TALL, AHEAD = 384, 2048, 2
+WIDE, TALL, AHEAD = 384, 1024, 3
 
 
 def expert_kernel(pieces, x_ref, gate_ref, up_hbm, down_hbm, out_hbm,
@@ -205,7 +205,7 @@
 def project(me, a, mine, other):
     rows, depth = a.shape
     members, half, columns = mine.shape
-    tiles = 4
+    tiles = 8
     result = pl.pallas_call(
         project_kernel,
         out_shape=pltpu.HBM((tiles, rows // tiles, columns), BF16),

time: 164 us -> 164 us (level)
  no operation moved by 1% of the time
where the time goes in v9:
time: 164 us; the launch traced here: 163 us
  waiting for transfers between devices  64.8 us (40%)
  blocking collectives  38.9 us (24%)
  starting transfers between devices  29.3 us (18%)
  Pallas kernels  19.5 us (12%)
  local copies, waits for them, and re-layouts  4.16 us (3%)
  matrix products  3.36 us (2%)
  other arithmetic  2.58 us (2%)
    all_to_all x1, blocking collectives, shards(): lax.all_to_all(outgoing.reshape(expert_total, slots * pieces, block), ('r...  38.9 us
    all_to_all x1, waiting for transfers between devices, shards(): lax.all_to_all(result.reshape(expert_total, slots * pieces, block), ('rol...  27.2 us
    all_to_all x1, waiting for transfers between devices, shards(): lax.all_to_all(part.reshape(chips, rows, width // members), 'dev', 0, 0,...  24 us
    all_to_all x1, waiting for transfers between devices, shards(): context = lax.all_to_all(context, 'dev', 0, 0, tiled=True)  10.5 us
    all_to_all x1, starting transfers between devices, shards(): context = lax.all_to_all(context, 'dev', 0, 0, tiled=True)  9.42 us
    pallas_call x1, Pallas kernels, experts(): pl.pallas_call(functools.partial(expert_kernel, pieces), out_shape=pltpu....  9.41 us
    all_to_all x1, starting transfers between devices, shards(): lax.all_to_all(part.reshape(chips, rows, width // members), 'dev', 0, 0,...  7.16 us
    pallas_call x1, Pallas kernels, attend(): pl.pallas_call(functools.partial(attend_kernel, copies), grid=(kv_heads,)...  6.72 us
  transfers between devices with their start and end apart: 5, of which 5 were waited for; matrix products, arithmetic and copies ran while one was open for 2% of the time, Pallas kernels for 4%

profile of v9, /device:TPU:5, one launch (start us, length us, event | category | flops | bytes accessed | tf_op | source)
XLA Modules:
  0.0 162.9 jit_solution(11603687806066860631)
XLA Ops:
  0.0 0.0 copy-start
  0.0 1.2 copy-done
  1.3 0.9 copy.47
  2.1 4.2 %all-to-all-start.1 = ((bf16[4,64,1024]{2,1,0:T(8,128)(2,1)}), bf16[4,64,1024]{2,1,0:T(8,128)(2,1)S(1)}, u32[]{:S(2)}, u32[]{:S(2)}) async-start(bf16[4,64,1024]{2,1,0:T(8,128)(2,1)} %bitcast.85), calls=%async_computation.1 | async-start | bytes 1048576 | tf_op jit(solution)/shard_map/all_to_all | solution.py:263
  6.3 6.7 %shard_map.127 = bf16[16,4,16,512]{3,2,1,0:T(8,128)(2,1)} custom-call(s32[16]{0:T(128)} %len_ref.1, bf16[16,8192]{1,0:T(8,128)(2,1)} %q_ref.1, bf16[16,4,128,128]{3,2,1,0:T(8,128)(2,1)} %k_ref.1, bf16[16,4,128,128]{3,2,1,0:T(8,128)(2,1)} %v_ref.1, bf16[128,128]{1,0:T(8,128)(2,1)} %constant.25.clone.table_ref), custom_call_target="tpu_custom_call" | custom-call | flops 67108864 | bytes 5242880 | tf_op jit(solution)/shard_map/pallas_call | solution.py:70
  13.0 1.6 all-to-all-done.1.mine_hbm
  14.6 0.0 copy-start.1
  14.6 9.4 %all-to-all-start = ((bf16[64,16,512]{2,1,0:T(8,128)(2,1)}), bf16[64,16,512]{2,1,0:T(8,128)(2,1)S(1)}, u32[]{:S(2)}, u32[]{:S(2)}) async-start(bf16[64,16,512]{2,1,0:T(8,128)(2,1)} %bitcast.102), calls=%async_computation | async-start | bytes 2097152 | tf_op jit(solution)/shard_map/all_to_all | solution.py:268
  24.0 2.3 %collective-permute-start = (bf16[4,64,1024]{2,1,0:T(8,128)(2,1)S(1)}, bf16[4,64,1024]{2,1,0:T(8,128)(2,1)S(1)}, u32[]{:S(2)}, u32[]{:S(2)}) collective-permute-start(bf16[4,64,1024]{2,1,0:T(8,128)(2,1)S(1)} %all-to-all-done.1.mine_hbm), channel_id=1, source_target_pairs={{0,64},{64,0},{1,65},{65,1},{2,66},{66,2},{3,67},{67,3},{4,68},{68... | collective-permute-start | bytes 1572872 | tf_op jit(solution)/shard_map/ppermute | solution.py:264
  26.3 1.5 collective-permute-done.other_hbm
  27.8 0.0 copy-start.2
  27.8 10.5 %all-to-all-done = bf16[64,16,512]{2,1,0:T(8,128)(2,1)S(1)} async-done(((bf16[64,16,512]{2,1,0:T(8,128)(2,1)}), bf16[64,16,512]{2,1,0:T(8,128)(2,1)S(1)}, u32[]{:S(2)}, u32[]{:S(2)}) %all-to-all-start) | async-done | bytes 1048608 | tf_op jit(solution)/shard_map/all_to_all | solution.py:268
  38.3 0.0 copy-done.1
  38.3 0.0 copy-done.2
  38.3 3.4 %shard_map.128 = bf16[8,128,1024]{2,1,0:T(8,128)(2,1)} custom-call(s32[1]{0:T(128)} %bitcast.1.me_ref, bf16[1024,512]{1,0:T(8,128)(2,1)S(1)} %bitcast.90, bf16[4,64,1024]{2,1,0:T(8,128)(2,1)} %copy-done.1, bf16[4,64,1024]{2,1,0:T(8,128)(2,1)} %copy-done.2), custom_call_target="tpu_custom_call" | custom-call | flops 1073741824 | bytes 4194304 | tf_op jit(solution)/shard_map/pallas_call | solution.py:209
  41.7 0.0 copy-start.3
  41.7 0.0 copy-start.4
  41.7 7.2 %all-to-all-start.2 = ((bf16[64,16,1024]{2,1,0:T(8,128)(2,1)}), bf16[64,16,1024]{2,1,0:T(8,128)(2,1)S(1)}, u32[]{:S(2)}, u32[]{:S(2)}) async-start(bf16[64,16,1024]{2,1,0:T(8,128)(2,1)} %bitcast.92), calls=%async_computation.2 | async-start | bytes 4194304 | tf_op jit(solution)/shard_map/all_to_all | solution.py:270
  48.9 0.0 copy-done.3
  48.9 0.7 mul.46
  49.7 0.0 copy-done.4
  49.7 0.1 copy.33
  49.7 0.1 eq.240
  49.8 0.2 convert_reduce_fusion.1
  50.0 0.1 reduce_sum.40
  50.1 0.1 copy.34
  50.2 0.1 add.69
  50.3 0.1 add.71
  50.4 24.0 %all-to-all-done.2 = bf16[64,16,1024]{2,1,0:T(8,128)(2,1)S(1)} async-done(((bf16[64,16,1024]{2,1,0:T(8,128)(2,1)}), bf16[64,16,1024]{2,1,0:T(8,128)(2,1)S(1)}, u32[]{:S(2)}, u32[]{:S(2)}) %all-to-all-start.2) | async-done | bytes 2097184 | tf_op jit(solution)/shard_map/all_to_all | solution.py:270
  74.4 0.0 slice-start
  74.4 0.4 convert_reduce_fusion
  74.9 0.2 multiply_reduce_fusion
  75.0 0.1 multiply_convert_fusion
  75.1 0.0 slice-start.1
  75.2 1.1 convolution_convert_fusion
  76.2 38.9 %all_to_all.25 = bf16[128,16,512]{2,1,0:T(8,128)(2,1)S(1)} all-to-all(bf16[128,16,512]{2,1,0:T(8,128)(2,1)S(1)} %bitcast.103), channel_id=1, replica_groups=mesh['role'=2,'dev'=64] {'role','dev'}, dimensions={0} | all-to-all | bytes 4194304 | tf_op jit(solution)/shard_map/all_to_all | solution.py:297
  115.2 0.0 slice-done
  115.2 0.0 slice-done.1
  115.2 9.4 %shard_map.129 = bf16[8,256,512]{2,1,0:T(8,128)(2,1)} custom-call(bf16[8,256,512]{2,1,0:T(8,128)(2,1)S(1)} %bitcast.86, bf16[4096,768]{1,0:T(8,128)(2,1)S(1)} %bitcast.89, bf16[4096,768]{1,0:T(8,128)(2,1)} %bitcast.94, bf16[768,4096]{1,0:T(8,128)(2,1)} %bitcast.95), custom_call_target="tpu_custom_call" | custom-call | flops 4831838208 | bytes 16777216 | tf_op jit(solution)/shard_map/pallas_call | solution.py:155
  124.6 0.0 copy-start.5
  124.6 6.3 %all-to-all-start.4 = ((bf16[128,16,512]{2,1,0:T(8,128)(2,1)}), bf16[128,16,512]{2,1,0:T(8,128)(2,1)}, u32[]{:S(2)}, u32[]{:S(2)}) async-start(bf16[128,16,512]{2,1,0:T(8,128)(2,1)} %bitcast.93), calls=%async_computation.4 | async-start | bytes 4194304 | tf_op jit(solution)/shard_map/all_to_all | solution.py:303
  130.9 0.0 copy-done.5
  130.9 0.1 reshape.75
  131.0 1.6 reduce-precision_convert_fusion
  132.6 27.2 %all-to-all-done.4 = bf16[128,16,512]{2,1,0:T(8,128)(2,1)} async-done(((bf16[128,16,512]{2,1,0:T(8,128)(2,1)}), bf16[128,16,512]{2,1,0:T(8,128)(2,1)}, u32[]{:S(2)}, u32[]{:S(2)}) %all-to-all-start.4) | async-done | bytes 2097184 | tf_op jit(solution)/shard_map/all_to_all | solution.py:303
  159.8 2.3 %fusion.1 = f32[256,512]{1,0:T(8,128)S(1)} fusion(bf16[2048,512]{1,0:T(8,128)(2,1)} %bitcast.31, bf16[128,2048]{1,0:T(8,128)(2,1)S(1)} %get-tuple-element.8, bf16[128,2048]{1,0:T(8,128)(2,1)S(1)} %get-tuple-element.7), kind=kOutput, calls=%fused_computation.5 | convolution fusion | flops 538968064 | bytes 3670016 | tf_op jit(solution)/shard_map/dot_general | solution.py:315
  162.2 0.1 fusion.22
  162.2 0.7 copy.38
  (16 shorter events, 0.2 us)
Async XLA Ops:
  0.0 1.2 copy-start
  2.1 12.5 %all-to-all-start.1 = ((bf16[4,64,1024]{2,1,0:T(8,128)(2,1)}), bf16[4,64,1024]{2,1,0:T(8,128)(2,1)S(1)}, u32[]{:S(2)}, u32[]{:S(2)}) async-start(bf16[4,64,1024]{2,1,0:T(8,128)(2,1)} %bitcast.85), calls=%async_computation.1 | async-start | bytes 1048576 | tf_op jit(solution)/shard_map/all_to_all | solution.py:263
  14.6 23.7 %copy-start.1 = (bf16[4,64,1024]{2,1,0:T(8,128)(2,1)}, bf16[4,64,1024]{2,1,0:T(8,128)(2,1)S(1)}, u32[]{:S(2)}) copy-start(bf16[4,64,1024]{2,1,0:T(8,128)(2,1)S(1)} %all-to-all-done.1.mine_hbm) | copy-start | bytes 1572868
  14.6 23.7 %all-to-all-start = ((bf16[64,16,512]{2,1,0:T(8,128)(2,1)}), bf16[64,16,512]{2,1,0:T(8,128)(2,1)S(1)}, u32[]{:S(2)}, u32[]{:S(2)}) async-start(bf16[64,16,512]{2,1,0:T(8,128)(2,1)} %bitcast.102), calls=%async_computation | async-start | bytes 2097152 | tf_op jit(solution)/shard_map/all_to_all | solution.py:268
  24.0 3.8 %collective-permute-start = (bf16[4,64,1024]{2,1,0:T(8,128)(2,1)S(1)}, bf16[4,64,1024]{2,1,0:T(8,128)(2,1)S(1)}, u32[]{:S(2)}, u32[]{:S(2)}) collective-permute-start(bf16[4,64,1024]{2,1,0:T(8,128)(2,1)S(1)} %all-to-all-done.1.mine_hbm), channel_id=1, source_target_pairs={{0,64},{64,0},{1,65},{65,1},{2,66},{66,2},{3,67},{67,3},{4,68},{68... | collective-permute-start | bytes 1572872 | tf_op jit(solution)/shard_map/ppermute | solution.py:264
  27.8 10.5 %copy-start.2 = (bf16[4,64,1024]{2,1,0:T(8,128)(2,1)}, bf16[4,64,1024]{2,1,0:T(8,128)(2,1)S(1)}, u32[]{:S(2)}) copy-start(bf16[4,64,1024]{2,1,0:T(8,128)(2,1)S(1)} %collective-permute-done.other_hbm) | copy-start | bytes 1572868
  41.7 7.2 %copy-start.3 = (bf16[16,4096]{1,0:T(8,128)(2,1)S(1)}, bf16[16,4096]{1,0:T(8,128)(2,1)}, u32[]{:S(2)}) copy-start(bf16[16,4096]{1,0:T(8,128)(2,1)} %param.13) | copy-start | bytes 393220
  41.7 7.9 %copy-start.4 = (s32[16,8]{0,1:T(8,128)S(1)}, s32[16,8]{0,1:T(8,128)}, u32[]{:S(2)}) copy-start(s32[16,8]{0,1:T(8,128)} %param.20) | copy-start | bytes 1540
  41.7 32.7 %all-to-all-start.2 = ((bf16[64,16,1024]{2,1,0:T(8,128)(2,1)}), bf16[64,16,1024]{2,1,0:T(8,128)(2,1)S(1)}, u32[]{:S(2)}, u32[]{:S(2)}) async-start(bf16[64,16,1024]{2,1,0:T(8,128)(2,1)} %bitcast.92), calls=%async_computation.2 | async-start | bytes 4194304 | tf_op jit(solution)/shard_map/all_to_all | solution.py:270
  74.4 40.8 %slice-start = ((s8[6291456]{0:T(1024)(128)(4,1)}), s8[4194304]{0:T(1024)(128)(4,1)S(1)}, s32[]{:S(2)}) async-start(s8[6291456]{0:T(1024)(128)(4,1)} %bitcast.87), calls=%async_computation.5 | async-start | bytes 8388608
  75.1 40.0 %slice-start.1 = ((s8[6291456]{0:T(1024)(128)(4,1)}), s8[2097152]{0:T(1024)(128)(4,1)S(1)}, s32[]{:S(2)}) async-start(s8[6291456]{0:T(1024)(128)(4,1)} %bitcast.87), calls=%async_computation.6 | async-start | bytes 4194304
  124.6 6.3 %copy-start.5 = (f32[16,8]{0,1:T(8,128)S(1)}, f32[16,8]{0,1:T(8,128)}, u32[]{:S(2)}) copy-start(f32[16,8]{0,1:T(8,128)} %param.21) | copy-start | bytes 1540
  124.6 35.2 %all-to-all-start.4 = ((bf16[128,16,512]{2,1,0:T(8,128)(2,1)}), bf16[128,16,512]{2,1,0:T(8,128)(2,1)}, u32[]{:S(2)}, u32[]{:S(2)}) async-start(bf16[128,16,512]{2,1,0:T(8,128)(2,1)} %bitcast.93), calls=%async_computation.4 | async-start | bytes 4194304 | tf_op jit(solution)/shard_map/all_to_all | solution.py:303
